TPU v7x, 32 devices: a whole 2x2x4 slice. The times are simulated.
32 devices in a mesh: section: 2 (over y), dp: 16 (over z, x, core).
Axes of the slice: x: 2, y: 2, z: 4, core: 2. Of those that a mesh axis runs over, the one named last changes fastest.
Arguments:
- layer_input: bfloat16 [2, 2, 16, 256, 512], P('section', None, 'dp'), may hold values from -6 to 6
- lengths: int32 [2, 16], P(None, 'dp'), may hold values from 64 to 256, as said below
- attn_qkv: bfloat16 [2, 512, 1536], P('section'), may hold values from -0.25 to 0.25
- attn_out: bfloat16 [2, 512, 512], P('section'), may hold values from -2 to 2
- ffn_in: bfloat16 [2, 512, 2048], P('section'), may hold values from -0.25 to 0.25
- ffn_out: bfloat16 [2, 2048, 512], P('section'), may hold values from -0.125 to 0.125
- cross_weight: bfloat16 [2, 512, 1024], P('section'), as said below
- norm_gain: float32 [2, 3, 512], P('section'), may hold values from 0.5 to 1.5
- norm_bias: float32 [2, 3, 512], P('section'), may hold values from -3 to 3
- cotangent: bfloat16 [2, 2, 16, 256, 512], P('section', None, 'dp'), may hold values from -6 to 6
Outputs:
- layer_output: bfloat16 [2, 2, 16, 256, 512], P('section', None, 'dp')
- input_grad: bfloat16 [2, 2, 16, 256, 512], P('section', None, 'dp')
- grad_attn_qkv: float32 [2, 512, 1536], P('section')
- grad_attn_out: float32 [2, 512, 512], P('section')
- grad_ffn_in: float32 [2, 512, 2048], P('section')
- grad_ffn_out: float32 [2, 2048, 512], P('section')
- grad_cross: float32 [2, 512, 1024], P('section')
- grad_norm_gain: float32 [2, 3, 512], P('section')
- grad_norm_bias: float32 [2, 3, 512], P('section')
Inputs may be any that keep to these rules, and one draw needn't show every extreme that they name: `lengths`: in every micro-batch one sentence has the full length 256. `cross_weight`: independent normal entries of mean zero.
All inputs are finite; a program needn't handle non-finite values.
Results may differ from a plain program's by a relative error of at most 0.019.
Values may be sent and summed in bfloat16 or wider, within the bound.
A program may use at most 192 MiB of HBM per device.

v0:
```python
import jax
import jax.numpy as jnp
from jax import lax
from jax.sharding import PartitionSpec as P

HEADS = 8


def shifted(value, axis, steps):
    count = lax.axis_size(axis)
    leading, last = (max(0, -steps), min(count, count - steps))
    return lax.ppermute(value, axis, [(source, source + steps) for source in range(leading, last)])


def product(left_side, right_side):
    return jnp.dot(left_side, right_side, preferred_element_type=jnp.float32)


def product_tn(left_side, right_side):
    return lax.dot_general(
        left_side, right_side, (((0,), (0,)), ((), ())), preferred_element_type=jnp.float32
    )


def product_nt(left_side, right_side):
    return lax.dot_general(
        left_side, right_side, (((1,), (1,)), ((), ())), preferred_element_type=jnp.float32
    )


def gelu_exact(pre_act):
    return jax.nn.gelu(pre_act, approximate=False)


def layer_norm(source, norm_scale, norm_shift):
    center = source - jnp.mean(source, axis=-1, keepdims=True)
    spread = jnp.mean(center * center, axis=-1, keepdims=True)
    return center * lax.rsqrt(spread + 1e-05) * norm_scale + norm_shift


def split_heads(matrix):
    return matrix.reshape(matrix.shape[:-1] + (HEADS, matrix.shape[-1] // HEADS))


def masked_scores(queries, key_rows, usable):
    head_size = queries.shape[-1] // HEADS
    scores = jnp.einsum(
        "qhd,khd->hqk",
        split_heads(queries),
        split_heads(key_rows),
        preferred_element_type=jnp.float32,
    ) * head_size ** (-0.5)
    return jnp.where(usable[None, None, :], scores, -1e30)


def attend(queries, key_rows, value_rows, usable):
    scores = masked_scores(queries, key_rows, usable)
    highest = jnp.max(scores, axis=-1, keepdims=True)
    weights = jnp.exp(scores - highest)
    denominator = jnp.sum(weights, axis=-1, keepdims=True)
    chances = (weights / denominator).astype(jnp.bfloat16)
    blended = jnp.einsum(
        "hqk,khd->qhd", chances, split_heads(value_rows), preferred_element_type=jnp.float32
    )
    return (blended.reshape(queries.shape).astype(jnp.bfloat16), highest + jnp.log(denominator))


def attend_back(grad_blended, queries, key_rows, value_rows, usable, log_total):
    factor = (queries.shape[-1] // HEADS) ** (-0.5)
    scores = masked_scores(queries, key_rows, usable)
    chances = jnp.exp(scores - log_total)
    heads_grad = split_heads(grad_blended)
    grad_values = jnp.einsum(
        "hqk,qhd->khd", chances.astype(jnp.bfloat16), heads_grad, preferred_element_type=jnp.float32
    )
    grad_chances = jnp.einsum(
        "qhd,khd->hqk", heads_grad, split_heads(value_rows), preferred_element_type=jnp.float32
    )
    grad_scores = (
        chances * (grad_chances - jnp.sum(chances * grad_chances, axis=-1, keepdims=True))
    ).astype(jnp.bfloat16)
    grad_queries = (
        jnp.einsum(
            "hqk,khd->qhd", grad_scores, split_heads(key_rows), preferred_element_type=jnp.float32
        )
        * factor
    )
    grad_keys = (
        jnp.einsum(
            "hqk,qhd->khd", grad_scores, split_heads(queries), preferred_element_type=jnp.float32
        )
        * factor
    )
    row_shape = queries.shape
    return (
        grad_queries.reshape(row_shape),
        grad_keys.reshape(row_shape),
        grad_values.reshape(row_shape),
    )


def self_forward(inputs, usable, weight_qkv, weight_out, norm_scale, norm_shift):
    breadth = inputs.shape[-1]
    normed = layer_norm(inputs, norm_scale, norm_shift).astype(jnp.bfloat16)
    packed = product(normed, weight_qkv).astype(jnp.bfloat16)
    blended, log_total = attend(
        packed[:, :breadth], packed[:, breadth : 2 * breadth], packed[:, 2 * breadth :], usable
    )
    residual = inputs + product(blended, weight_out)
    return (residual, (normed, packed, blended, log_total))


def self_backward(upstream, inputs, usable, stored, weight_qkv, weight_out, norm_scale, norm_shift):
    normed, packed, blended, log_total = stored
    breadth = inputs.shape[-1]
    low_grad = upstream.astype(jnp.bfloat16)
    out_term = product_tn(blended, low_grad)
    grad_blended = product_nt(low_grad, weight_out).astype(jnp.bfloat16)
    grad_queries, grad_keys, grad_values = attend_back(
        grad_blended,
        packed[:, :breadth],
        packed[:, breadth : 2 * breadth],
        packed[:, 2 * breadth :],
        usable,
        log_total,
    )
    grad_packed = jnp.concatenate([grad_queries, grad_keys, grad_values], axis=1).astype(
        jnp.bfloat16
    )
    qkv_term = product_tn(normed, grad_packed)
    _, pullback = jax.vjp(layer_norm, inputs, norm_scale, norm_shift)
    grad_inner, gain_term, bias_term = pullback(product_nt(grad_packed, weight_qkv))
    return (upstream + grad_inner, qkv_term, out_term, gain_term, bias_term)


def ffn_forward(residual, weight_up, weight_down, norm_scale, norm_shift):
    normed = layer_norm(residual, norm_scale, norm_shift).astype(jnp.bfloat16)
    pre_act = product(normed, weight_up)
    hidden = gelu_exact(pre_act).astype(jnp.bfloat16)
    return (residual + product(hidden, weight_down), (normed, pre_act, hidden))


def ffn_backward(upstream, residual, stored, weight_up, weight_down, norm_scale, norm_shift):
    normed, pre_act, hidden = stored
    low_grad = upstream.astype(jnp.bfloat16)
    down_term = product_tn(hidden, low_grad)
    _, gelu_pullback = jax.vjp(gelu_exact, pre_act)
    grad_pre = gelu_pullback(product_nt(low_grad, weight_down))[0].astype(jnp.bfloat16)
    up_term = product_tn(normed, grad_pre)
    _, pullback = jax.vjp(layer_norm, residual, norm_scale, norm_shift)
    grad_inner, gain_term, bias_term = pullback(product_nt(grad_pre, weight_up))
    return (upstream + grad_inner, up_term, down_term, gain_term, bias_term)


def send_ahead(payload):
    return shifted(payload, "section", 1)


def send_behind(payload):
    return shifted(payload, "section", -1)


def local(
    layer_input,
    lengths,
    attn_qkv,
    attn_out,
    ffn_in,
    ffn_out,
    cross_weight,
    norm_gain,
    norm_bias,
    cotangent,
):
    is_encoder = lax.axis_index("section") == 0
    inputs = layer_input[0, :, 0].astype(jnp.float32)
    cotangents = cotangent[0, :, 0].astype(jnp.float32)
    micro_count, length, breadth = inputs.shape
    positions = jnp.arange(length, dtype=jnp.int32)
    key_masks = positions[None, :] < lengths[:, 0][:, None]
    w_qkv = attn_qkv[0]
    w_out = attn_out[0]
    w_up = ffn_in[0]
    w_down = ffn_out[0]
    w_cross = cross_weight[0]
    gains = norm_gain[0]
    biases = norm_bias[0]
    pair_width = 2 * breadth

    def encoder_forward(index):
        residual, self_kept = self_forward(
            inputs[index], key_masks[index], w_qkv, w_out, gains[0], biases[0]
        )
        after, ffn_kept = ffn_forward(residual, w_up, w_down, gains[1], biases[1])
        states = layer_norm(after, gains[2], biases[2]).astype(jnp.bfloat16)
        outgoing = product(states, w_cross).astype(jnp.bfloat16)
        return (outgoing, states, (residual, after, states, self_kept, ffn_kept))

    def encoder_top(index, stored, returned, grads):
        g_qkv, g_out, g_up, g_down, g_cross, g_gain, g_bias, g_pair = grads
        residual, after, states, self_kept, ffn_kept = stored
        g_cross = g_cross + product_tn(states, returned)
        from_cross = lax.optimization_barrier(
            product_nt(returned, w_cross).astype(jnp.bfloat16)
        ).astype(jnp.float32)
        _, pullback = jax.vjp(layer_norm, after, gains[2], biases[2])
        grad_after, gain_last, bias_last = pullback(cotangents[index] + from_cross)
        grad_residual, up_term, down_term, gain_ffn, bias_ffn = ffn_backward(
            grad_after, residual, ffn_kept, w_up, w_down, gains[1], biases[1]
        )
        g_gain = g_gain.at[1].add(gain_ffn).at[2].add(gain_last)
        g_bias = g_bias.at[1].add(bias_ffn).at[2].add(bias_last)
        return (
            grad_residual,
            (g_qkv, g_out, g_up + up_term, g_down + down_term, g_cross, g_gain, g_bias, g_pair),
        )

    def encoder_bottom(index, stored, grad_residual, in_grads, grads):
        g_qkv, g_out, g_up, g_down, g_cross, g_gain, g_bias, g_pair = grads
        residual, after, states, self_kept, ffn_kept = stored
        grad_input, qkv_term, out_term, gain_self, bias_self = self_backward(
            grad_residual,
            inputs[index],
            key_masks[index],
            self_kept,
            w_qkv,
            w_out,
            gains[0],
            biases[0],
        )
        in_grads = in_grads.at[index].set(grad_input.astype(jnp.bfloat16))
        grads = (
            g_qkv + qkv_term,
            g_out + out_term,
            g_up,
            g_down,
            g_cross,
            g_gain.at[0].add(gain_self),
            g_bias.at[0].add(bias_self),
            g_pair,
        )
        return (in_grads, grads)

    def decoder_step(index, incoming, grads):
        g_qkv, g_out, g_up, g_down, g_cross, g_gain, g_bias, g_pair = grads
        usable = key_masks[index]
        residual, self_kept = self_forward(inputs[index], usable, w_qkv, w_out, gains[0], biases[0])
        normed = layer_norm(residual, gains[1], biases[1]).astype(jnp.bfloat16)
        queries = product(normed, w_cross[:, :breadth]).astype(jnp.bfloat16)
        blended, log_total = attend(queries, incoming[:, :breadth], incoming[:, breadth:], usable)
        middle = residual + product(blended, w_cross[:, breadth:])
        after, ffn_kept = ffn_forward(middle, w_up, w_down, gains[2], biases[2])
        grad_middle, up_term, down_term, gain_ffn, bias_ffn = ffn_backward(
            cotangents[index], middle, ffn_kept, w_up, w_down, gains[2], biases[2]
        )
        low_grad = grad_middle.astype(jnp.bfloat16)
        cross_out_term = product_tn(blended, low_grad)
        grad_blended = product_nt(low_grad, w_cross[:, breadth:]).astype(jnp.bfloat16)
        grad_queries, grad_keys, grad_values = attend_back(
            grad_blended, queries, incoming[:, :breadth], incoming[:, breadth:], usable, log_total
        )
        low_queries = grad_queries.astype(jnp.bfloat16)
        grad_pairs = jnp.concatenate([grad_keys, grad_values], axis=1).astype(jnp.bfloat16)
        cross_in_term = product_tn(normed, low_queries)
        _, pullback = jax.vjp(layer_norm, residual, gains[1], biases[1])
        grad_inner, gain_cross, bias_cross = pullback(product_nt(low_queries, w_cross[:, :breadth]))
        grad_input, qkv_term, out_term, gain_self, bias_self = self_backward(
            grad_middle + grad_inner,
            inputs[index],
            usable,
            self_kept,
            w_qkv,
            w_out,
            gains[0],
            biases[0],
        )
        grads = (
            g_qkv + qkv_term,
            g_out + out_term,
            g_up + up_term,
            g_down + down_term,
            g_cross + jnp.concatenate([cross_in_term, cross_out_term], axis=1),
            g_gain + jnp.stack([gain_self, gain_cross, gain_ffn]),
            g_bias + jnp.stack([bias_self, bias_cross, bias_ffn]),
            g_pair,
        )
        return (after.astype(jnp.bfloat16), grad_input.astype(jnp.bfloat16), grads, grad_pairs)

    blank_send = jnp.zeros((length, pair_width), jnp.bfloat16)
    blank_store = jax.tree.map(jnp.zeros_like, encoder_forward(0)[2])
    results = jnp.zeros((micro_count, length, breadth), jnp.bfloat16)
    in_grads = jnp.zeros((micro_count, length, breadth), jnp.bfloat16)
    grads = (
        jnp.zeros(w_qkv.shape, jnp.float32),
        jnp.zeros(w_out.shape, jnp.float32),
        jnp.zeros(w_up.shape, jnp.float32),
        jnp.zeros(w_down.shape, jnp.float32),
        jnp.zeros(w_cross.shape, jnp.float32),
        jnp.zeros(gains.shape, jnp.float32),
        jnp.zeros(biases.shape, jnp.float32),
        jnp.zeros(w_cross.shape, jnp.float32),
    )
    arrived_ahead = blank_send
    arrived_back = blank_send
    stored_list = []

    def make_ticks(tick_now):

        def encoder_tick(operands):
            results_now, in_grads_now, grads_now, ahead_now, back_now, stored_old = operands
            outgoing = blank_send
            stored_new = blank_store
            if tick_now < micro_count:
                outgoing, states, stored_new = encoder_forward(tick_now)
                results_now = results_now.at[tick_now].set(states)
            if tick_now >= 2:
                grad_residual, grads_now = encoder_top(
                    tick_now - 2, stored_old, back_now, grads_now
                )
                in_grads_now, grads_now = encoder_bottom(
                    tick_now - 2, stored_old, grad_residual, in_grads_now, grads_now
                )
            return (results_now, in_grads_now, grads_now, outgoing, blank_send, stored_new)

        def decoder_tick(operands):
            results_now, in_grads_now, grads_now, ahead_now, back_now, stored_old = operands
            outgoing = blank_send
            if 1 <= tick_now <= micro_count:
                result, grad_input, grads_now, outgoing = decoder_step(
                    tick_now - 1, ahead_now, grads_now
                )
                results_now = results_now.at[tick_now - 1].set(result)
                in_grads_now = in_grads_now.at[tick_now - 1].set(grad_input)
            return (results_now, in_grads_now, grads_now, blank_send, outgoing, blank_store)

        return (encoder_tick, decoder_tick)

    for tick_now in range(micro_count + 1):
        encoder_tick, decoder_tick = make_ticks(tick_now)
        stored_old = stored_list[tick_now - 2] if tick_now >= 2 else blank_store
        operands = (results, in_grads, grads, arrived_ahead, arrived_back, stored_old)
        results, in_grads, grads, ahead_value, behind_value, stored_new = lax.cond(
            is_encoder, encoder_tick, decoder_tick, operands
        )
        if tick_now < micro_count:
            stored_list.append(stored_new)
            arrived_ahead = send_ahead(ahead_value)
        if tick_now >= 1:
            arrived_back = send_behind(behind_value)
    last_index = micro_count - 1
    last_store = stored_list[last_index]

    def full_encoder(operands):
        in_grads_now, grads_now, back_now = operands
        residual_grad, grads_now = encoder_top(last_index, last_store, back_now, grads_now)
        return encoder_bottom(last_index, last_store, residual_grad, in_grads_now, grads_now)

    def full_decoder(operands):
        in_grads_now, grads_now, back_now = operands
        return (in_grads_now, grads_now)

    in_grads, grads = lax.cond(
        is_encoder, full_encoder, full_decoder, (in_grads, grads, arrived_back)
    )
    sum_qkv, sum_out, sum_up, sum_down, sum_cross, sum_gain, sum_bias = lax.psum(
        (grads[0], grads[1], grads[2], grads[3], grads[4], grads[5], grads[6]), "dp"
    )
    return (
        results[None, :, None],
        in_grads[None, :, None],
        sum_qkv[None],
        sum_out[None],
        sum_up[None],
        sum_down[None],
        sum_cross[None],
        sum_gain[None],
        sum_bias[None],
    )


def solution(mesh):
    placed = (
        P("section", None, "dp", None, None),
        P(None, "dp"),
        P("section", None, None),
        P("section", None, None),
        P("section", None, None),
        P("section", None, None),
        P("section", None, None),
        P("section", None, None),
        P("section", None, None),
        P("section", None, "dp", None, None),
    )
    return jax.shard_map(
        local,
        mesh=mesh,
        in_specs=placed,
        out_specs=(
            P("section", None, "dp", None, None),
            P("section", None, "dp", None, None),
            P("section", None, None),
            P("section", None, None),
            P("section", None, None),
            P("section", None, None),
            P("section", None, None),
            P("section", None, None),
            P("section", None, None),
        ),
        check_vma=False,
    )
```

profile of v0, /device:TPU:0, one launch (start us, length us, event | category | flops | bytes accessed | tf_op | source)
XLA Modules:
  0.0 620.5 jit_solution(4897126911793395292)
XLA Ops:
  9.8 21.6 %conditional.4 = (bf16[2,256,512]{2,1,0:T(8,128)(2,1)}, bf16[256,1024]{1,0:T(8,128)(2,1)}, f32[256,512]{1,0:T(8,128)S(1)}, f32[256,512]{1,0:T(8,128)}, bf16[256,...) conditional(s32[]{:T(128)} %convert_element_type.312, ...), branch_computations={%region_0.0_spmd, %region_1.10_spmd} | conditional | flops 2058877696 | bytes 70392472 | solution.py:342
  10.4 2.1 convolution_convert_fusion
  16.5 5.8 fusion.2
  22.4 1.5 fusion.191
  25.3 2.0 add_convert_fusion
  29.3 2.2 convolution_convert_fusion.1
  34.2 2.1 bitcast_convert_fusion.10
  36.4 9.9 %collective-permute-done = bf16[256,1024]{0,1:T(8,128)(2,1)S(1)} collective-permute-done((bf16[256,1024]{0,1:T(8,128)(2,1)S(1)}, bf16[256,1024]{0,1:T(8,128)(2,1)S(1)}, u32[]{:S(2)}, u32[]{:S(2)}) %collective-permute-start) | collective-permute-done | bytes 524320 | tf_op jit(solution)/shard_map/ppermute | solution.py:12
  46.3 36.7 %conditional.5 = (bf16[2,256,512]{2,1,0:T(8,128)(2,1)}, bf16[2,256,512]{2,1,0:T(8,128)(2,1)}, f32[512,1536]{1,0:T(8,128)}, f32[512,512]{1,0:T(8,128)}, f32[512,2...) conditional(s32[]{:T(128)} %convert_element_type.312, ...), branch_computations={%region_10.35_spmd, %region_35.44_spmd} | conditional | flops 6523716096 | bytes 247859520 | solution.py:342
  53.4 2.1 convolution_convert_fusion.11
  60.4 7.6 %fusion.61 = (bf16[256,2048]{1,0:T(8,128)(2,1)S(1)}, f32[256,2048]{1,0:T(8,128)}) fusion(bf16[256,512]{1,0:T(8,128)(2,1)S(1)} %add_convert_fusion.15, bf16[512,2048]{1,0:T(8,128)(2,1)} %get-tuple-element.510), kind=kOutput, calls=%fused_computation.173 | convolution fusion | flops 570949632 | bytes 5505024 | tf_op jit(solution)/shard_map/cond/branch_1_fun/dot_general | solution.py:16
  74.2 1.6 broadcast_in_dim.268
  75.8 2.0 broadcast_in_dim.264
  77.9 2.5 broadcast_in_dim.267
  80.4 2.5 broadcast_in_dim.266
  84.3 36.2 %collective-permute-start.1 = (bf16[256,1024]{0,1:T(8,128)(2,1)S(1)}, bf16[256,1024]{0,1:T(8,128)(2,1)S(1)}, u32[]{:S(2)}, u32[]{:S(2)}) collective-permute-start(bf16[256,1024]{0,1:T(8,128)(2,1)S(1)} %copy.168), channel_id=1, source_target_pairs={{0,16},{1,17},{2,18},{3,19},{4,20},{5,21},{6,22},{7,23},{8,24},{9,... | collective-permute-start | bytes 1572872 | tf_op jit(solution)/shard_map/ppermute | solution.py:12
  123.0 8.6 %collective-permute-done.1 = bf16[256,1024]{0,1:T(8,128)(2,1)S(1)} collective-permute-done((bf16[256,1024]{0,1:T(8,128)(2,1)S(1)}, bf16[256,1024]{0,1:T(8,128)(2,1)S(1)}, u32[]{:S(2)}, u32[]{:S(2)}) %collective-permute-start.1) | collective-permute-done | bytes 524320 | tf_op jit(solution)/shard_map/ppermute | solution.py:12
  131.7 5.5 collective-permute-done.2
  137.2 92.8 %conditional.6 = (bf16[2,256,512]{2,1,0:T(8,128)(2,1)}, f32[512,1536]{1,0:T(8,128)}, f32[512,512]{1,0:T(8,128)}, f32[512,2048]{1,0:T(8,128)}, f32[2048,512]{1,0:...) conditional(s32[]{:T(128)} %convert_element_type.312, ...), branch_computations={%region_44.69_spmd, %region_69.89_spmd} | conditional | flops 6527388672 | bytes 227940368 | solution.py:342
  150.1 1.5 convolution_convert_fusion.24
  151.7 1.6 multiply_reduce_fusion.30
  154.6 7.1 %fusion.120 = bf16[256,2048]{1,0:T(8,128)(2,1)S(1)} fusion(f32[256,2048]{1,0:T(8,128)} %get-tuple-element.539, bf16[2048,512]{1,0:T(8,128)(2,1)S(1)} %copy-done.51, f32[256,512]{1,0:T(8,128)S(1)} %get-tuple-element.995, f32[256]{0:T(256)S(1)} %negate_multiply_fusion.13), kind=kOutput, calls=%fused_computation.349 | convolution fusion | flops 574881792 | bytes 5768192 | tf_op jit(solution)/shard_map/cond/branch_1_fun/dot_general | solution.py:26
  165.9 2.5 copy.173
  168.4 1.7 fusion.128
  171.5 1.4 fusion.217
  175.4 2.2 multiply_reduce_fusion.29
  179.0 2.9 copy.176
  181.9 2.3 convolution_add_fusion.14
  184.2 1.8 copy.160
  186.1 3.6 copy.171
  189.7 4.1 fusion.115
  193.7 3.6 copy.156
  197.3 5.5 copy.175
  202.8 5.0 bitcast_add_fusion.2
  207.8 5.3 copy.159
  213.2 5.5 copy.174
  218.6 4.9 bitcast_add_fusion.3
  223.5 5.4 copy.158
  232.6 13.2 %collective-permute-done.3 = bf16[256,1024]{1,0:T(8,128)(2,1)} collective-permute-done((bf16[256,1024]{1,0:T(8,128)(2,1)S(1)}, bf16[256,1024]{1,0:T(8,128)(2,1)}, u32[]{:S(2)}, u32[]{:S(2)}) %collective-permute-start.3) | collective-permute-done | bytes 524320 | tf_op jit(solution)/shard_map/ppermute | solution.py:12
  245.8 84.4 %conditional.7 = (f32[512,1024]{1,0:T(8,128)S(1)}, f32[3,512]{1,0:T(4,128)S(1)}, f32[3,512]{1,0:T(4,128)S(1)}, bf16[1,2,1,256,512]{4,3,2,1,0:T(8,128)(2,1)}, f32...) conditional(s32[]{:T(128)} %convert_element_type.312, ...), branch_computations={%region_89.0_spmd, %region_90.110_spmd} | conditional | flops 4154985728 | bytes 199171520 | solution.py:362
  251.0 1.5 copy.184
  252.5 1.6 convolution_convert_fusion.27
  255.7 7.0 %fusion.149 = bf16[256,2048]{1,0:T(8,128)(2,1)S(1)} fusion(f32[256,2048]{1,0:T(8,128)} %get-tuple-element.579, bf16[2048,512]{1,0:T(8,128)(2,1)S(1)} %copy-done.52, f32[256,512]{1,0:T(8,128)S(1)} %get-tuple-element.1001, f32[256]{0:T(256)S(1)} %negate_multiply_fusion.17), kind=kOutput, calls=%fused_computation.438 | convolution fusion | flops 574881792 | bytes 5768192 | tf_op jit(solution)/shard_map/cond/branch_1_fun/dot_general | solution.py:26
  266.4 1.9 fusion.215
  268.3 2.5 copy.186
  270.8 1.6 fusion.157
  277.7 2.3 multiply_reduce_fusion.39
  281.5 2.9 copy.189
  284.4 2.2 convolution_add_fusion.15
  286.7 3.6 copy.185
  290.3 4.1 fusion.144
  294.5 3.6 copy.220
  298.1 5.4 copy.188
  303.5 5.2 bitcast_add_fusion.5
  308.7 5.3 copy.226
  314.0 5.4 copy.187
  319.5 4.9 bitcast_add_fusion.6
  324.4 5.4 copy.224
  331.5 61.5 %all-reduce.2 = (f32[1,3,512]{2,0,1:T(1,128)}, f32[1,3,512]{2,0,1:T(1,128)}) all-reduce(f32[1,3,512]{2,0,1:T(1,128)S(1)} %broadcast_in_dim.316, f32[1,3,512]{2,0,1:T(1,128)S(1)} %broadcast_in_dim.317), channel_id=1, replica_groups=mesh['section'=2,'dp'=16] {'dp'}, use_global_device_ids=true, to_apply=%region_115.0 | all-reduce | flops 3072 | bytes 24576 | tf_op jit(solution)/shard_map/psum | solution.py:365
  393.0 207.1 %all-reduce.6.cloned.1.call-done = (f32[1,512,1536]{2,1,0:T(8,128)}, f32[1,512,512]{2,1,0:T(8,128)}, f32[1,512,2048]{2,1,0:T(8,128)}, f32[1,2048,512]{2,1,0:T(8,128)}, f32[1,512,1024]{2,1,0:T(8,128)}) async-done(((f32[1,512,1536]{2,1,0:T(8,128)}, f32[1,512,512]{2,1,0:T(8,128)}, f32[1,512,2048]{2,1,0:T(8,128)}, f32[1,2048,512]{2,1,0:T(8,128)}, f32[1,512,1024]{2,1,0:T(8,128)}), (f32[1,512,1536]{2,1,0:T(8,128)}, ...) | async-done | bytes 14680080 | tf_op jit(solution)/shard_map/psum | solution.py:365
  600.1 3.9 copy.361
  605.0 2.1 copy.363
  607.1 1.6 copy-done.69
  608.7 2.1 copy.364
  (305 shorter events, 69.2 us)
Async XLA Ops:
  7.2 592.9 %all-reduce.6.cloned.1.call-start = ((), (), s32[]{:S(2)}) async-start(), calls=%async_computation | async-start | bytes 29360128 | tf_op jit(solution)/shard_map/psum | solution.py:365
  10.4 2.2 copy-start.78
  14.8 7.6 %copy-start.92 = (bf16[8,64,256]{2,1,0:T(8,128)(2,1)}, bf16[8,64,256]{2,1,0:T(8,128)(2,1)S(1)}, u32[]{:S(2)}) copy-start(bf16[8,64,256]{2,1,0:T(8,128)(2,1)S(1)} %convolution_convert_fusion.2) | copy-start | bytes 786436 | tf_op jit(solution)/shard_map/cond
  14.8 1.7 copy-start.132
  15.5 6.9 %copy-start.29 = (f32[256,512]{1,0:T(8,128)}, f32[256,512]{1,0:T(8,128)S(1)}, u32[]{:S(2)}) copy-start(f32[256,512]{1,0:T(8,128)S(1)} %get-tuple-element.1139) | copy-start | bytes 1572868 | tf_op jit(solution)/shard_map/cond
  16.5 5.9 copy-start.116
  16.5 5.9 copy-start.47
  22.4 1.5 copy-start.45
  23.9 5.4 copy-start.4
  25.2 6.2 copy-start.30
  31.4 14.8 %copy-start.31 = (f32[256,512]{1,0:T(8,128)}, f32[256,512]{1,0:T(8,128)S(1)}, u32[]{:S(2)}) copy-start(f32[256,512]{1,0:T(8,128)S(1)} %get-tuple-element.1255) | copy-start | bytes 1572868
  32.9 13.4 %collective-permute-start = (bf16[256,1024]{0,1:T(8,128)(2,1)S(1)}, bf16[256,1024]{0,1:T(8,128)(2,1)S(1)}, u32[]{:S(2)}, u32[]{:S(2)}) collective-permute-start(bf16[256,1024]{0,1:T(8,128)(2,1)S(1)} %copy.167), channel_id=1, source_target_pairs={{0,16},{1,17},{2,18},{3,19},{4,20},{5,21},{6,22},{7,23},{8,24},{9,... | collective-permute-start | bytes 1572872 | tf_op jit(solution)/shard_map/ppermute | solution.py:12
  53.4 2.2 copy-start.74
  58.5 9.5 %copy-start.27 = (f32[256,512]{1,0:T(8,128)}, f32[256,512]{1,0:T(8,128)S(1)}, u32[]{:S(2)}) copy-start(f32[256,512]{1,0:T(8,128)S(1)} %get-tuple-element.1181) | copy-start | bytes 1572868 | tf_op jit(solution)/shard_map/cond
  59.1 9.0 %copy-start.114 = (bf16[256,512]{1,0:T(8,128)(2,1)}, bf16[256,512]{1,0:T(8,128)(2,1)S(1)}, u32[]{:S(2)}) copy-start(bf16[256,512]{1,0:T(8,128)(2,1)S(1)} %add_convert_fusion.15) | copy-start | bytes 786436 | tf_op jit(solution)/shard_map/cond
  60.4 7.6 %copy-start.49 = (bf16[2048,512]{1,0:T(8,128)(2,1)S(1)}, bf16[2048,512]{1,0:T(8,128)(2,1)}, u32[]{:S(2)}) copy-start(bf16[2048,512]{1,0:T(8,128)(2,1)} %get-tuple-element.511) | copy-start | bytes 6291460 | tf_op jit(solution)/shard_map/cond
  68.0 2.1 copy-start.8
  69.0 4.1 copy-start.33
  70.1 5.7 copy-start.76
  82.9 54.2 %copy-start.131 = (bf16[256,512]{1,0:T(8,128)(2,1)}, bf16[256,512]{1,0:T(8,128)(2,1)S(1)}, u32[]{:S(2)}) copy-start(bf16[256,512]{1,0:T(8,128)(2,1)S(1)} %get-tuple-element.1299) | copy-start | bytes 786436
  84.3 47.4 %collective-permute-start.1 = (bf16[256,1024]{0,1:T(8,128)(2,1)S(1)}, bf16[256,1024]{0,1:T(8,128)(2,1)S(1)}, u32[]{:S(2)}, u32[]{:S(2)}) collective-permute-start(bf16[256,1024]{0,1:T(8,128)(2,1)S(1)} %copy.168), channel_id=1, source_target_pairs={{0,16},{1,17},{2,18},{3,19},{4,20},{5,21},{6,22},{7,23},{8,24},{9,... | collective-permute-start | bytes 1572872 | tf_op jit(solution)/shard_map/ppermute | solution.py:12
  121.7 15.4 %collective-permute-start.2 = (bf16[256,1024]{1,0:T(8,128)(2,1)S(1)}, bf16[256,1024]{1,0:T(8,128)(2,1)}, u32[]{:S(2)}, u32[]{:S(2)}) collective-permute-start(bf16[256,1024]{1,0:T(8,128)(2,1)S(1)} %copy.169), channel_id=1, source_target_pairs={{16,0},{17,1},{18,2},{19,3},{20,4},{21,5},{22,6},{23,7},{24,8},{25... | collective-permute-start | bytes 1572872 | tf_op jit(solution)/shard_map/ppermute | solution.py:12
  144.9 5.2 copy-start.12
  145.1 6.5 %copy-start.25 = (f32[2,256,512]{2,1,0:T(8,128)S(1)}, f32[2,256,512]{2,1,0:T(8,128)}, u32[]{:S(2)}) copy-start(f32[2,256,512]{2,1,0:T(8,128)} %get-tuple-element.534) | copy-start | bytes 3145732 | tf_op jit(solution)/shard_map/cond
  151.6 2.9 copy-start.51
  154.5 8.5 %copy-start.67 = (f32[256,512]{1,0:T(8,128)}, f32[256,512]{1,0:T(8,128)S(1)}, u32[]{:S(2)}) copy-start(f32[256,512]{1,0:T(8,128)S(1)} %get-tuple-element.995) | copy-start | bytes 1572868 | tf_op jit(solution)/shard_map/cond
  154.6 7.1 %copy-start.32 = (f32[256,512]{1,0:T(8,128)S(1)}, f32[256,512]{1,0:T(8,128)}, u32[]{:S(2)}) copy-start(f32[256,512]{1,0:T(8,128)} %get-tuple-element.542) | copy-start | bytes 1572868 | tf_op jit(solution)/shard_map/cond
  154.6 7.1 %copy-start.135 = (bf16[512,2048]{1,0:T(8,128)(2,1)S(1)}, bf16[512,2048]{1,0:T(8,128)(2,1)}, u32[]{:S(2)}) copy-start(bf16[512,2048]{1,0:T(8,128)(2,1)} %get-tuple-element.541) | copy-start | bytes 6291460 | tf_op jit(solution)/shard_map/cond
  163.0 1.8 copy-start.65
  168.4 3.0 copy-start.73
  174.6 2.9 copy-start.104
  175.0 2.5 copy-start.123
  186.0 3.6 copy-start.79
  186.0 3.6 copy-start.105
  186.0 3.6 copy-start.124
  197.3 5.5 copy-start.46
  197.3 5.5 copy-start.68
  213.2 5.5 copy-start.99
  213.2 5.5 copy-start.117
  231.3 14.5 %collective-permute-start.3 = (bf16[256,1024]{1,0:T(8,128)(2,1)S(1)}, bf16[256,1024]{1,0:T(8,128)(2,1)}, u32[]{:S(2)}, u32[]{:S(2)}) collective-permute-start(bf16[256,1024]{1,0:T(8,128)(2,1)S(1)} %copy.177), channel_id=1, source_target_pairs={{16,0},{17,1},{18,2},{19,3},{20,4},{21,5},{22,6},{23,7},{24,8},{25... | collective-permute-start | bytes 1572872 | tf_op jit(solution)/shard_map/ppermute | solution.py:12
  245.8 6.7 %copy-start.13 = (bf16[512,1024]{1,0:T(8,128)(2,1)S(1)}, bf16[512,1024]{1,0:T(8,128)(2,1)}, u32[]{:S(2)}) copy-start(bf16[512,1024]{1,0:T(8,128)(2,1)} %get-tuple-element.576) | copy-start | bytes 3145732 | tf_op jit(solution)/shard_map/cond
  248.4 5.7 copy-start.26
  252.5 1.6 copy-start.34
  254.1 1.6 copy-start.52
  254.8 9.2 %copy-start.66 = (f32[256,512]{1,0:T(8,128)}, f32[256,512]{1,0:T(8,128)S(1)}, u32[]{:S(2)}) copy-start(f32[256,512]{1,0:T(8,128)S(1)} %get-tuple-element.1001) | copy-start | bytes 1572868 | tf_op jit(solution)/shard_map/cond
  255.7 7.0 %copy-start.28 = (f32[256,512]{1,0:T(8,128)S(1)}, f32[256,512]{1,0:T(8,128)}, u32[]{:S(2)}) copy-start(f32[256,512]{1,0:T(8,128)} %get-tuple-element.582) | copy-start | bytes 1572868 | tf_op jit(solution)/shard_map/cond
  255.7 7.1 %copy-start.136 = (bf16[512,2048]{1,0:T(8,128)(2,1)S(1)}, bf16[512,2048]{1,0:T(8,128)(2,1)}, u32[]{:S(2)}) copy-start(bf16[512,2048]{1,0:T(8,128)(2,1)} %get-tuple-element.581) | copy-start | bytes 6291460 | tf_op jit(solution)/shard_map/cond
  264.0 1.2 copy-start.63
  276.9 3.0 copy-start.106
  277.4 2.6 copy-start.125
  277.7 2.3 copy-start.127
  281.5 2.9 copy-start.77
  286.7 3.7 copy-start.75
  286.7 3.7 copy-start.107
  286.7 3.7 copy-start.126
  286.7 3.6 copy-start.128
  298.1 5.4 copy-start.44
  314.0 5.5 copy-start.97
  314.0 5.5 copy-start.115
  330.1 1.3 copy-start.53
  600.1 3.9 copy-start.118
  600.1 4.9 copy-start.70
  605.0 3.7 copy-start.69
  608.7 3.1 copy-start.93
  (9 other events, 9.2 us)
Sparse Core Ops, SparseCore 0:
  331.6 268.4 all-reduce.5
where the time goes:
time: 629 us; the launch traced here: 620 us
  waiting for transfers between devices  244 us (39%)
  local copies, waits for them, and re-layouts  120 us (19%)
  matrix products  93.6 us (15%)
  blocking collectives  61.5 us (10%)
  starting transfers between devices  40.1 us (6%)
  other arithmetic  30 us (5%)
  loops' own time  16.2 us (3%)
  between operations  14.7 us (2%)
    psum x1, waiting for transfers between devices, local(): lax.psum((grads[0], grads[1], grads[2], grads[3], grads[4], grads[5], gra...  207 us
    another operation x23, local copies, waits for them, and re-layouts  62.8 us
    psum x1, blocking collectives, local(): lax.psum((grads[0], grads[1], grads[2], grads[3], grads[4], grads[5], gra...  61.5 us
    ppermute x4, starting transfers between devices, shifted(): lax.ppermute(value, axis, [(source, source + steps) for source in range(l...  40.1 us
    ppermute x4, waiting for transfers between devices, shifted(): lax.ppermute(value, axis, [(source, source + steps) for source in range(l...  37.2 us
    dot_general x10, matrix products, product_tn(): lax.dot_general(left_side, right_side, (((0,), (0,)), ((), ())), preferre...  36.1 us
    dot_general x10, matrix products, product(): return jnp.dot(left_side, right_side, preferred_element_type=jnp.float32)  24.2 us
    dot_general x10, matrix products, product_nt(): lax.dot_general(left_side, right_side, (((1,), (1,)), ((), ())), preferre...  24 us
  transfers between devices with their start and end apart: 5, of which 5 were waited for; matrix products, arithmetic and copies ran while one was open for 1% of the time, Pallas kernels for 0%

commit v1 on v0

--- a/solution.py
+++ b/solution.py
@@ -1,7 +1,175 @@
+import functools
 import jax
 import jax.numpy as jnp
 from jax import lax
+from jax.experimental import pallas as pl
+from jax.experimental.pallas import tpu as pltpu
 from jax.sharding import PartitionSpec as P
+MESH = pl.DeviceIdType.MESH
+
+def peers():
+    sec = lax.axis_index("section"); dp = lax.axis_index("dp")
+    n = lax.axis_size("dp") // 2
+    core = lax.rem(dp, 2); chip = dp // 2
+    x = lax.rem(chip, 2); z = chip // 2
+    pos = jnp.where(x == 0, z, n - 1 - z)
+    def at(q):
+        q = lax.rem(q + n, n)
+        zz = jnp.where(q < n // 2, q, n - 1 - q)
+        xx = jnp.where(q < n // 2, 0, 1)
+        return (zz * 2 + xx) * 2 + core
+    return sec, dp, n, core, pos, at(pos + 1), at(pos - 1), dp + 1 - 2 * core
+
+def barrier(sec, targets):
+    bar = pltpu.get_barrier_semaphore()
+    for t in targets:
+        pl.semaphore_signal(bar, inc=1, device_id=(sec, t), device_id_type=MESH)
+    pl.semaphore_wait(bar, len(targets))
+
+def ring_kernel(n, units, g0, g1, ng, o0, o1, o_norm,
+                G0, G1, NG, S0, S1, NS, R0, R1, NR, E0, E1, NE,
+                ld_sem, sib_s, sib_r, rs_s, rs_r, ag_s, ag_r, sh_s, sh_r, o_sem):
+    sec, dp, _, core, pos, nxt, prv, sibling = peers()
+    loads = [pltpu.make_async_copy(g0, G0, ld_sem.at[0]), pltpu.make_async_copy(g1, G1, ld_sem.at[1]), pltpu.make_async_copy(ng, NG, ld_sem.at[2])]
+    for c in loads: c.start()
+    barrier(sec, [nxt, prv, sibling])
+    for c in loads: c.wait()
+    half = 16 * n
+    def rows(d, k, c=core):
+        return pl.ds(pl.multiple_of(c * 2 * half + d * half + k * 16, 16), 16)
+    def srows(d, k):
+        return pl.ds(pl.multiple_of(d * half + k * 16, 16), 16)
+    class Stream: pass
+    streams = []
+    for gi, (G, S, R, E) in enumerate(((G0, S0, R0, E0), (G1, S1, R1, E1))):
+        for d in (0, 1):
+            st = Stream(); st.i = gi * 2 + d; st.d = d; st.g = gi
+            st.own = lambda k, G=G, d=d: G.at[:, rows(d, k), :]
+            st.other = lambda k, G=G, d=d: G.at[:, rows(d, k, 1 - core), :]
+            st.sib = lambda k, S=S, d=d: S.at[:, srows(d, k), :]
+            st.rs = lambda s, R=R, d=d: R.at[d, s]
+            st.res = lambda k, E=E, d=d: E.at[:, rows(d, k), :]
+            st.res_other = lambda k, E=E, d=d: E.at[:, rows(d, k, 1 - core), :]
+            st.to = nxt if d == 0 else prv
+            streams.append(st)
+    st = Stream(); st.i = 4; st.d = 0; st.g = 2
+    st.own = lambda k: NG.at[core, k]; st.other = lambda k: NG.at[1 - core, k]; st.sib = lambda k: NS.at[k]
+    st.rs = lambda s: NR.at[s]; st.res = lambda k: NE.at[core, k]; st.res_other = lambda k: NE.at[1 - core, k]; st.to = nxt
+    streams.append(st)
+    def chunk(st, s):
+        return lax.rem(pos - s + 2 * n, n) if st.d == 0 else lax.rem(pos + s, n)
+    def remote(src, dst, ss, rs, to):
+        return pltpu.make_async_remote_copy(src_ref=src, dst_ref=dst, send_sem=ss, recv_sem=rs, device_id=(sec, to), device_id_type=MESH)
+    def sib_copy(st, k): return remote(st.other(k), st.sib(k), sib_s.at[st.i, k], sib_r.at[st.i, k], sibling)
+    def rs_copy(st, s): return remote(st.own(chunk(st, s)), st.rs(s), rs_s.at[st.i, s], rs_r.at[st.i, s], st.to)
+    def ag_copy(st, t):
+        k = chunk(st, t + n - 1)
+        return remote(st.res(k), st.res(k), ag_s.at[st.i, t], ag_r.at[st.i, t], st.to)
+    def sh_copy(st, t):
+        k = chunk(st, t + n - 1)
+        return remote(st.res(k), st.res(k), sh_s.at[st.i, t], sh_r.at[st.i, t], sibling)
+    def loop(a, b, f):
+        lax.fori_loop(a, b, lambda i, c: (f(i), c)[1], 0)
+    def f32(r): return r[...].astype(jnp.float32)
+    def share(s):
+        for st in streams: sib_copy(st, chunk(st, s)).start()
+    loop(0, n, share)
+    def first():
+        for st in streams:
+            k = chunk(st, 0)
+            sib_copy(st, k).wait_recv()
+            own = st.own(k)
+            own[...] = (f32(own) + f32(st.sib(k))).astype(own.dtype)
+            rs_copy(st, 0).start()
+    first()
+    def middle(s):
+        for st in streams:
+            k = chunk(st, s)
+            sib_copy(st, k).wait_recv()
+            rs_copy(st, s - 1).wait_recv()
+            own = st.own(k)
+            own[...] = (f32(own) + f32(st.sib(k)) + f32(st.rs(s - 1))).astype(own.dtype)
+            rs_copy(st, s).start()
+    loop(1, n - 1, middle)
+    for st in streams:
+        k = chunk(st, n - 1)
+        sib_copy(st, k).wait_recv()
+        rs_copy(st, n - 2).wait_recv()
+        own = st.own(k); res = st.res(k)
+        res[...] = (f32(own) + f32(st.sib(k)) + f32(st.rs(n - 2))).astype(own.dtype)
+        ag_copy(st, 0).start()
+        sh_copy(st, 0).start()
+    def out_copy(st, k, c, slot):
+        src = st.res(k) if c == 0 else st.res_other(k)
+        if st.g == 2:
+            return pltpu.make_async_copy(src, o_norm.at[core if c == 0 else 1 - core, k], o_sem.at[st.i, slot])
+        row = rows(st.d, k, core if c == 0 else 1 - core)
+        return pltpu.make_async_copy(src, (o0, o1)[st.g].at[:, row, :], o_sem.at[st.i, slot])
+    def emit(st, t):
+        k = chunk(st, t + n - 1)
+        sh_copy(st, t).wait_recv()
+        out_copy(st, k, 0, 2 * t).start()
+        out_copy(st, k, 1, 2 * t + 1).start()
+    def gather(t):
+        for st in streams:
+            ag_copy(st, t).wait_recv()
+            @pl.when(t < n - 2)
+            def _(): ag_copy(st, t + 1).start()
+            sh_copy(st, t + 1).start()
+        for st in streams:
+            emit(st, t)
+    loop(0, n - 1, gather)
+    for st in streams:
+        emit(st, n - 1)
+    def drain(s):
+        for st in streams:
+            sib_copy(st, s).wait_send(); sh_copy(st, s).wait_send()
+            out_copy(st, chunk(st, s + n - 1), 0, 2 * s).wait(); out_copy(st, chunk(st, s + n - 1), 1, 2 * s + 1).wait()
+            @pl.when(s < n - 1)
+            def _():
+                rs_copy(st, s).wait_send(); ag_copy(st, s).wait_send()
+    loop(0, n, drain)
+
+def all_reduce(g0, g1, ng, n):
+    u0, u1 = g0.shape[0], g1.shape[0]
+    bf, f4 = jnp.bfloat16, jnp.float32
+    any_ = pl.BlockSpec(memory_space=pl.ANY)
+    V = pltpu.VMEM; D = pltpu.SemaphoreType.DMA
+    return pl.pallas_call(
+        functools.partial(ring_kernel, n, (u0, u1)),
+        out_shape=[jax.ShapeDtypeStruct(a.shape, a.dtype) for a in (g0, g1, ng)], in_specs=[any_] * 3, out_specs=[any_] * 3,
+        scratch_shapes=[V(g0.shape, bf), V(g1.shape, bf), V(ng.shape, f4),
+            V((u0, 32 * n, 512), bf), V((u1, 32 * n, 512), bf), V((n, 8, 128), f4),
+            V((2, n - 1, u0, 16, 512), bf), V((2, n - 1, u1, 16, 512), bf), V((n - 1, 8, 128), f4),
+            V(g0.shape, bf), V(g1.shape, bf), V(ng.shape, f4),
+            D((3,)), D((5, n)), D((5, n)), D((5, n)), D((5, n)), D((5, n)), D((5, n)), D((5, n)), D((5, n)), D((5, 2 * n))],
+        compiler_params=pltpu.CompilerParams(collective_id=0, has_side_effects=True, vmem_limit_bytes=60 * 2**20),
+        name="ring",
+    )(g0, g1, ng)
+
+
+def pack_blocks(blocks, n):
+    flat = jnp.concatenate(blocks, axis=0).astype(jnp.bfloat16)
+    units = -(-flat.shape[0] // (64 * n))
+    flat = jnp.pad(flat, ((0, units * 64 * n - flat.shape[0]), (0, 0)))
+    return flat.reshape(units, 64 * n, 512)
+
+def columns(weight):
+    return [weight[:, 512 * j:512 * (j + 1)] for j in range(weight.shape[1] // 512)]
+
+def pack_norm(gain, bias, n):
+    both = jnp.stack([gain, bias]).reshape(2, 3, 4, 128).transpose(0, 2, 1, 3)
+    return jnp.pad(both, ((0, 0), (0, n - 4), (0, 5), (0, 0)))
+
+def sum_gradients(grads, n):
+    g_qkv, g_out, g_up, g_down, g_cross, g_gain, g_bias = grads[:7]
+    e0, e1, en = all_reduce(pack_blocks(columns(g_up) + [g_down], n), pack_blocks(columns(g_qkv) + [g_out] + columns(g_cross), n), pack_norm(g_gain, g_bias, n), n)
+    e0 = e0.reshape(-1, 512)[:8 * 512].reshape(8, 512, 512)
+    e1 = e1.reshape(-1, 512)[:6 * 512].reshape(6, 512, 512)
+    def wide(blocks):
+        return blocks.transpose(1, 0, 2).reshape(512, -1).astype(jnp.float32)
+    en = en[:, :4, :3].transpose(0, 2, 1, 3).reshape(2, 3, 512)
+    return (wide(e1[:3]), e1[3].astype(jnp.float32), wide(e0[:4]), e0[4:].reshape(2048, 512).astype(jnp.float32), wide(e1[4:]), en[0], en[1])
 
 HEADS = 8
 
@@ -362,9 +530,7 @@
     in_grads, grads = lax.cond(
         is_encoder, full_encoder, full_decoder, (in_grads, grads, arrived_back)
     )
-    sum_qkv, sum_out, sum_up, sum_down, sum_cross, sum_gain, sum_bias = lax.psum(
-        (grads[0], grads[1], grads[2], grads[3], grads[4], grads[5], grads[6]), "dp"
-    )
+    sum_qkv, sum_out, sum_up, sum_down, sum_cross, sum_gain, sum_bias = sum_gradients(grads, lax.axis_size("dp") // 2)
     return (
         results[None, :, None],
         in_grads[None, :, None],

time: 629 us -> 463 us (0.74)
  waiting for transfers between devices: 244 us -> 37.1 us
  Pallas kernels: 0 us -> 82.6 us
  blocking collectives: 61.5 us -> 0 us
  local copies, waits for them, and re-layouts: 120 us -> 143 us
  other arithmetic: 30 us -> 45 us
  between operations: 14.7 us -> 1.31 us
    psum x1 -> x0, waiting for transfers between devices: 207 us -> none  [local(): lax.psum((grads[0], grads[1], grads[2], grads[3], grads[4], grads[5], gra...]
    pallas_call x0 -> x1, Pallas kernels: none -> 82.6 us  [all_reduce(): pl.pallas_call(functools.partial(ring_kernel, n, (u0, u1)), out_shape=[ja...]
    psum x1 -> x0, blocking collectives: 61.5 us -> none  [local(): lax.psum((grads[0], grads[1], grads[2], grads[3], grads[4], grads[5], gra...]
    cond x4 -> x2, local copies, waits for them, and re-layouts: 15.7 us -> 4.92 us  [local(): lax.cond(is_encoder, full_encoder, full_decoder, (in_grads, grads, arrive...]
    convert_element_type x0 -> x3, local copies, waits for them, and re-layouts: none -> 10.6 us  [wide(): return blocks.transpose(1, 0, 2).reshape(512, -1).astype(jnp.float32)]
    concatenate x0 -> x3, local copies, waits for them, and re-layouts: none -> 9.72 us  [pack_blocks(): flat = jnp.concatenate(blocks, axis=0).astype(jnp.bfloat16)]
    convert_element_type x0 -> x4, other arithmetic: none -> 8.51 us  [the longest x2 3.61 us: wide(): return blocks.transpose(1, 0, 2).reshape(512, -1).astype(jnp.float32)]
    unnamed x20, local copies, waits for them, and re-layouts: 15 us -> 22.3 us
  transfers between devices with their start and end apart: 5 -> 4, of which waited for: 5 -> 4; matrix products, arithmetic and copies ran while one was open for 1% -> 1% of each run, Pallas kernels for 0% -> 0%
where the time goes in v1:
time: 463 us; the launch traced here: 454 us
  local copies, waits for them, and re-layouts  143 us (31%)
  matrix products  89 us (19%)
  Pallas kernels  82.6 us (18%)
  other arithmetic  45 us (10%)
  starting transfers between devices  39.7 us (9%)
  waiting for transfers between devices  37.1 us (8%)
  loops' own time  16.3 us (4%)
    pallas_call x1, Pallas kernels, all_reduce(): pl.pallas_call(functools.partial(ring_kernel, n, (u0, u1)), out_shape=[ja...  82.6 us
    another operation x23, local copies, waits for them, and re-layouts  63 us
    ppermute x4, starting transfers between devices, shifted(): lax.ppermute(value, axis, [(source, source + steps) for source in range(l...  39.7 us
    ppermute x4, waiting for transfers between devices, shifted(): lax.ppermute(value, axis, [(source, source + steps) for source in range(l...  37.1 us
    dot_general x10, matrix products, product_tn(): lax.dot_general(left_side, right_side, (((0,), (0,)), ((), ())), preferre...  31.5 us
    dot_general x10, matrix products, product_nt(): lax.dot_general(left_side, right_side, (((1,), (1,)), ((), ())), preferre...  24.3 us
    dot_general x10, matrix products, product(): return jnp.dot(left_side, right_side, preferred_element_type=jnp.float32)  23.9 us
    unnamed x20, local copies, waits for them, and re-layouts  22.3 us
  transfers between devices with their start and end apart: 4, of which 4 were waited for; matrix products, arithmetic and copies ran while one was open for 1% of the time, Pallas kernels for 0%

profile of v1, /device:TPU:0, one launch (start us, length us, event | category | flops | bytes accessed | tf_op | source)
XLA Modules:
  0.0 453.7 jit_solution(1443366510797149932)
XLA Ops:
  3.3 21.6 %conditional.4 = (bf16[2,256,512]{2,1,0:T(8,128)(2,1)}, bf16[256,1024]{1,0:T(8,128)(2,1)}, f32[256,512]{1,0:T(8,128)S(1)}, f32[256,512]{1,0:T(8,128)}, bf16[256,...) conditional(s32[]{:T(128)} %convert_element_type.399, ...), branch_computations={%region_0.0_spmd, %region_1.10_spmd} | conditional | flops 2058877696 | bytes 70392472 | solution.py:510
  3.8 2.1 convolution_convert_fusion
  9.9 5.8 %fusion.2 = (bf16[256,2048]{1,0:T(8,128)(2,1)S(1)}, f32[256,2048]{1,0:T(8,128)}) fusion(bf16[256,512]{1,0:T(8,128)(2,1)S(1)} %add_convert_fusion.1, bf16[512,2048]{1,0:T(8,128)(2,1)S(1)} %copy-done.123), kind=kOutput, calls=%fused_computation.4 | convolution fusion | flops 570949632 | bytes 5505024 | tf_op jit(solution)/shard_map/cond/branch_1_fun/dot_general | solution.py:184
  18.7 2.0 add_convert_fusion
  22.7 2.2 convolution_convert_fusion.1
  27.6 2.1 bitcast_convert_fusion.11
  29.8 9.9 %collective-permute-done = bf16[256,1024]{0,1:T(8,128)(2,1)S(1)} collective-permute-done((bf16[256,1024]{0,1:T(8,128)(2,1)S(1)}, bf16[256,1024]{0,1:T(8,128)(2,1)S(1)}, u32[]{:S(2)}, u32[]{:S(2)}) %collective-permute-start) | collective-permute-done | bytes 524320 | tf_op jit(solution)/shard_map/ppermute | solution.py:180
  39.7 37.3 %conditional.5 = (bf16[2,256,512]{2,1,0:T(8,128)(2,1)}, bf16[2,256,512]{2,1,0:T(8,128)(2,1)}, f32[512,1536]{1,0:T(8,128)}, f32[512,512]{1,0:T(8,128)}, f32[512,2...) conditional(s32[]{:T(128)} %convert_element_type.399, ...), branch_computations={%region_10.35_spmd, %region_35.44_spmd} | conditional | flops 6523716096 | bytes 247859520 | solution.py:510
  47.0 2.1 convolution_convert_fusion.11
  54.8 7.3 %fusion.61 = (bf16[256,2048]{1,0:T(8,128)(2,1)S(1)}, f32[256,2048]{1,0:T(8,128)}) fusion(bf16[256,512]{1,0:T(8,128)(2,1)} %add_convert_fusion.15, bf16[512,2048]{1,0:T(8,128)(2,1)} %get-tuple-element.593), kind=kOutput, calls=%fused_computation.173 | convolution fusion | flops 570949632 | bytes 5505024 | tf_op jit(solution)/shard_map/cond/branch_1_fun/dot_general | solution.py:184
  69.8 2.0 broadcast_in_dim.266
  71.9 2.5 broadcast_in_dim.269
  74.4 2.5 broadcast_in_dim.268
  78.3 35.7 %collective-permute-start.1 = (bf16[256,1024]{0,1:T(8,128)(2,1)S(1)}, bf16[256,1024]{0,1:T(8,128)(2,1)S(1)}, u32[]{:S(2)}, u32[]{:S(2)}) collective-permute-start(bf16[256,1024]{0,1:T(8,128)(2,1)S(1)} %copy.167), channel_id=1, source_target_pairs={{0,16},{1,17},{2,18},{3,19},{4,20},{5,21},{6,22},{7,23},{8,24},{9,... | collective-permute-start | bytes 1572872 | tf_op jit(solution)/shard_map/ppermute | solution.py:180
  116.6 8.6 %collective-permute-done.1 = bf16[256,1024]{0,1:T(8,128)(2,1)S(1)} collective-permute-done((bf16[256,1024]{0,1:T(8,128)(2,1)S(1)}, bf16[256,1024]{0,1:T(8,128)(2,1)S(1)}, u32[]{:S(2)}, u32[]{:S(2)}) %collective-permute-start.1) | collective-permute-done | bytes 524320 | tf_op jit(solution)/shard_map/ppermute | solution.py:180
  125.2 5.5 %collective-permute-done.2 = bf16[256,1024]{1,0:T(8,128)(2,1)} collective-permute-done((bf16[256,1024]{1,0:T(8,128)(2,1)S(1)}, bf16[256,1024]{1,0:T(8,128)(2,1)}, u32[]{:S(2)}, u32[]{:S(2)}) %collective-permute-start.2) | collective-permute-done | bytes 524320 | tf_op jit(solution)/shard_map/ppermute | solution.py:180
  130.7 94.1 %conditional.6 = (bf16[2,256,512]{2,1,0:T(8,128)(2,1)}, f32[512,1536]{1,0:T(8,128)}, f32[512,512]{1,0:T(8,128)}, f32[512,2048]{1,0:T(8,128)}, f32[2048,512]{1,0:...) conditional(s32[]{:T(128)} %convert_element_type.399, ...), branch_computations={%region_44.69_spmd, %region_69.89_spmd} | conditional | flops 6527388672 | bytes 227940368 | solution.py:510
  148.1 7.1 %fusion.120 = bf16[256,2048]{1,0:T(8,128)(2,1)S(1)} fusion(f32[256,2048]{1,0:T(8,128)} %get-tuple-element.622, bf16[2048,512]{1,0:T(8,128)(2,1)S(1)} %copy-done.51, f32[256,512]{1,0:T(8,128)S(1)} %get-tuple-element.1153, f32[256]{0:T(256)S(1)} %negate_multiply_fusion.13), kind=kOutput, calls=%fused_computation.349 | convolution fusion | flops 574881792 | bytes 5768192 | tf_op jit(solution)/shard_map/cond/branch_1_fun/dot_general | solution.py:194
  158.9 1.9 fusion.217
  160.8 2.5 copy.172
  170.2 2.2 multiply_reduce_fusion.29
  173.8 2.9 copy.175
  176.7 2.3 convolution_add_fusion.14
  180.9 3.6 copy.170
  184.5 4.1 fusion.115
  188.6 3.6 copy.155
  192.2 5.5 %copy.174 = f32[2048,512]{0,1:T(8,128)} copy(f32[2048,512]{1,0:T(8,128)} %get-tuple-element.972) | data formatting | bytes 8388608 | tf_op jit(solution)/shard_map
  197.7 5.0 %bitcast_add_fusion.2 = f32[2048,512]{0,1:T(8,128)} fusion(f32[2048,512]{0,1:T(8,128)} %copy.174, bf16[256,2048]{1,0:T(8,128)(2,1)S(1)} %copy-done.46, f32[256,512]{1,0:T(8,128)S(1)} %copy-done.68, f32[256]{0:T(256)S(1)} %negate_multiply_fusion.13), kind=kOutput, calls=%fused_computation.340 | convolution fusion | flops 538181632 | bytes 9962496 | tf_op jit(solution)/shard_map/cond/branch_1_fun/dot_general | solution.py:188
  202.6 5.3 %copy.158 = f32[2048,512]{1,0:T(8,128)} copy(f32[2048,512]{0,1:T(8,128)} %bitcast_add_fusion.2) | data formatting | bytes 8388608 | tf_op jit(solution)/shard_map
  208.0 5.5 %copy.173 = f32[512,2048]{0,1:T(8,128)} copy(f32[512,2048]{1,0:T(8,128)} %get-tuple-element.970) | data formatting | bytes 8388608 | tf_op jit(solution)/shard_map
  213.5 4.9 %bitcast_add_fusion.3 = f32[512,2048]{0,1:T(8,128)} fusion(f32[512,2048]{0,1:T(8,128)} %copy.173, bf16[256,2048]{1,0:T(8,128)(2,1)S(1)} %copy-done.97, bf16[256,512]{1,0:T(8,128)(2,1)S(1)} %copy-done.111), kind=kOutput, calls=%fused_computation.341 | convolution fusion | flops 537919488 | bytes 9699328 | tf_op jit(solution)/shard_map/cond/branch_1_fun/dot_general | solution.py:188
  218.3 5.4 %copy.157 = f32[512,2048]{1,0:T(8,128)} copy(f32[512,2048]{0,1:T(8,128)} %bitcast_add_fusion.3) | data formatting | bytes 8388608 | tf_op jit(solution)/shard_map
  227.3 13.1 %collective-permute-done.3 = bf16[256,1024]{1,0:T(8,128)(2,1)S(1)} collective-permute-done((bf16[256,1024]{1,0:T(8,128)(2,1)S(1)}, bf16[256,1024]{1,0:T(8,128)(2,1)S(1)}, u32[]{:S(2)}, u32[]{:S(2)}) %collective-permute-start.3) | collective-permute-done | bytes 524320 | tf_op jit(solution)/shard_map/ppermute | solution.py:180
  240.4 68.0 %conditional.7 = (bf16[1,2,1,256,512]{4,3,2,1,0:T(8,128)(2,1)}, f32[3,512]{1,0:T(4,128)S(1)}, f32[3,512]{1,0:T(4,128)S(1)}, bf16[512,512]{0,1:T(8,128)(2,1)}, bf...) conditional(s32[]{:T(128)} %convert_element_type.399, ...), branch_computations={%region_89.0_spmd.clone, %region_90.110_spmd.clone} | conditional | flops 4157607168 | bytes 171908384 | solution.py:530
  241.2 2.0 copy.239
  248.7 6.9 %fusion.151 = bf16[256,2048]{1,0:T(8,128)(2,1)S(1)} fusion(f32[256,2048]{1,0:T(8,128)} %get-tuple-element.1059, bf16[2048,512]{1,0:T(8,128)(2,1)S(1)} %copy-done.52, f32[256,512]{1,0:T(8,128)S(1)} %get-tuple-element.1159, f32[256]{0:T(256)S(1)} %negate_multiply_fusion.17), kind=kOutput, calls=%fused_computation.440 | convolution fusion | flops 574881792 | bytes 5768192 | tf_op jit(solution)/shard_map/cond/branch_1_fun/dot_general | solution.py:194
  255.6 1.9 copy.236
  257.5 2.5 multiply_reduce_fusion.41
  265.6 2.5 copy.233
  275.0 2.2 multiply_reduce_fusion.39
  278.4 3.6 copy.237
  282.0 4.1 fusion.146
  286.1 3.6 copy.240
  289.7 5.4 %copy.238 = f32[512,2048]{0,1:T(8,128)} copy(f32[512,2048]{1,0:T(8,128)} %get-tuple-element.1077) | data formatting | bytes 8388608 | tf_op jit(solution)/shard_map
  295.1 3.0 fusion.144
  299.5 5.4 %copy.234 = f32[2048,512]{0,1:T(8,128)} copy(f32[2048,512]{1,0:T(8,128)} %get-tuple-element.1066) | data formatting | bytes 8388608 | tf_op jit(solution)/shard_map
  304.9 3.2 fusion.145
  308.4 2.1 convert.121
  310.6 2.2 constant_dynamic-update-slice_fusion.4
  312.9 1.9 constant_dynamic-update-slice_fusion.3
  314.7 1.9 constant_dynamic-update-slice_fusion.2
  319.9 6.4 %copy.189 = bf16[4096,512]{1,0:T(8,128)(2,1)} copy(bf16[4096,512]{0,1:T(8,128)(2,1)} %constant_dynamic-update-slice_fusion) | data formatting | bytes 8388608 | tf_op jit(solution)/shard_map/concatenate | solution.py:152
  327.0 2.1 convert_dynamic-update-slice_fusion
  329.1 1.9 constant_dynamic-update-slice_fusion.6
  332.8 82.6 %ring.1 = (bf16[8,512,512]{2,1,0:T(8,128)(2,1)}, bf16[6,512,512]{2,1,0:T(8,128)(2,1)}, f32[2,8,8,128]{3,2,1,0:T(8,128)}) custom-call(bf16[8,512,512]{2,1,0:T(8,128)(2,1)} %bitcast.553, bf16[6,512,512]{2,1,0:T(8,128)(2,1)} %bitcast.564, f32[2,8,8,128]{3,2,1,0:T(8,128)} %pad.46.ng), custom_call_target="tpu_custom_call" | custom-call | tf_op jit(solution)/shard_map/ring/pallas_call | solution.py:138
  415.4 2.3 slice_convert_fusion
  419.2 2.1 convert_bitcast_fusion.1
  423.3 3.5 copy.192
  426.8 3.5 copy.197
  432.2 2.9 copy.199
  435.1 4.9 %fusion.223 = (bf16[4,512,512]{2,1,0:T(8,128)(2,1)S(1)}, f32[512,4,512]{2,0,1:T(8,128)}) fusion(bf16[8,512,512]{2,1,0:T(8,128)(2,1)} %get-tuple-element.796), kind=kLoop, calls=%fused_computation.589 | loop fusion | flops 1048576 | bytes 10485760 | tf_op jit(solution)/shard_map/slice | solution.py:172
  440.0 2.6 bitcast_convert_fusion.10
  442.6 5.2 %copy.193 = f32[512,4,512]{0,2,1:T(8,128)} copy(f32[512,4,512]{2,0,1:T(8,128)} %get-tuple-element.1294) | data formatting | bytes 8388608 | tf_op jit(solution)/shard_map/convert_element_type | solution.py:170
  447.8 5.3 %copy.198 = f32[1,512,2048]{2,1,0:T(8,128)} copy(f32[1,512,2048]{1,2,0:T(8,128)} %bitcast.554) | data formatting | bytes 8388608
  (305 shorter events, 91.1 us)
Async XLA Ops:
  3.8 2.2 copy-start.75
  5.9 1.1 copy-start.63
  7.5 1.0 copy-start.14
  8.2 7.6 %copy-start.89 = (bf16[8,64,256]{2,1,0:T(8,128)(2,1)}, bf16[8,64,256]{2,1,0:T(8,128)(2,1)S(1)}, u32[]{:S(2)}) copy-start(bf16[8,64,256]{2,1,0:T(8,128)(2,1)S(1)} %convolution_convert_fusion.2) | copy-start | bytes 786436 | tf_op jit(solution)/shard_map/cond
  8.2 1.7 copy-start.123
  8.9 6.9 %copy-start.29 = (f32[256,512]{1,0:T(8,128)}, f32[256,512]{1,0:T(8,128)S(1)}, u32[]{:S(2)}) copy-start(f32[256,512]{1,0:T(8,128)S(1)} %get-tuple-element.1313) | copy-start | bytes 1572868 | tf_op jit(solution)/shard_map/cond
  9.9 5.9 %copy-start.110 = (bf16[256,512]{1,0:T(8,128)(2,1)}, bf16[256,512]{1,0:T(8,128)(2,1)S(1)}, u32[]{:S(2)}) copy-start(bf16[256,512]{1,0:T(8,128)(2,1)S(1)} %add_convert_fusion.1) | copy-start | bytes 786436 | tf_op jit(solution)/shard_map/cond
  9.9 5.9 %copy-start.47 = (bf16[2048,512]{1,0:T(8,128)(2,1)S(1)}, bf16[2048,512]{1,0:T(8,128)(2,1)}, u32[]{:S(2)}) copy-start(bf16[2048,512]{1,0:T(8,128)(2,1)} %get-tuple-element.572) | copy-start | bytes 6291460 | tf_op jit(solution)/shard_map/cond
  15.8 1.5 copy-start.45
  17.3 5.4 %copy-start.4 = (bf16[512,1024]{1,0:T(8,128)(2,1)S(1)}, bf16[512,1024]{1,0:T(8,128)(2,1)}, u32[]{:S(2)}) copy-start(bf16[512,1024]{1,0:T(8,128)(2,1)} %get-tuple-element.573) | copy-start | bytes 3145732 | tf_op jit(solution)/shard_map/cond
  18.7 6.2 %copy-start.30 = (f32[256,512]{1,0:T(8,128)S(1)}, f32[256,512]{1,0:T(8,128)}, u32[]{:S(2)}) copy-start(f32[256,512]{1,0:T(8,128)} %copy-done.29) | copy-start | bytes 1572868 | tf_op jit(solution)/shard_map/cond
  24.9 14.8 %copy-start.31 = (f32[256,512]{1,0:T(8,128)}, f32[256,512]{1,0:T(8,128)S(1)}, u32[]{:S(2)}) copy-start(f32[256,512]{1,0:T(8,128)S(1)} %get-tuple-element.1437) | copy-start | bytes 1572868
  26.3 13.4 %collective-permute-start = (bf16[256,1024]{0,1:T(8,128)(2,1)S(1)}, bf16[256,1024]{0,1:T(8,128)(2,1)S(1)}, u32[]{:S(2)}, u32[]{:S(2)}) collective-permute-start(bf16[256,1024]{0,1:T(8,128)(2,1)S(1)} %copy.166), channel_id=1, source_target_pairs={{0,16},{1,17},{2,18},{3,19},{4,20},{5,21},{6,22},{7,23},{8,24},{9,... | collective-permute-start | bytes 1572872 | tf_op jit(solution)/shard_map/ppermute | solution.py:180
  47.0 2.2 copy-start.73
  49.1 1.1 copy-start.61
  50.7 1.0 copy-start.17
  52.1 9.9 %copy-start.27 = (f32[256,512]{1,0:T(8,128)}, f32[256,512]{1,0:T(8,128)S(1)}, u32[]{:S(2)}) copy-start(f32[256,512]{1,0:T(8,128)S(1)} %get-tuple-element.1355) | copy-start | bytes 1572868 | tf_op jit(solution)/shard_map/cond
  54.8 7.3 %copy-start.49 = (bf16[2048,512]{1,0:T(8,128)(2,1)S(1)}, bf16[2048,512]{1,0:T(8,128)(2,1)}, u32[]{:S(2)}) copy-start(bf16[2048,512]{1,0:T(8,128)(2,1)} %get-tuple-element.594) | copy-start | bytes 6291460 | tf_op jit(solution)/shard_map/cond
  62.1 1.0 copy-start.43
  62.1 2.1 copy-start.8
  63.0 4.0 copy-start.33
  64.1 5.7 %copy-start.90 = (bf16[256,512]{1,0:T(8,128)(2,1)}, bf16[256,512]{1,0:T(8,128)(2,1)S(1)}, u32[]{:S(2)}) copy-start(bf16[256,512]{1,0:T(8,128)(2,1)S(1)} %get-tuple-element.1357) | copy-start | bytes 786436 | tf_op jit(solution)/shard_map/cond
  77.0 53.8 %copy-start.120 = (bf16[256,512]{1,0:T(8,128)(2,1)}, bf16[256,512]{1,0:T(8,128)(2,1)S(1)}, u32[]{:S(2)}) copy-start(bf16[256,512]{1,0:T(8,128)(2,1)S(1)} %get-tuple-element.1475) | copy-start | bytes 786436
  78.3 46.9 %collective-permute-start.1 = (bf16[256,1024]{0,1:T(8,128)(2,1)S(1)}, bf16[256,1024]{0,1:T(8,128)(2,1)S(1)}, u32[]{:S(2)}, u32[]{:S(2)}) collective-permute-start(bf16[256,1024]{0,1:T(8,128)(2,1)S(1)} %copy.167), channel_id=1, source_target_pairs={{0,16},{1,17},{2,18},{3,19},{4,20},{5,21},{6,22},{7,23},{8,24},{9,... | collective-permute-start | bytes 1572872 | tf_op jit(solution)/shard_map/ppermute | solution.py:180
  115.3 15.4 %collective-permute-start.2 = (bf16[256,1024]{1,0:T(8,128)(2,1)S(1)}, bf16[256,1024]{1,0:T(8,128)(2,1)}, u32[]{:S(2)}, u32[]{:S(2)}) collective-permute-start(bf16[256,1024]{1,0:T(8,128)(2,1)S(1)} %copy.168), channel_id=1, source_target_pairs={{16,0},{17,1},{18,2},{19,3},{20,4},{21,5},{22,6},{23,7},{24,8},{25... | collective-permute-start | bytes 1572872 | tf_op jit(solution)/shard_map/ppermute | solution.py:180
  138.5 5.2 %copy-start.12 = (bf16[512,1024]{1,0:T(8,128)(2,1)S(1)}, bf16[512,1024]{1,0:T(8,128)(2,1)}, u32[]{:S(2)}) copy-start(bf16[512,1024]{1,0:T(8,128)(2,1)} %get-tuple-element.619) | copy-start | bytes 3145732 | tf_op jit(solution)/shard_map/cond
  138.6 6.5 %copy-start.25 = (f32[2,256,512]{2,1,0:T(8,128)S(1)}, f32[2,256,512]{2,1,0:T(8,128)}, u32[]{:S(2)}) copy-start(f32[2,256,512]{2,1,0:T(8,128)} %get-tuple-element.617) | copy-start | bytes 3145732 | tf_op jit(solution)/shard_map/cond
  145.2 2.9 copy-start.51
  148.1 7.1 %copy-start.66 = (f32[256,512]{1,0:T(8,128)}, f32[256,512]{1,0:T(8,128)S(1)}, u32[]{:S(2)}) copy-start(f32[256,512]{1,0:T(8,128)S(1)} %get-tuple-element.1153) | copy-start | bytes 1572868 | tf_op jit(solution)/shard_map/cond
  148.1 7.1 %copy-start.32 = (f32[256,512]{1,0:T(8,128)S(1)}, f32[256,512]{1,0:T(8,128)}, u32[]{:S(2)}) copy-start(f32[256,512]{1,0:T(8,128)} %get-tuple-element.625) | copy-start | bytes 1572868 | tf_op jit(solution)/shard_map/cond
  148.1 7.1 %copy-start.126 = (bf16[512,2048]{1,0:T(8,128)(2,1)S(1)}, bf16[512,2048]{1,0:T(8,128)(2,1)}, u32[]{:S(2)}) copy-start(bf16[512,2048]{1,0:T(8,128)(2,1)} %get-tuple-element.624) | copy-start | bytes 6291460 | tf_op jit(solution)/shard_map/cond
  155.2 1.0 copy-start.96
  155.3 1.4 copy-start.67
  156.2 1.1 copy-start.20
  156.6 1.2 copy-start.64
  169.5 2.9 copy-start.102
  169.9 2.5 copy-start.116
  180.9 3.6 copy-start.76
  180.9 3.6 copy-start.103
  180.9 3.6 copy-start.117
  192.2 5.5 %copy-start.46 = (bf16[256,2048]{1,0:T(8,128)(2,1)S(1)}, bf16[256,2048]{1,0:T(8,128)(2,1)}, u32[]{:S(2)}) copy-start(bf16[256,2048]{1,0:T(8,128)(2,1)} %get-tuple-element.639) | copy-start | bytes 3145732 | tf_op jit(solution)/shard_map/cond
  192.2 5.5 %copy-start.68 = (f32[256,512]{1,0:T(8,128)S(1)}, f32[256,512]{1,0:T(8,128)}, u32[]{:S(2)}) copy-start(f32[256,512]{1,0:T(8,128)} %copy-done.66) | copy-start | bytes 1572868 | tf_op jit(solution)/shard_map/cond
  208.0 5.5 %copy-start.97 = (bf16[256,2048]{1,0:T(8,128)(2,1)S(1)}, bf16[256,2048]{1,0:T(8,128)(2,1)}, u32[]{:S(2)}) copy-start(bf16[256,2048]{1,0:T(8,128)(2,1)} %copy-done.96) | copy-start | bytes 3145732 | tf_op jit(solution)/shard_map/cond
  208.0 5.5 %copy-start.111 = (bf16[256,512]{1,0:T(8,128)(2,1)S(1)}, bf16[256,512]{1,0:T(8,128)(2,1)}, u32[]{:S(2)}) copy-start(bf16[256,512]{1,0:T(8,128)(2,1)} %get-tuple-element.637) | copy-start | bytes 786436 | tf_op jit(solution)/shard_map/cond
  226.0 14.4 %collective-permute-start.3 = (bf16[256,1024]{1,0:T(8,128)(2,1)S(1)}, bf16[256,1024]{1,0:T(8,128)(2,1)S(1)}, u32[]{:S(2)}, u32[]{:S(2)}) collective-permute-start(bf16[256,1024]{1,0:T(8,128)(2,1)S(1)} %copy.176), channel_id=1, source_target_pairs={{16,0},{17,1},{18,2},{19,3},{20,4},{21,5},{22,6},{23,7},{24,8},{25... | collective-permute-start | bytes 1572872 | tf_op jit(solution)/shard_map/ppermute | solution.py:180
  240.4 0.8 copy-start.92
  241.2 2.0 copy-start.91
  243.2 1.6 copy-start.13
  243.2 1.6 copy-start.93
  244.9 1.7 copy-start.28
  245.4 1.6 copy-start.34
  245.4 2.0 copy-start.26
  247.1 1.6 copy-start.52
  248.0 7.6 %copy-start.65 = (f32[256,512]{1,0:T(8,128)}, f32[256,512]{1,0:T(8,128)S(1)}, u32[]{:S(2)}) copy-start(f32[256,512]{1,0:T(8,128)S(1)} %get-tuple-element.1159) | copy-start | bytes 1572868 | tf_op jit(solution)/shard_map/cond
  255.6 1.9 copy-start.121
  260.0 2.1 copy-start.21
  260.4 2.2 copy-start.62
  278.4 3.6 copy-start.74
  289.7 5.4 %copy-start.122 = (bf16[256,2048]{1,0:T(8,128)(2,1)S(1)}, bf16[256,2048]{1,0:T(8,128)(2,1)}, u32[]{:S(2)}) copy-start(bf16[256,2048]{1,0:T(8,128)(2,1)} %copy-done.121) | copy-start | bytes 3145732 | tf_op jit(solution)/shard_map/cond
  299.5 5.4 %copy-start.44 = (bf16[256,2048]{1,0:T(8,128)(2,1)S(1)}, bf16[256,2048]{1,0:T(8,128)(2,1)}, u32[]{:S(2)}) copy-start(bf16[256,2048]{1,0:T(8,128)(2,1)} %get-tuple-element.1065) | copy-start | bytes 3145732 | tf_op jit(solution)/shard_map/cond
  310.6 7.9 %copy-start.69 = (bf16[3072,512]{1,0:T(8,128)(2,1)}, bf16[3072,512]{1,0:T(8,128)(2,1)S(1)}, u32[]{:S(2)}) copy-start(bf16[3072,512]{1,0:T(8,128)(2,1)S(1)} %slice_dynamic-update-slice_fusion) | copy-start | bytes 9437188
  415.4 3.8 copy-start.72

commit v2 on v1

v2 whole, which is shorter than its diff:
```python
import functools
import jax
import jax.numpy as jnp
from jax import lax
from jax.experimental import pallas as pl
from jax.experimental.pallas import tpu as pltpu
from jax.sharding import PartitionSpec as P
MESH = pl.DeviceIdType.MESH

def peers():
    sec = lax.axis_index("section"); dp = lax.axis_index("dp")
    n = lax.axis_size("dp") // 2
    core = lax.rem(dp, 2); chip = dp // 2
    x = lax.rem(chip, 2); z = chip // 2
    pos = jnp.where(x == 0, z, n - 1 - z)
    def at(q):
        q = lax.rem(q + n, n)
        zz = jnp.where(q < n // 2, q, n - 1 - q)
        xx = jnp.where(q < n // 2, 0, 1)
        return (zz * 2 + xx) * 2 + core
    return sec, dp, n, core, pos, at(pos + 1), at(pos - 1), dp + 1 - 2 * core

def barrier(sec, targets):
    bar = pltpu.get_barrier_semaphore()
    for t in targets:
        pl.semaphore_signal(bar, inc=1, device_id=(sec, t), device_id_type=MESH)
    pl.semaphore_wait(bar, len(targets))

def ring_kernel(n, units, g0, g1, ng, o0, o1, o_norm,
                G0, G1, NG, S0, S1, NS, R0, R1, NR, E0, E1, NE,
                ld_sem, sib_s, sib_r, rs_s, rs_r, ag_s, ag_r, sh_s, sh_r, o_sem):
    sec, dp, _, core, pos, nxt, prv, sibling = peers()
    loads = [pltpu.make_async_copy(g0, G0, ld_sem.at[0]), pltpu.make_async_copy(g1, G1, ld_sem.at[1]), pltpu.make_async_copy(ng, NG, ld_sem.at[2])]
    for c in loads: c.start()
    barrier(sec, [nxt, prv, sibling])
    for c in loads: c.wait()
    half = 16 * n
    def rows(d, k, c=core):
        return pl.ds(pl.multiple_of(c * 2 * half + d * half + k * 16, 16), 16)
    def srows(d, k):
        return pl.ds(pl.multiple_of(d * half + k * 16, 16), 16)
    class Stream: pass
    streams = []
    for gi, (G, S, R, E) in enumerate(((G0, S0, R0, E0), (G1, S1, R1, E1))):
        for d in (0, 1):
            st = Stream(); st.i = gi * 2 + d; st.d = d; st.g = gi
            st.own = lambda k, G=G, d=d: G.at[:, rows(d, k), :]
            st.other = lambda k, G=G, d=d: G.at[:, rows(d, k, 1 - core), :]
            st.sib = lambda k, S=S, d=d: S.at[:, srows(d, k), :]
            st.rs = lambda s, R=R, d=d: R.at[d, s]
            st.res = lambda k, E=E, d=d: E.at[:, rows(d, k), :]
            st.res_other = lambda k, E=E, d=d: E.at[:, rows(d, k, 1 - core), :]
            st.to = nxt if d == 0 else prv
            streams.append(st)
    st = Stream(); st.i = 4; st.d = 0; st.g = 2
    st.own = lambda k: NG.at[core, k]; st.other = lambda k: NG.at[1 - core, k]; st.sib = lambda k: NS.at[k]
    st.rs = lambda s: NR.at[s]; st.res = lambda k: NE.at[core, k]; st.res_other = lambda k: NE.at[1 - core, k]; st.to = nxt
    streams.append(st)
    def chunk(st, s):
        return lax.rem(pos - s + 2 * n, n) if st.d == 0 else lax.rem(pos + s, n)
    def remote(src, dst, ss, rs, to):
        return pltpu.make_async_remote_copy(src_ref=src, dst_ref=dst, send_sem=ss, recv_sem=rs, device_id=(sec, to), device_id_type=MESH)
    def sib_copy(st, k): return remote(st.other(k), st.sib(k), sib_s.at[st.i, k], sib_r.at[st.i, k], sibling)
    def rs_copy(st, s): return remote(st.own(chunk(st, s)), st.rs(s), rs_s.at[st.i, s], rs_r.at[st.i, s], st.to)
    def ag_copy(st, t):
        k = chunk(st, t + n - 1)
        return remote(st.res(k), st.res(k), ag_s.at[st.i, t], ag_r.at[st.i, t], st.to)
    def sh_copy(st, t):
        k = chunk(st, t + n - 1)
        return remote(st.res(k), st.res(k), sh_s.at[st.i, t], sh_r.at[st.i, t], sibling)
    def loop(a, b, f):
        lax.fori_loop(a, b, lambda i, c: (f(i), c)[1], 0)
    def f32(r): return r[...].astype(jnp.float32)
    def share(s):
        for st in streams: sib_copy(st, chunk(st, s)).start()
    loop(0, n, share)
    def first():
        for st in streams:
            k = chunk(st, 0)
            sib_copy(st, k).wait_recv()
            own = st.own(k)
            own[...] = (f32(own) + f32(st.sib(k))).astype(own.dtype)
            rs_copy(st, 0).start()
    first()
    def middle(s):
        for st in streams:
            k = chunk(st, s)
            sib_copy(st, k).wait_recv()
            rs_copy(st, s - 1).wait_recv()
            own = st.own(k)
            own[...] = (f32(own) + f32(st.sib(k)) + f32(st.rs(s - 1))).astype(own.dtype)
            rs_copy(st, s).start()
    loop(1, n - 1, middle)
    for st in streams:
        k = chunk(st, n - 1)
        sib_copy(st, k).wait_recv()
        rs_copy(st, n - 2).wait_recv()
        own = st.own(k); res = st.res(k)
        res[...] = (f32(own) + f32(st.sib(k)) + f32(st.rs(n - 2))).astype(own.dtype)
        ag_copy(st, 0).start()
        sh_copy(st, 0).start()
    def out_copy(st, k, c, slot):
        src = st.res(k) if c == 0 else st.res_other(k)
        if st.g == 2:
            return pltpu.make_async_copy(src, o_norm.at[core if c == 0 else 1 - core, k], o_sem.at[st.i, slot])
        row = rows(st.d, k, core if c == 0 else 1 - core)
        return pltpu.make_async_copy(src, (o0, o1)[st.g].at[:, row, :], o_sem.at[st.i, slot])
    def emit(st, t):
        k = chunk(st, t + n - 1)
        sh_copy(st, t).wait_recv()
        out_copy(st, k, 0, 2 * t).start()
        out_copy(st, k, 1, 2 * t + 1).start()
    def gather(t):
        for st in streams:
            ag_copy(st, t).wait_recv()
            @pl.when(t < n - 2)
            def _(): ag_copy(st, t + 1).start()
            sh_copy(st, t + 1).start()
        for st in streams:
            emit(st, t)
    loop(0, n - 1, gather)
    for st in streams:
        emit(st, n - 1)
    def drain(s):
        for st in streams:
            sib_copy(st, s).wait_send(); sh_copy(st, s).wait_send()
            out_copy(st, chunk(st, s + n - 1), 0, 2 * s).wait(); out_copy(st, chunk(st, s + n - 1), 1, 2 * s + 1).wait()
            @pl.when(s < n - 1)
            def _():
                rs_copy(st, s).wait_send(); ag_copy(st, s).wait_send()
    loop(0, n, drain)

def all_reduce(g0, g1, ng, n):
    u0, u1 = g0.shape[0], g1.shape[0]
    bf, f4 = jnp.bfloat16, jnp.float32
    any_ = pl.BlockSpec(memory_space=pl.ANY)
    V = pltpu.VMEM; D = pltpu.SemaphoreType.DMA
    return pl.pallas_call(
        functools.partial(ring_kernel, n, (u0, u1)),
        out_shape=[jax.ShapeDtypeStruct(a.shape, a.dtype) for a in (g0, g1, ng)], in_specs=[any_] * 3, out_specs=[any_] * 3,
        scratch_shapes=[V(g0.shape, bf), V(g1.shape, bf), V(ng.shape, f4),
            V((u0, 32 * n, 512), bf), V((u1, 32 * n, 512), bf), V((n, 8, 128), f4),
            V((2, n - 1, u0, 16, 512), bf), V((2, n - 1, u1, 16, 512), bf), V((n - 1, 8, 128), f4),
            V(g0.shape, bf), V(g1.shape, bf), V(ng.shape, f4),
            D((3,)), D((5, n)), D((5, n)), D((5, n)), D((5, n)), D((5, n)), D((5, n)), D((5, n)), D((5, n)), D((5, 2 * n))],
        compiler_params=pltpu.CompilerParams(collective_id=0, has_side_effects=True, vmem_limit_bytes=60 * 2**20),
        name="ring",
    )(g0, g1, ng)


def transpose(value):
    return value.T


def dot(a, b):
    return jnp.dot(a, b, preferred_element_type=jnp.float32)


def dot_nt(a, b):
    return lax.dot_general(a, b, (((1,), (1,)), ((), ())), preferred_element_type=jnp.float32)


def gelu_parts(u):
    size = jnp.abs(u)
    t = 1.0 / (1.0 + (0.3275911 * 0.5 ** 0.5) * size)
    bell = jnp.exp(-0.5 * u * u)
    poly = t * (0.127414796 + t * (-0.142248368 + t * (0.7107068705 + t * (-0.7265760135 + t * 0.5307027145))))
    tail = poly * bell
    cdf = jnp.where(u >= 0, 1.0 - tail, tail)
    return u * cdf, cdf + u * bell * 0.3989422804014327


def normalize(value):
    center = value - jnp.mean(value, axis=-1, keepdims=True)
    spread = jnp.mean(center * center, axis=-1, keepdims=True)
    scale = lax.rsqrt(spread + 1e-05)
    return center * scale, scale


def norm_back(grad, unit, scale, gain):
    inner = grad * gain
    mean = jnp.mean(inner, axis=-1, keepdims=True)
    along = jnp.mean(inner * unit, axis=-1, keepdims=True)
    return scale * (inner - mean - unit * along)


def loop(start, stop, body):
    lax.fori_loop(start, stop, lambda i, carry: (body(i), carry)[1], 0)


ROWS = 64


def compute_kernel(n, lens, x, ct, wq, wo, w1, w2, wc, gn, bs, g0, g1, ng, out, gin,
                   X, CT, WQ, WO, W1, W2, WC, WC0, GN, BS,
                   H1, QKV, PT, O, RR, ST, HQ, CQ, KV, PT2, O2, N2, A, GP, AFT, D, LOW, LOWC, LOWS, DO, DQKV, DCQ, DKV, DST,
                   TT, G0, G1, NG, PG, PB,
                   ld, wc_s, wc_r, sh_s, sh_r, st_s, st_r, ds_s, ds_r, dk_s, dk_r, o_sem):
    sec, dp = lax.axis_index("section"), lax.axis_index("dp")
    core = lax.rem(dp, 2)
    sibling = dp + 1 - 2 * core
    other = 1 - sec
    enc = sec == 0
    dec = sec == 1
    bf = jnp.bfloat16
    length = X.shape[1]
    width = X.shape[2]
    heads = width // 64
    pairs = heads // 2
    loads = {}
    for i, (name, src, dst) in enumerate((("x", x, X), ("gn", gn, GN), ("bs", bs, BS), ("wq", wq, WQ), ("wo", wo, WO), ("w1", w1, W1), ("w2", w2, W2),
                                          ("ct", ct, CT), ("wc", wc, WC))):
        loads[name] = pltpu.make_async_copy(src, dst, ld.at[i])
        loads[name].start()
    bar = pltpu.get_barrier_semaphore()
    for target in ((other, dp), (sec, sibling)):
        pl.semaphore_signal(bar, inc=1, device_id=target, device_id_type=MESH)
    pl.semaphore_wait(bar, 2)

    def remote(src, dst, ss, rs, to):
        return pltpu.make_async_remote_copy(src_ref=src, dst_ref=dst, send_sem=ss, recv_sem=rs, device_id=to, device_id_type=MESH)

    half = pl.ds(pl.multiple_of(core * (width // 2), 16), width // 2)
    other_half = pl.ds(pl.multiple_of((1 - core) * (width // 2), 16), width // 2)
    wc_copy = remote(wc.at[half], WC0.at[half], wc_s, wc_r, (other, dp))
    wc_share = remote(WC0.at[half], WC0.at[half], sh_s, sh_r, (sec, sibling))

    def mrows(m):
        return pl.ds(pl.multiple_of(m * length, length), length)

    def st_copy(m): return remote(ST.at[mrows(m)], ST.at[mrows(m)], st_s.at[m], st_r.at[m], (other, dp))
    def ds_copy(m): return remote(DST.at[mrows(m)], DST.at[mrows(m)], ds_s.at[m], ds_r.at[m], (other, dp))
    def dk_copy(m): return remote(DKV.at[mrows(m)], DKV.at[mrows(m)], dk_s.at[m], dk_r.at[m], (other, dp))

    @pl.when(enc)
    def _(): wc_copy.start()

    PG[...] = jnp.zeros_like(PG)
    PB[...] = jnp.zeros_like(PB)

    def by_rows(m, body):
        loop(0, length // ROWS, lambda i: body(pl.ds(pl.multiple_of(m * length + i * ROWS, ROWS), ROWS), pl.ds(pl.multiple_of(i * ROWS, ROWS), ROWS)))

    def gain_at(i): return GN[pl.ds(i, 1), :]
    def bias_at(i): return BS[pl.ds(i, 1), :]

    def add_norm_grads(i, grad, unit):
        at = pl.ds(i, 1)
        PG[at, :] = PG[at, :] + jnp.sum(grad * unit, axis=0, keepdims=True)
        PB[at, :] = PB[at, :] + jnp.sum(grad, axis=0, keepdims=True)

    lane_low = lax.broadcasted_iota(jnp.int32, (length, 128), 1) < 64
    lane_row = lax.broadcasted_iota(jnp.int32, (1, 128), 1) < 64
    head_masks = (jnp.where(lane_row, 1.0, 0.0).astype(bf), jnp.where(lane_row, 0.0, 1.0).astype(bf))

    def attention(m, q, q0, k, k0, v, v0, P, out_ref):
        rows = mrows(m)
        usable = lax.broadcasted_iota(jnp.int32, (length, length), 0) < lens[m]
        def pair(j):
            def cols(c0): return pl.ds(pl.multiple_of(c0 + j * 128, 128), 128)
            q2, k2, vt = q[rows, cols(q0)], k[rows, cols(k0)], transpose(v[rows, cols(v0)])
            parts = []
            for e in (0, 1):
                s = dot_nt(k2, q2 * head_masks[e]) * 0.125
                s = jnp.where(usable, s, -1e30)
                w = jnp.exp(s - jnp.max(s, axis=0, keepdims=True))
                p = (w * (1.0 / jnp.sum(w, axis=0, keepdims=True))).astype(bf)
                P[m * heads + 2 * j + e] = p
                parts.append(dot(vt[64 * e:64 * (e + 1)], p))
            out_ref[rows, cols(0)] = transpose(jnp.concatenate(parts, axis=0)).astype(bf)
        loop(0, pairs, pair)

    def attention_back(m, do, q, q0, k, k0, v, v0, P, dq, dq0, dk, dk0, dv, dv0):
        rows = mrows(m)
        def pair(j):
            def cols(c0): return pl.ds(pl.multiple_of(c0 + j * 128, 128), 128)
            q2, k2, v2, do2 = q[rows, cols(q0)], k[rows, cols(k0)], v[rows, cols(v0)], do[rows, cols(0)]
            kt = transpose(k2)
            dvs, dks, dqs = [], [], []
            for e in (0, 1):
                p = P[m * heads + 2 * j + e]
                pf = p.astype(jnp.float32)
                dpr = dot_nt(v2, do2 * head_masks[e])
                t = pf * dpr
                ds = (t - pf * jnp.sum(t, axis=0, keepdims=True)).astype(bf)
                dvs.append(dot(p, do2))
                dks.append(dot(ds, q2))
                dqs.append(dot(kt[64 * e:64 * (e + 1)], ds))
            dv[rows, cols(dv0)] = jnp.where(lane_low, dvs[0], dvs[1]).astype(bf)
            dk[rows, cols(dk0)] = (jnp.where(lane_low, dks[0], dks[1]) * 0.125).astype(bf)
            dq[rows, cols(dq0)] = (transpose(jnp.concatenate(dqs, axis=0)) * 0.125).astype(bf)
        loop(0, pairs, pair)

    def product(src, weight, cols, m, store, tile=256):
        rows = mrows(m)
        def one(j):
            at = pl.ds(pl.multiple_of(j * tile, tile), tile)
            store(rows, at, dot(src[rows, :], weight[:, at]))
        loop(0, cols // tile, one)

    def product_nt(src, s0, sw, weight, w0, m, store, tile=256):
        rows = mrows(m)
        def one(j):
            at = pl.ds(pl.multiple_of(j * tile, tile), tile)
            store(rows, at, dot_nt(src[rows, s0:s0 + sw], weight[at, w0:w0 + sw]))
        loop(0, weight.shape[0] // tile, one)

    def norm_into(source, m, index, target):
        def one(rows, _):
            unit, _ = normalize(source[rows, :])
            target[rows, :] = (unit * gain_at(index) + bias_at(index)).astype(bf)
        by_rows(m, one)

    def self_forward(m):
        def one(rows, local):
            unit, _ = normalize(X[m, local, :].astype(jnp.float32))
            H1[rows, :] = (unit * gain_at(0) + bias_at(0)).astype(bf)
        by_rows(m, one)
        def put(rows, at, value): QKV[rows, at] = value.astype(bf)
        product(H1, WQ, 3 * width, m, put)
        attention(m, QKV, 0, QKV, width, QKV, 2 * width, PT, O)
        def add(rows, at, value): RR[0, rows, at] = value + X[m, :, at].astype(jnp.float32)
        product(O, WO, width, m, add)

    def ffn_forward(m, source, index, last):
        norm_into(source, m, index, N2)
        def act(rows, at, value):
            A[rows, at], GP[rows, at] = (part.astype(bf) for part in gelu_parts(value))
        product(N2, W1, W1.shape[1], m, act)
        product(A, W2, width, m, last)

    for name in ("x", "gn", "bs", "wq", "wo"): loads[name].wait()
    def front(m):
        self_forward(m)
        @pl.when(enc)
        def _():
            @pl.when(m == 0)
            def _():
                loads["w1"].wait()
                loads["w2"].wait()
            def last(rows, at, value): AFT[rows, at] = value + RR[0, rows, at]
            ffn_forward(m, RR.at[0], 1, last)
            norm_into(AFT, m, 2, ST)
            st_copy(m).start()
    loop(0, 2, front)
    for name in ("ct", "wc"): loads[name].wait()
    @pl.when(dec)
    def _():
        loads["w1"].wait()
        loads["w2"].wait()
        wc_copy.wait_recv()
        wc_share.start()
        wc_share.wait_recv()

    def middle(m):
        rows = mrows(m)
        @pl.when(enc)
        def _():
            ds_copy(m).wait_recv()
            def one(r, local):
                unit, scale = normalize(AFT[r, :])
                grad = CT[m, local, :].astype(jnp.float32) + DST[r, :].astype(jnp.float32)
                add_norm_grads(2, grad, unit)
                back = norm_back(grad, unit, scale, gain_at(2))
                D[r, :] = back
                LOW[r, :] = back.astype(bf)
            by_rows(m, one)
        @pl.when(dec)
        def _():
            norm_into(RR.at[0], m, 1, HQ)
            def put_q(rows, at, value): CQ[rows, at] = value.astype(bf)
            product(HQ, WC.at[:, pl.ds(0, width)], width, m, put_q)
            st_copy(m).wait_recv()
            def put_kv(rows, at, value): KV[rows, at] = value.astype(bf)
            product(ST, WC0, 2 * width, m, put_kv)
            attention(m, CQ, 0, KV, 0, KV, width, PT2, O2)
            def add(rows, at, value): RR[1, rows, at] = value + RR[0, rows, at]
            product(O2, WC.at[:, pl.ds(width, width)], width, m, add)
            def last(rows, at, value): AFT[rows, at] = value + RR[1, rows, at]
            ffn_forward(m, RR.at[1], 2, last)
            def one(r, local):
                D[r, :] = CT[m, local, :].astype(jnp.float32)
                LOW[r, :] = CT[m, local, :]
            by_rows(m, one)
        def put_du(rows, at, value): GP[rows, at] = (value * GP[rows, at].astype(jnp.float32)).astype(bf)
        product_nt(LOW, 0, width, W2, 0, m, put_du)
        def put_dn(rows, at, value): AFT[rows, at] = value
        def emit(r, local):
            @pl.when(enc)
            def _(): out_v(m, local, ST[r, :])
            @pl.when(dec)
            def _(): out_v(m, local, AFT[r, :].astype(bf))
        by_rows(m, emit)
        product_nt(GP, 0, W1.shape[1], W1, 0, m, put_dn)
        def one(r, local):
            unit, scale = normalize(RR[sec, r, :])
            grad = AFT[r, :]
            add_norm_grads(1 + sec, grad, unit)
            D[r, :] = D[r, :] + norm_back(grad, unit, scale, gain_at(1 + sec))
        by_rows(m, one)
        @pl.when(dec)
        def _():
            def low(r, local): LOWC[r, :] = D[r, :].astype(bf)
            by_rows(m, low)
            def put_do(rows, at, value): DO[rows, at] = value.astype(bf)
            product_nt(LOWC, 0, width, WC.at[:, pl.ds(width, width)], 0, m, put_do)
            attention_back(m, DO, CQ, 0, KV, 0, KV, width, PT2, DCQ, 0, DKV, 0, DKV, width)
            def put_ds(rows, at, value): DST[rows, at] = value.astype(bf)
            product_nt(DKV, 0, 2 * width, WC0, 0, m, put_ds)
            ds_copy(m).start()
            @pl.when(m == 1)
            def _():
                dk_copy(0).start()
                dk_copy(1).start()
            def put_dh(rows, at, value): AFT[rows, at] = value
            product_nt(DCQ, 0, width, WC.at[:, pl.ds(0, width)], 0, m, put_dh)
            def two(r, local):
                unit, scale = normalize(RR[0, r, :])
                grad = AFT[r, :]
                add_norm_grads(1, grad, unit)
                D[r, :] = D[r, :] + norm_back(grad, unit, scale, gain_at(1))
            by_rows(m, two)

    OUT, GIN = TT[1], TT[2]
    def out_v(m, local, value): OUT[m, local, :] = value
    loop(0, 2, middle)
    outs = [pltpu.make_async_copy(OUT, out, o_sem.at[0])]
    outs[0].start()

    T = TT[0]
    def block(G, b):
        if 64 * n == 512: return G.at[b]
        return G.at[b * 512 // (64 * n), pl.ds(pl.multiple_of(lax.rem(b * 512, 64 * n), 512), 512)]
    def weight_grads(source, grad, c0, count, G, b0):
        T[...] = transpose(source[...])
        def one(i):
            at = pl.ds(pl.multiple_of(c0 + i * 512, 512), 512)
            block(G, b0 + i)[...] = dot(T[...], grad[:, at]).astype(bf)
        loop(0, count, one)

    weight_grads(N2, GP, 0, 4, G0, 0)
    def down(i):
        at = pl.ds(pl.multiple_of(i * 512, 512), 512)
        block(G0, 4 + i)[...] = dot(transpose(A[:, at]), LOW[...]).astype(bf)
    loop(0, 4, down)

    def bottom(m):
        def low(r, local): LOWS[r, :] = D[r, :].astype(bf)
        by_rows(m, low)
        def put_do(rows, at, value): DO[rows, at] = value.astype(bf)
        product_nt(LOWS, 0, width, WO, 0, m, put_do)
        attention_back(m, DO, QKV, 0, QKV, width, QKV, 2 * width, PT, DQKV, 0, DQKV, width, DQKV, 2 * width)
        def put_dh(rows, at, value): AFT[rows, at] = value
        product_nt(DQKV, 0, 3 * width, WQ, 0, m, put_dh)
        def one(r, local):
            unit, scale = normalize(X[m, local, :].astype(jnp.float32))
            grad = AFT[r, :]
            add_norm_grads(0, grad, unit)
            GIN[m, local, :] = (D[r, :] + norm_back(grad, unit, scale, gain_at(0))).astype(bf)
        by_rows(m, one)
    loop(0, 2, bottom)
    outs.append(pltpu.make_async_copy(GIN, gin, o_sem.at[1]))
    outs[1].start()
    weight_grads(H1, DQKV, 0, 3, G1, 0)
    weight_grads(O, LOWS, 0, 1, G1, 3)
    @pl.when(enc)
    def _():
        dk_copy(0).wait_recv()
        dk_copy(1).wait_recv()
        weight_grads(ST, DKV, 0, 2, G1, 4)
    @pl.when(dec)
    def _():
        weight_grads(HQ, DCQ, 0, 1, G1, 4)
        weight_grads(O2, LOWC, 0, 1, G1, 5)
    NG[...] = jnp.zeros_like(NG)
    for j in range(4):
        NG[0, j] = PG[:, 128 * j:128 * (j + 1)]
        NG[1, j] = PB[:, 128 * j:128 * (j + 1)]
    for i, (src, dst) in enumerate(((G0, g0), (G1, g1), (NG, ng))):
        outs.append(pltpu.make_async_copy(src, dst, o_sem.at[2 + i]))
        outs[-1].start()
    for c in outs: c.wait()
    @pl.when(enc)
    def _():
        wc_copy.wait_send()
        st_copy(0).wait_send()
        st_copy(1).wait_send()
    @pl.when(dec)
    def _():
        wc_share.wait_send()
        for m in (0, 1):
            ds_copy(m).wait_send()
            dk_copy(m).wait_send()


def layers(lens, x, ct, wq, wo, w1, w2, wc, gn, bs, n):
    bf, f4 = jnp.bfloat16, jnp.float32
    micro, length, width = x.shape
    rows, hidden = micro * length, w1.shape[1]
    any_ = pl.BlockSpec(memory_space=pl.ANY)
    V, DMA = pltpu.VMEM, pltpu.SemaphoreType.DMA
    def units(count): return (-(-count * 512 // (64 * n)), 64 * n, 512)
    shapes = [units(8), units(6)]
    sq = V((rows, width), bf)
    probs = V((micro * width // 64, length, length), bf)
    scratch = [V(a.shape, a.dtype) for a in (x, ct, wq, wo, w1, w2, wc)] + [V(wc.shape, bf), V(gn.shape, f4), V(bs.shape, f4)]
    scratch += [sq, V((rows, 3 * width), bf), probs, sq, V((2, rows, width), f4), sq, sq, sq, V((rows, 2 * width), bf), probs, sq, sq,
                V((rows, hidden), bf), V((rows, hidden), bf), V((rows, width), f4), V((rows, width), f4),
                sq, sq, sq, sq, V((rows, 3 * width), bf), sq, V((rows, 2 * width), bf), sq]
    scratch += [[V((width, rows), bf), V(x.shape, bf), V(x.shape, bf)], V(shapes[0], bf), V(shapes[1], bf), V((2, n, 8, 128), f4), V((8, width), f4), V((8, width), f4)]
    scratch += [DMA((9,)), DMA, DMA, DMA, DMA] + [DMA((2,))] * 6 + [DMA((5,))]
    return pl.pallas_call(
        functools.partial(compute_kernel, n),
        out_shape=[jax.ShapeDtypeStruct(s, bf) for s in shapes] + [jax.ShapeDtypeStruct((2, n, 8, 128), f4), jax.ShapeDtypeStruct(x.shape, bf), jax.ShapeDtypeStruct(x.shape, bf)],
        in_specs=[pl.BlockSpec(memory_space=pltpu.SMEM)] + [any_] * 9,
        out_specs=[any_] * 5,
        scratch_shapes=scratch,
        compiler_params=pltpu.CompilerParams(collective_id=1, has_side_effects=True, vmem_limit_bytes=62 * 2**20),
        name="layers",
    )(lens, x, ct, wq, wo, w1, w2, wc, gn, bs)


def pack_norm(en):
    return en[:, :4, :3].transpose(0, 2, 1, 3).reshape(2, 3, 512)


def local(layer_input, lengths, attn_qkv, attn_out, ffn_in, ffn_out, cross_weight, norm_gain, norm_bias, cotangent):
    n = lax.axis_size("dp") // 2
    g0, g1, ng, out, gin = layers(lengths[:, 0], layer_input[0, :, 0], cotangent[0, :, 0], attn_qkv[0], attn_out[0], ffn_in[0], ffn_out[0],
                                  cross_weight[0], norm_gain[0], norm_bias[0], n)
    e0, e1, en = all_reduce(g0, g1, ng, n)
    e0 = e0.reshape(-1, 512)[:8 * 512].reshape(8, 512, 512)
    e1 = e1.reshape(-1, 512)[:6 * 512].reshape(6, 512, 512)
    def wide(blocks):
        return blocks.transpose(1, 0, 2).reshape(1, 512, -1).astype(jnp.float32)
    en = pack_norm(en)
    return (out[None, :, None], gin[None, :, None], wide(e1[:3]), e1[3:4].astype(jnp.float32), wide(e0[:4]),
            e0[4:].reshape(1, 2048, 512).astype(jnp.float32), wide(e1[4:]), en[0:1], en[1:2])


def solution(mesh):
    data = P("section", None, "dp", None, None)
    weight = P("section", None, None)
    return jax.shard_map(
        local, mesh=mesh,
        in_specs=(data, P(None, "dp")) + (weight,) * 7 + (data,),
        out_specs=(data, data) + (weight,) * 7,
        check_vma=False,
    )
```

time: 463 us -> 220 us (0.48); the launches traced: 454 us -> 219 us
  local copies, waits for them, and re-layouts: 143 us -> 23.9 us
  Pallas kernels: 82.6 us -> 179 us
  matrix products: 89 us -> 0 us
  starting transfers between devices: 39.7 us -> 0 us
  waiting for transfers between devices: 37.1 us -> 0 us
  other arithmetic: 45 us -> 16 us
  loops' own time: 16.3 us -> 0 us
    pallas_call x0 -> x1, Pallas kernels: none -> 95.1 us  [layers(): pl.pallas_call(functools.partial(compute_kernel, n), out_shape=[jax.Shape...]
    dot_general x44 -> x0, matrix products: 89 us -> none  [the longest x10 31.5 us: product_tn(): lax.dot_general(left_side, right_side, (((0,), (0,)), ((), ())), preferre...]
    another operation x23 -> x0, local copies, waits for them, and re-layouts: 63 us -> none
    ppermute x4 -> x0, starting transfers between devices: 39.7 us -> none  [shifted(): lax.ppermute(value, axis, [(source, source + steps) for source in range(l...]
    ppermute x4 -> x0, waiting for transfers between devices: 37.1 us -> none  [shifted(): lax.ppermute(value, axis, [(source, source + steps) for source in range(l...]
    another operation x4 -> x0, loops' own time: 16.3 us -> none  [the longest x3 15.6 us: local(): lax.cond(is_encoder, encoder_tick, decoder_tick, operands)]
    reduce_sum x28 -> x0, other arithmetic: 13.8 us -> none  [the longest x14 5.74 us: layer_norm(): center = source - jnp.mean(source, axis=-1, keepdims=True)]
    cond x114 -> x0, local copies, waits for them, and re-layouts: 13.7 us -> none  [the longest x4 5.26 us: local(): lax.cond(is_encoder, encoder_tick, decoder_tick, operands)]
  transfers between devices with their start and end apart: 4 -> 0, of which waited for: 4 -> 0; matrix products, arithmetic and copies ran while one was open for 1% -> 0% of each run, Pallas kernels for 0% -> 0%
where the time goes in v2:
time: 220 us; the launch traced here: 219 us
  Pallas kernels  179 us (81%)
  local copies, waits for them, and re-layouts  23.9 us (11%)
  other arithmetic  16 us (7%)
    pallas_call x1, Pallas kernels, layers(): pl.pallas_call(functools.partial(compute_kernel, n), out_shape=[jax.Shape...  95.1 us
    pallas_call x1, Pallas kernels, all_reduce(): pl.pallas_call(functools.partial(ring_kernel, n, (u0, u1)), out_shape=[ja...  83.4 us
    unnamed x10, local copies, waits for them, and re-layouts  12.4 us
    convert_element_type x3, local copies, waits for them, and re-layouts, wide(): return blocks.transpose(1, 0, 2).reshape(1, 512, -1).astype(jnp.float32)  9.53 us
    convert_element_type x2, other arithmetic, wide(): return blocks.transpose(1, 0, 2).reshape(1, 512, -1).astype(jnp.float32)  6.35 us
    slice x1, other arithmetic, local(): e0[4:].reshape(1, 2048, 512).astype(jnp.float32)  4.93 us

profile of v2, /device:TPU:0, one launch (start us, length us, event | category | flops | bytes accessed | tf_op | source)
XLA Modules:
  0.0 219.2 jit_solution(2102845077221889454)
XLA Ops:
  0.6 1.3 copy_bitcast_fusion
  2.0 95.1 %layers.1 = (bf16[8,512,512]{2,1,0:T(8,128)(2,1)}, bf16[6,512,512]{2,1,0:T(8,128)(2,1)}, f32[2,8,8,128]{3,2,1,0:T(8,128)}, bf16[2,256,512]{2,1,0:T(8,128)(2,1)}, bf16[2,256,512]{2,1,0:T(8,128)(2,1)}) custom-call(s32[2]{0:T(128)} %bitcast.50, bf16[2,256,512]{2,1,0:T(8,128)(2,1)} %bitcast.43, bf16[2,256,512]{2,1,0:T(8,128)(2,1)} %bitcast.44, ...), custom_call_target="tpu_custom_call" | custom-call | tf_op jit(solution)/shard_map/layers/pallas_call | solution.py:512
  97.1 83.4 %ring.1 = (bf16[8,512,512]{2,1,0:T(8,128)(2,1)}, bf16[6,512,512]{2,1,0:T(8,128)(2,1)}, f32[2,8,8,128]{3,2,1,0:T(8,128)}) custom-call(bf16[8,512,512]{2,1,0:T(8,128)(2,1)} %get-tuple-element.19.g0, bf16[6,512,512]{2,1,0:T(8,128)(2,1)} %get-tuple-element.20.g1, f32[2,8,8,128]{3,2,1,0:T(8,128)} %get-tuple-element.21.ng), custom_call_target="tpu_custom_call" | custom-call | tf_op jit(solution)/shard_map/ring/pallas_call | solution.py:138
  180.5 3.5 %convert_bitcast_fusion.1 = f32[512,3,512]{2,0,1:T(8,128)} fusion(bf16[6,512,512]{2,1,0:T(8,128)(2,1)} %get-tuple-element.22), kind=kLoop, calls=%fused_computation.1 | loop fusion | flops 786432 | bytes 4718592 | tf_op jit(solution)/shard_map/convert_element_type | solution.py:535
  184.0 2.4 %copy.21 = f32[512,3,512]{0,2,1:T(8,128)S(1)} copy(f32[512,3,512]{2,0,1:T(8,128)} %convert_bitcast_fusion.1) | data formatting | bytes 6291456 | tf_op jit(solution)/shard_map/convert_element_type | solution.py:535
  186.4 2.4 %copy.28 = f32[1,512,1536]{2,1,0:T(8,128)} copy(f32[1,512,1536]{1,2,0:T(8,128)S(1)} %bitcast.36) | data formatting | bytes 6291456
  188.8 2.8 %convert_bitcast_fusion.2 = f32[512,2,512]{2,0,1:T(8,128)} fusion(bf16[6,512,512]{2,1,0:T(8,128)(2,1)} %get-tuple-element.22), kind=kLoop, calls=%fused_computation.3 | loop fusion | flops 524288 | bytes 3145728 | tf_op jit(solution)/shard_map/convert_element_type | solution.py:535
  191.6 1.9 copy.23
  193.5 1.8 copy.30
  195.3 2.1 slice_convert_fusion
  197.5 4.9 %fusion = (bf16[4,512,512]{2,1,0:T(8,128)(2,1)S(1)}, f32[512,4,512]{2,0,1:T(8,128)}) fusion(bf16[8,512,512]{2,1,0:T(8,128)(2,1)} %get-tuple-element.23), kind=kLoop, calls=%fused_computation.8 | loop fusion | flops 1048576 | bytes 10485760 | tf_op jit(solution)/shard_map/slice | solution.py:538
  202.4 5.2 %copy.22 = f32[512,4,512]{0,2,1:T(8,128)} copy(f32[512,4,512]{2,0,1:T(8,128)} %get-tuple-element.44) | data formatting | bytes 8388608 | tf_op jit(solution)/shard_map/convert_element_type | solution.py:535
  207.6 5.3 %copy.29 = f32[1,512,2048]{2,1,0:T(8,128)} copy(f32[1,512,2048]{1,2,0:T(8,128)} %bitcast.35) | data formatting | bytes 8388608
  213.0 0.0 copy-start.1
  213.0 0.0 copy-start
  213.0 2.6 %bitcast_convert_fusion = f32[1,2048,512]{2,1,0:T(8,128)} fusion(bf16[1,2048,512]{2,1,0:T(8,128)(2,1)S(1)} %bitcast.37), kind=kLoop, calls=%fused_computation.2 | loop fusion | flops 1048576 | bytes 6291456 | tf_op jit(solution)/shard_map/convert_element_type | solution.py:538
  215.6 0.8 slice_bitcast_fusion
  216.4 0.6 copy.24
  217.0 0.6 copy.25
  217.6 0.0 copy-done.1
  217.6 0.8 copy.37
  218.4 0.0 copy-done
  218.4 0.8 copy.38
  (1 shorter events, 0.0 us)
Async XLA Ops:
  213.0 4.6 %copy-start.1 = (bf16[2,256,512]{2,1,0:T(8,128)(2,1)S(1)}, bf16[2,256,512]{2,1,0:T(8,128)(2,1)}, u32[]{:S(2)}) copy-start(bf16[2,256,512]{2,1,0:T(8,128)(2,1)} %get-tuple-element.17) | copy-start | bytes 1572868
  213.0 5.4 %copy-start = (bf16[2,256,512]{2,1,0:T(8,128)(2,1)S(1)}, bf16[2,256,512]{2,1,0:T(8,128)(2,1)}, u32[]{:S(2)}) copy-start(bf16[2,256,512]{2,1,0:T(8,128)(2,1)} %get-tuple-element.18) | copy-start | bytes 1572868

commit v3 on v2

v3 whole, which is shorter than its diff:
```python
import functools

import jax
import jax.numpy as jnp
from jax import lax
from jax.experimental import pallas as pl
from jax.experimental.pallas import tpu as pltpu
from jax.sharding import PartitionSpec as P

MESH = pl.DeviceIdType.MESH
BF = jnp.bfloat16
F4 = jnp.float32
SIDE = 512
TILE = 256


def dot(a, b):
    return jnp.dot(a, b, preferred_element_type=F4)


def dot_nt(a, b):
    return lax.dot_general(a, b, (((1,), (1,)), ((), ())), preferred_element_type=F4)


def gelu_parts(u):
    size = jnp.abs(u)
    t = 1.0 / (1.0 + (0.3275911 * 0.5 ** 0.5) * size)
    bell = jnp.exp(-0.5 * u * u)
    poly = t * (0.127414796 + t * (-0.142248368 + t * (0.7107068705 + t * (-0.7265760135 + t * 0.5307027145))))
    tail = poly * bell
    cdf = jnp.where(u >= 0, 1.0 - tail, tail)
    return u * cdf, cdf + u * bell * 0.3989422804014327


def normalize(value):
    center = value - jnp.mean(value, axis=-1, keepdims=True)
    spread = jnp.mean(center * center, axis=-1, keepdims=True)
    scale = lax.rsqrt(spread + 1e-05)
    return center * scale, scale


def norm_back(grad, unit, scale, gain):
    inner = grad * gain
    mean = jnp.mean(inner, axis=-1, keepdims=True)
    along = jnp.mean(inner * unit, axis=-1, keepdims=True)
    return scale * (inner - mean - unit * along)


def loop(start, stop, body, unroll=1):
    lax.fori_loop(start, stop, lambda i, carry: (body(i), carry)[1], 0, unroll=unroll)


def ds(start, size):
    return pl.ds(pl.multiple_of(start, size), size)


def block(ref, b):
    rows = ref.shape[1]
    return ref.at[b * SIDE // rows, pl.ds(b * SIDE % rows, SIDE)]


def remote(src, dst, ss, rs, to):
    return pltpu.make_async_remote_copy(src_ref=src, dst_ref=dst, send_sem=ss, recv_sem=rs, device_id=to, device_id_type=MESH)


class Stream:
    pass


def layers_kernel(n, lens, x, ct, wq, wo, w1, w2, wc, gn, bs,
                  WF, WR, EN, OUT, GIN,
                  X, CT, WC0, GN, BS, H1, QKV, PT, O, RR, ST, HQ, CQ, KV, PT2, O2, N2, A, GP, AFT, D, LOW, LOWC, DO, DQKV, DCQ, DKV, DST, T,
                  G0, G1, NG, S0, S1, NS, R0, R1, NR, PG, PB,
                  ld, wc_s, wc_r, wh_s, wh_r, st_s, st_r, ds_s, ds_r, dk_s, dk_r,
                  sib_s, sib_r, rs_s, rs_r, ag_s, ag_r, sh_s, sh_r):
    sec, dp = lax.axis_index("section"), lax.axis_index("dp")
    core, chip = lax.rem(dp, 2), dp // 2
    side, line = lax.rem(chip, 2), chip // 2
    pos = jnp.where(side == 0, line, n - 1 - line)

    def ring_at(q):
        q = lax.rem(q + n, n)
        return (jnp.where(q < n // 2, q, n - 1 - q) * 2 + jnp.where(q < n // 2, 0, 1)) * 2 + core

    sibling = dp + 1 - 2 * core
    partner, beside, after, before = (1 - sec, dp), (sec, sibling), (sec, ring_at(pos + 1)), (sec, ring_at(pos - 1))
    enc, dec = sec == 0, sec == 1
    length, width = X.shape[1], X.shape[2]
    hidden = A.shape[1]
    heads = width // 64
    pairs = heads // 2

    loads = {}

    def load(name, src, dst):
        loads.setdefault(name, []).append(pltpu.make_async_copy(src, dst, ld.at[sum(map(len, loads.values()))]))
        loads[name][-1].start()

    def columns(b): return pl.ds(b * SIDE, SIDE)
    load("first", x, X)
    load("first", gn, GN)
    load("first", bs, BS)
    for b in range(3): load("first", wq.at[:, columns(b)], block(WR, b))
    load("first", wo, block(WR, 3))
    for b in range(4): load("ffn", w1.at[:, columns(b)], block(WF, b))
    for b in range(4): load("ffn", w2.at[columns(b), :], block(WF, 4 + b))
    for b in range(2): load("cross", wc.at[:, columns(b)], block(WR, 4 + b))
    load("cross", ct, CT)

    def arrived(name):
        for copy in loads[name]: copy.wait()

    bar = pltpu.get_barrier_semaphore()
    for target in (partner, beside, after, before):
        pl.semaphore_signal(bar, inc=1, device_id=target, device_id_type=MESH)
    pl.semaphore_wait(bar, 4)

    half = ds(core * (width // 2), width // 2)
    wc_copy = remote(wc.at[half], WC0.at[half], wc_s, wc_r, partner)
    wc_share = remote(WC0.at[half], WC0.at[half], wh_s, wh_r, beside)

    def mrows(m): return ds(m * length, length)
    def st_copy(m): return remote(ST.at[mrows(m)], ST.at[mrows(m)], st_s.at[m], st_r.at[m], partner)
    ds_copy = remote(DST.at[mrows(1)], DST.at[mrows(1)], ds_s, ds_r, partner)
    def dk_copy(m): return remote(DKV.at[mrows(m)], DKV.at[mrows(m)], dk_s.at[m], dk_r.at[m], partner)

    @pl.when(enc)
    def _(): wc_copy.start()

    PG[...] = jnp.zeros_like(PG)
    PB[...] = jnp.zeros_like(PB)

    def gain_at(i): return GN[i]
    def bias_at(i): return BS[i]

    def add_norm_grads(i, grad, unit):
        at = pl.ds(i, 1)
        PG[at, :] = PG[at, :] + jnp.sum(grad * unit, axis=0, keepdims=True)
        PB[at, :] = PB[at, :] + jnp.sum(grad, axis=0, keepdims=True)

    lane_low = lax.broadcasted_iota(jnp.int32, (length, 128), 1) < 64
    lane_row = lax.broadcasted_iota(jnp.int32, (1, 128), 1) < 64
    head_masks = (jnp.where(lane_row, 1.0, 0.0).astype(BF), jnp.where(lane_row, 0.0, 1.0).astype(BF))
    query_masks = (jnp.where(lane_row, 0.125, 0.0).astype(BF), jnp.where(lane_row, 0.0, 0.125).astype(BF))

    def attention(m, q, q0, k, k0, v, v0, P, out_ref):
        rows = mrows(m)
        usable = lax.broadcasted_iota(jnp.int32, (length, length), 0) < lens[0, m]
        def pair(j):
            def cols(c0): return ds(c0 + j * 128, 128)
            q2, k2, vt = q[rows, cols(q0)], k[rows, cols(k0)], v[rows, cols(v0)].T
            parts = []
            for e in (0, 1):
                s = jnp.where(usable, dot_nt(k2, q2 * query_masks[e]), -1e30)
                w = jnp.exp(s - jnp.max(s, axis=0, keepdims=True))
                p = (w * (1.0 / jnp.sum(w, axis=0, keepdims=True))).astype(BF)
                P[m * heads + 2 * j + e] = p
                parts.append(dot(vt[64 * e:64 * (e + 1)], p))
            out_ref[rows, cols(0)] = jnp.concatenate(parts, axis=0).T.astype(BF)
        loop(0, pairs, pair, unroll=4)

    def attention_back(m, do, q, q0, k, k0, v, v0, P, dq, dq0, dk, dk0, dv, dv0):
        rows = mrows(m)
        def pair(j):
            def cols(c0): return ds(c0 + j * 128, 128)
            q2, k2, v2, do2 = q[rows, cols(q0)], k[rows, cols(k0)], v[rows, cols(v0)], do[rows, cols(0)]
            kt = k2.T
            dvs, dks, dqs = [], [], []
            for e in (0, 1):
                p = P[m * heads + 2 * j + e]
                pf = p.astype(F4)
                t = pf * dot_nt(v2, do2 * head_masks[e])
                dsc = (t - pf * jnp.sum(t, axis=0, keepdims=True)).astype(BF)
                dvs.append(dot(p, do2))
                dks.append(dot(dsc, q2))
                dqs.append(dot(kt[64 * e:64 * (e + 1)], dsc))
            dv[rows, cols(dv0)] = jnp.where(lane_low, dvs[0], dvs[1]).astype(BF)
            dk[rows, cols(dk0)] = (jnp.where(lane_low, dks[0], dks[1]) * 0.125).astype(BF)
            dq[rows, cols(dq0)] = (jnp.concatenate(dqs, axis=0).T * 0.125).astype(BF)
        loop(0, pairs, pair, unroll=4)

    def tiles(count): return [(t, pl.ds(t * TILE, TILE)) for t in range(count // TILE)]
    def tile_of(ref, b0, t): return block(ref, b0 + t * TILE // SIDE)[:, pl.ds(t * TILE % SIDE, TILE)]
    def rows_of(ref, b0, t): return block(ref, b0 + t * TILE // SIDE)[pl.ds(t * TILE % SIDE, TILE), :]

    def norm_into(source, m, index, target):
        rows = mrows(m)
        unit, _ = normalize(source[rows, :])
        target[rows, :] = (unit * gain_at(index) + bias_at(index)).astype(BF)

    def self_forward(m):
        rows = mrows(m)
        unit, _ = normalize(X[m].astype(F4))
        H1[rows, :] = (unit * gain_at(0) + bias_at(0)).astype(BF)
        for t, at in tiles(3 * width): QKV[rows, at] = dot(H1[rows, :], tile_of(WR, 0, t)).astype(BF)
        attention(m, QKV, 0, QKV, width, QKV, 2 * width, PT, O)
        for t, at in tiles(width): RR[0, rows, at] = dot(O[rows, :], tile_of(WR, 3, t)) + X[m, :, at].astype(F4)

    def ffn_forward(m, source, index):
        rows = mrows(m)
        norm_into(source, m, index, N2)
        for t, at in tiles(hidden):
            A[rows, at], GP[rows, at] = (part.astype(BF) for part in gelu_parts(dot(N2[rows, :], tile_of(WF, 0, t))))
        for t, at in tiles(width):
            total = source[rows, at]
            for b in range(hidden // SIDE): total = total + dot(A[rows, columns(b)], tile_of(WF, 4 + b, t))
            AFT[rows, at] = total

    arrived("first")

    def front(m):
        self_forward(m)
        @pl.when(enc)
        def _():
            @pl.when(m == 0)
            def _(): arrived("ffn")
            ffn_forward(m, RR.at[0], 1)
            norm_into(AFT, m, 2, ST)
            st_copy(m).start()
            OUT[m] = ST[mrows(m), :]
    loop(0, 2, front)
    arrived("cross")

    @pl.when(dec)
    def _():
        arrived("ffn")
        wc_copy.wait_recv()
        wc_share.start()
        wc_share.wait_recv()

    def middle(m):
        rows = mrows(m)
        @pl.when(enc)
        def _():
            @pl.when(m == 0)
            def _():
                dk_copy(0).wait_recv()
                for t, at in tiles(width):
                    total = dot_nt(DKV[rows, columns(0)], rows_of(WR, 4, t)) + dot_nt(DKV[rows, columns(1)], rows_of(WR, 5, t))
                    DST[rows, at] = total.astype(BF)
            @pl.when(m == 1)
            def _(): ds_copy.wait_recv()
            unit, scale = normalize(AFT[rows, :])
            grad = CT[m].astype(F4) + DST[rows, :].astype(F4)
            add_norm_grads(2, grad, unit)
            back = norm_back(grad, unit, scale, gain_at(2))
            D[rows, :] = back
            LOW[rows, :] = back.astype(BF)
        @pl.when(dec)
        def _():
            norm_into(RR.at[0], m, 1, HQ)
            for t, at in tiles(width): CQ[rows, at] = dot(HQ[rows, :], tile_of(WR, 4, t)).astype(BF)
            st_copy(m).wait_recv()
            for t, at in tiles(2 * width): KV[rows, at] = dot(ST[rows, :], WC0[:, at]).astype(BF)
            attention(m, CQ, 0, KV, 0, KV, width, PT2, O2)
            for t, at in tiles(width): RR[1, rows, at] = dot(O2[rows, :], tile_of(WR, 5, t)) + RR[0, rows, at]
            ffn_forward(m, RR.at[1], 2)
            OUT[m] = AFT[rows, :].astype(BF)
            D[rows, :] = CT[m].astype(F4)
            LOW[rows, :] = CT[m]
        for t, at in tiles(hidden): GP[rows, at] = (dot_nt(LOW[rows, :], rows_of(WF, 4, t)) * GP[rows, at].astype(F4)).astype(BF)
        for t, at in tiles(width):
            total = dot_nt(GP[rows, columns(0)], rows_of(WF, 0, t))
            for b in range(1, hidden // SIDE): total = total + dot_nt(GP[rows, columns(b)], rows_of(WF, b, t))
            AFT[rows, at] = total
        unit, scale = normalize(RR[sec, rows, :])
        grad = AFT[rows, :]
        add_norm_grads(1 + sec, grad, unit)
        D[rows, :] = D[rows, :] + norm_back(grad, unit, scale, gain_at(1 + sec))
        @pl.when(dec)
        def _():
            LOWC[rows, :] = D[rows, :].astype(BF)
            for t, at in tiles(width): DO[rows, at] = dot_nt(LOWC[rows, :], rows_of(WR, 5, t)).astype(BF)
            attention_back(m, DO, CQ, 0, KV, 0, KV, width, PT2, DCQ, 0, DKV, 0, DKV, width)
            @pl.when(m == 1)
            def _():
                for t, at in tiles(width): DST[rows, at] = dot_nt(DKV[rows, :], WC0[at, :]).astype(BF)
                ds_copy.start()
            dk_copy(m).start()
            for t, at in tiles(width): AFT[rows, at] = dot_nt(DCQ[rows, :], rows_of(WR, 4, t))
            unit, scale = normalize(RR[0, rows, :])
            grad = AFT[rows, :]
            add_norm_grads(1, grad, unit)
            D[rows, :] = D[rows, :] + norm_back(grad, unit, scale, gain_at(1))
    loop(0, 2, middle)

    part = 16 * n
    other_rows = ds((1 - core) * 2 * part, 2 * part)
    def rows_at(d, k, c): return ds((c * 2 + d) * part + k * 16, 16)
    streams = []
    for g, (G, S, R, E) in enumerate(((G0, S0, R0, WF), (G1, S1, R1, WR))):
        for d in (0, 1):
            st = Stream()
            st.i, st.d, st.g, st.to = len(streams), d, g, after if d == 0 else before
            st.own = lambda k, G=G, d=d: G.at[:, rows_at(d, k, core), :]
            st.sib = lambda k, S=S, d=d: S.at[:, rows_at(d, k, 0), :]
            st.slot = lambda s, R=R, d=d: R.at[d, s]
            st.res = lambda k, E=E, d=d: E.at[:, rows_at(d, k, core), :]
            streams.append(st)
    st = Stream()
    st.i, st.d, st.g, st.to = 4, 0, 1, after
    st.own, st.sib, st.slot, st.res = (lambda k: NG.at[core, k]), (lambda k: NS.at[k]), (lambda s: NR.at[s]), (lambda k: EN.at[core, k])
    streams.append(st)
    group = [[st for st in streams if st.g == g] for g in (0, 1)]

    def chunk(st, s): return lax.rem(pos - s + 2 * n, n) if st.d == 0 else lax.rem(pos + s, n)
    def rs_copy(st, s): return remote(st.own(chunk(st, s)), st.slot(s), rs_s.at[st.i, s], rs_r.at[st.i, s], st.to)
    def ag_copy(st, t):
        res = st.res(chunk(st, t + n - 1))
        return remote(res, res, ag_s.at[st.i, t], ag_r.at[st.i, t], st.to)
    def sh_copy(st, t):
        res = st.res(chunk(st, t + n - 1))
        return remote(res, res, sh_s.at[st.i, t], sh_r.at[st.i, t], beside)
    sib_copies = [[remote(G.at[u, other_rows], S.at[u], sib_s.at[g, u], sib_r.at[g, u], beside) for u in range(G.shape[0])]
                  for g, (G, S) in enumerate(((G0, S0), (G1, S1)))]
    sib_copies[1].append(remote(NG.at[1 - core], NS, sib_s.at[1, G1.shape[0]], sib_r.at[1, G1.shape[0]], beside))

    def reduce_step(g, s, first=False, last=False):
        for st in group[g]:
            own = st.own(chunk(st, s))
            total = own[...].astype(F4) + st.sib(chunk(st, s))[...].astype(F4)
            if not first:
                rs_copy(st, s - 1).wait_recv()
                total = total + st.slot(s - 1)[...].astype(F4)
            if last:
                st.res(chunk(st, s))[...] = total.astype(own.dtype)
                ag_copy(st, 0).start()
                sh_copy(st, 0).start()
            else:
                own[...] = total.astype(own.dtype)
                rs_copy(st, s).start()

    def gather_step(g, t):
        for st in group[g]:
            ag_copy(st, t).wait_recv()
            @pl.when(t < n - 2)
            def _(): ag_copy(st, t + 1).start()
            sh_copy(st, t + 1).start()

    def begin(g):
        for copy in sib_copies[g]: copy.wait_recv()
        reduce_step(g, 0, first=True)

    def done_blocks(g, G, count):
        per = G.shape[1] // SIDE
        for u in range(G.shape[0]):
            if count == min((u + 1) * per, (8, 6)[g]): sib_copies[g][u].start()

    def weight_grads(g, G, source, grad, count, b0):
        T[...] = source[...].T
        for b in range(count):
            block(G, b0 + b)[...] = dot(T[...], grad[:, columns(b)]).astype(BF)
            done_blocks(g, G, b0 + b + 1)

    weight_grads(0, G0, N2, GP, 4, 0)
    for b in range(4):
        block(G0, 4 + b)[...] = dot(A[:, columns(b)].T, LOW[...]).astype(BF)
        done_blocks(0, G0, 4 + b + 1)
    begin(0)

    def bottom(m):
        rows = mrows(m)
        LOW[rows, :] = D[rows, :].astype(BF)
        for t, at in tiles(width): DO[rows, at] = dot_nt(LOW[rows, :], rows_of(WR, 3, t)).astype(BF)
        attention_back(m, DO, QKV, 0, QKV, width, QKV, 2 * width, PT, DQKV, 0, DQKV, width, DQKV, 2 * width)
        for t, at in tiles(width):
            total = dot_nt(DQKV[rows, columns(0)], rows_of(WR, 0, t))
            for b in (1, 2): total = total + dot_nt(DQKV[rows, columns(b)], rows_of(WR, b, t))
            AFT[rows, at] = total
        unit, scale = normalize(X[m].astype(F4))
        grad = AFT[rows, :]
        add_norm_grads(0, grad, unit)
        GIN[m] = (D[rows, :] + norm_back(grad, unit, scale, gain_at(0))).astype(BF)
        reduce_step(0, m + 1)
    loop(0, 2, bottom)
    NG[...] = jnp.zeros_like(NG)
    for j in range(4):
        NG[0, j] = PG[:, 128 * j:128 * (j + 1)]
        NG[1, j] = PB[:, 128 * j:128 * (j + 1)]
    sib_copies[1][-1].start()
    weight_grads(1, G1, H1, DQKV, 3, 0)
    weight_grads(1, G1, O, LOW, 1, 3)
    @pl.when(enc)
    def _():
        dk_copy(1).wait_recv()
        T[...] = ST[...].T
        for b in range(2): block(G1, 4 + b)[...] = dot(T[...], DKV[:, columns(b)]).astype(BF)
    @pl.when(dec)
    def _():
        for b, (source, grad) in enumerate(((HQ, DCQ), (O2, LOWC))):
            T[...] = source[...].T
            block(G1, 4 + b)[...] = dot(T[...], grad[...]).astype(BF)
    for b in range(2): done_blocks(1, G1, 5 + b)
    reduce_step(0, 3)
    ahead = 4
    begin(1)
    if n - 1 > ahead:
        reduce_step(0, ahead)
        def both(i):
            reduce_step(1, i)
            reduce_step(0, i + ahead)
        loop(1, n - 1 - ahead, both)
        reduce_step(1, n - 1 - ahead)
    reduce_step(0, n - 1, last=True)
    def cross_over(i):
        reduce_step(1, n - ahead + i)
        gather_step(0, i)
    loop(0, ahead - 1, cross_over)
    reduce_step(1, n - 1, last=True)
    gather_step(0, ahead - 1)
    def both_out(i):
        gather_step(0, ahead + i)
        gather_step(1, i)
    loop(0, n - 1 - ahead, both_out)
    loop(n - 1 - ahead, n - 1, lambda t: gather_step(1, t))

    def drain(s):
        for st in streams:
            sh_copy(st, s).wait()
            @pl.when(s < n - 1)
            def _():
                rs_copy(st, s).wait_send()
                ag_copy(st, s).wait_send()
    loop(0, n, drain)
    for copy in sib_copies[0] + sib_copies[1]: copy.wait_send()

    @pl.when(enc)
    def _():
        wc_copy.wait_send()
        for m in (0, 1): st_copy(m).wait_send()
    @pl.when(dec)
    def _():
        wc_share.wait_send()
        ds_copy.wait_send()
        for m in (0, 1): dk_copy(m).wait_send()


def finish_kernel(e0, e1, en, out, gin, o_out, o_gin, o_qkv, o_wo, o_up, o_down, o_cross, o_gain, o_bias, F, sem, sem2):
    copies = [pltpu.make_async_copy(out, o_out, sem2.at[0]), pltpu.make_async_copy(gin, o_gin, sem2.at[1])]
    for copy in copies: copy.start()
    for j in range(4):
        at = pl.ds(128 * j, 128)
        for i in range(3):
            o_gain[i, :, at] = en[0, j, i:i + 1, :]
            o_bias[i, :, at] = en[1, j, i:i + 1, :]
    def columns(b): return pl.ds(b * SIDE, SIDE)
    targets = [(e0, b, o_up.at[0, :, columns(b)]) for b in range(4)] + [(e0, 4 + b, o_down.at[0, columns(b), :]) for b in range(4)]
    targets += [(e1, b, o_qkv.at[0, :, columns(b)]) for b in range(3)] + [(e1, 3, o_wo.at[0])]
    targets += [(e1, 4 + b, o_cross.at[0, :, columns(b)]) for b in range(2)]
    slots = F.shape[0]
    flight = []
    for i, (e, b, target) in enumerate(targets):
        if i >= slots: flight[i - slots].wait()
        F[i % slots] = block(e, b)[...].astype(F4)
        flight.append(pltpu.make_async_copy(F.at[i % slots], target, sem.at[i % slots]))
        flight[-1].start()
    for copy in flight[-slots:] + copies: copy.wait()


def layers(lens, x, ct, wq, wo, w1, w2, wc, gn, bs, n):
    micro, length, width = x.shape
    rows, hidden = micro * length, w1.shape[1]
    any_ = pl.BlockSpec(memory_space=pl.ANY)
    vmem = pl.BlockSpec(memory_space=pltpu.VMEM)
    V, DMA = pltpu.VMEM, pltpu.SemaphoreType.DMA
    def units(count): return (-(-count * SIDE // (64 * n)), 64 * n, SIDE)
    s0, s1 = units(8), units(6)
    norm = (2, n, 8, 128)
    def own(s): return (s[0], s[1] // 2, SIDE)
    def slots(s): return (2, n - 1, s[0], 16, SIDE)
    sq = V((rows, width), BF)
    probs = V((micro * width // 64, length, length), BF)
    scratch = [V(x.shape, BF), V(x.shape, BF), V(wc.shape, BF), V(gn.shape, F4), V(bs.shape, F4)]
    scratch += [sq, V((rows, 3 * width), BF), probs, sq, V((2, rows, width), F4), sq, sq, sq, V((rows, 2 * width), BF), probs, sq, sq,
                V((rows, hidden), BF), V((rows, hidden), BF), V((rows, width), F4), V((rows, width), F4),
                sq, sq, sq, V((rows, 3 * width), BF), sq, V((rows, 2 * width), BF), sq, V((width, rows), BF)]
    scratch += [V(s0, BF), V(s1, BF), V(norm, F4), V(own(s0), BF), V(own(s1), BF), V(norm[1:], F4), V(slots(s0), BF), V(slots(s1), BF), V((n - 1, 8, 128), F4),
                V((8, width), F4), V((8, width), F4)]
    scratch += [DMA((18,)), DMA, DMA, DMA, DMA, DMA((2,)), DMA((2,)), DMA, DMA, DMA((2,)), DMA((2,)), DMA((2, 9)), DMA((2, 9))] + [DMA((5, n))] * 6
    results = [V(s0, BF), V(s1, BF), V(norm, F4), V(x.shape, BF), V(x.shape, BF)]
    e0, e1, en, out, gin = pl.pallas_call(
        functools.partial(layers_kernel, n), out_shape=results,
        in_specs=[pl.BlockSpec(memory_space=pltpu.SMEM)] + [any_] * 9, out_specs=[vmem] * 5, scratch_shapes=scratch,
        compiler_params=pltpu.CompilerParams(collective_id=1, has_side_effects=True, vmem_limit_bytes=52 * 2**20),
        name="layers",
    )(lens, x, ct, wq, wo, w1, w2, wc, gn, bs)
    def f4(*shape): return jax.ShapeDtypeStruct(shape, F4)
    return pl.pallas_call(
        finish_kernel,
        out_shape=[jax.ShapeDtypeStruct(x.shape, BF)] * 2 + [f4(1, width, 3 * width), f4(1, width, width), f4(1, width, hidden), f4(1, hidden, width),
                                                            f4(1, width, 2 * width), f4(3, 1, width), f4(3, 1, width)],
        in_specs=[vmem] * 5, out_specs=[any_] * 7 + [vmem] * 2,
        scratch_shapes=[V((4, SIDE, SIDE), F4), DMA((4,)), DMA((2,))],
        compiler_params=pltpu.CompilerParams(vmem_limit_bytes=6 * 2**20),
        name="finish",
    )(e0, e1, en, out, gin)


def local(layer_input, lengths, attn_qkv, attn_out, ffn_in, ffn_out, cross_weight, norm_gain, norm_bias, cotangent):
    def flat(a): return a.reshape(a.shape[1:])
    n = lax.axis_size("dp") // 2
    data = (layer_input.shape[1],) + layer_input.shape[3:]
    out, gin, *grads, gain, bias = layers(lengths.T, layer_input.reshape(data), cotangent.reshape(data), flat(attn_qkv), flat(attn_out), flat(ffn_in), flat(ffn_out),
                              flat(cross_weight), norm_gain.transpose(1, 0, 2), norm_bias.transpose(1, 0, 2), n)
    return (out.reshape(layer_input.shape), gin.reshape(layer_input.shape), *grads, gain.transpose(1, 0, 2), bias.transpose(1, 0, 2))


def solution(mesh):
    data = P("section", None, "dp", None, None)
    weight = P("section", None, None)
    return jax.shard_map(
        local, mesh=mesh,
        in_specs=(data, P(None, "dp")) + (weight,) * 7 + (data,),
        out_specs=(data, data) + (weight,) * 7,
        check_vma=False,
    )
```

time: 220 us -> 160 us (0.73)
  local copies, waits for them, and re-layouts: 23.9 us -> 0 us
  Pallas kernels: 179 us -> 159 us
  other arithmetic: 16 us -> 0 us
    pallas_call x2, Pallas kernels: 179 us -> 159 us  [the longest x1 152 us: layers(): pl.pallas_call(functools.partial(layers_kernel, n), out_shape=results, in...]
    unnamed x10 -> x0, local copies, waits for them, and re-layouts: 12.4 us -> none
    convert_element_type x4 -> x0, other arithmetic: 11.1 us -> none  [the longest x2 6.35 us: wide(): return blocks.transpose(1, 0, 2).reshape(1, 512, -1).astype(jnp.float32)]
    convert_element_type x3 -> x0, local copies, waits for them, and re-layouts: 9.53 us -> none  [wide(): return blocks.transpose(1, 0, 2).reshape(1, 512, -1).astype(jnp.float32)]
    slice x1 -> x0, other arithmetic: 4.93 us -> none  [local(): e0[4:].reshape(1, 2048, 512).astype(jnp.float32)]
where the time goes in v3:
time: 160 us; the launch traced here: 159 us
  Pallas kernels  159 us (99%)
    pallas_call x1, Pallas kernels, layers(): pl.pallas_call(functools.partial(layers_kernel, n), out_shape=results, in...  152 us
    pallas_call x1, Pallas kernels, layers(): pl.pallas_call(finish_kernel, out_shape=[jax.ShapeDtypeStruct(x.shape, BF...  6.16 us

profile of v3, /device:TPU:0, one launch (start us, length us, event | category | flops | bytes accessed | tf_op | source)
XLA Modules:
  0.0 159.5 jit_solution(16066798030279713215)
XLA Ops:
  0.6 152.5 %layers.1 = (bf16[8,512,512]{2,1,0:T(8,128)(2,1)S(1)}, bf16[6,512,512]{2,1,0:T(8,128)(2,1)S(1)}, f32[2,8,8,128]{3,2,1,0:T(8,128)S(1)}, bf16[2,256,512]{2,1,0:T(8,128)(2,1)S(1)}, bf16[2,256,512]{2,1,0:T(8,128)(2,1)S(1)}) custom-call(s32[1,2]{1,0:T(1,128)} %bitcast.27, bf16[2,256,512]{2,1,0:T(8,128)(2,1)} %bitcast.22, bf16[2,256,512]{2,1,0:T(8,128)(2,1)} %bitcast.23, ...), custom_call_target="tpu_custom_call" | custom-call | tf_op jit(solution)/shard_map/layers/pallas_call | solution.py:481
  153.1 6.2 %finish.1 = (bf16[2,256,512]{2,1,0:T(8,128)(2,1)}, bf16[2,256,512]{2,1,0:T(8,128)(2,1)}, f32[1,512,1536]{2,1,0:T(8,128)}, f32[1,512,512]{2,1,0:T(8,128)}, f32[1,...) custom-call(bf16[8,512,512]{2,1,0:T(8,128)(2,1)S(1)} %get-tuple-elem, ...), custom_call_target="tpu_custom_call" | custom-call | tf_op jit(solution)/shard_map/finish/pallas_call | solution.py:488

commit v4 on v3

--- a/solution.py
+++ b/solution.py
@@ -63,15 +63,15 @@
     return pltpu.make_async_remote_copy(src_ref=src, dst_ref=dst, send_sem=ss, recv_sem=rs, device_id=to, device_id_type=MESH)
 
 
-class Stream:
+class Flow:
     pass
 
 
 def layers_kernel(n, lens, x, ct, wq, wo, w1, w2, wc, gn, bs,
                   WF, WR, EN, OUT, GIN,
-                  X, CT, WC0, GN, BS, H1, QKV, PT, O, RR, ST, HQ, CQ, KV, PT2, O2, N2, A, GP, AFT, D, LOW, LOWC, DO, DQKV, DCQ, DKV, DST, T,
-                  G0, G1, NG, S0, S1, NS, R0, R1, NR, PG, PB,
-                  ld, wc_s, wc_r, wh_s, wh_r, st_s, st_r, ds_s, ds_r, dk_s, dk_r,
+                  X, CT, WC0, GN, BS, H1, QKV, PT, O, RR, ST, HQ, CQ, KV, PT2, O2, N2, A, GP, AFT, D, LOW, LOWC, LOWS, DO, DQKV, DCQ, DKV, DST, T,
+                  G0, G1, NG, CG, CS, S0, S1, NS, R0, R1, NR, PG, PB,
+                  ld, wc_s, wc_r, wh_s, wh_r, st_s, st_r, ds_s, ds_r, dk_s, dk_r, cg_s, cg_r,
                   sib_s, sib_r, rs_s, rs_r, ag_s, ag_r, sh_s, sh_r):
     sec, dp = lax.axis_index("section"), lax.axis_index("dp")
     core, chip = lax.rem(dp, 2), dp // 2
@@ -84,7 +84,9 @@
 
     sibling = dp + 1 - 2 * core
     partner, beside, after, before = (1 - sec, dp), (sec, sibling), (sec, ring_at(pos + 1)), (sec, ring_at(pos - 1))
+    across = (sec, dp + 2 - 4 * side)
     enc, dec = sec == 0, sec == 1
+    direct = 64 * n == SIDE
     length, width = X.shape[1], X.shape[2]
     hidden = A.shape[1]
     heads = width // 64
@@ -111,17 +113,19 @@
         for copy in loads[name]: copy.wait()
 
     bar = pltpu.get_barrier_semaphore()
-    for target in (partner, beside, after, before):
+    for target in (partner, beside, after, before, across):
         pl.semaphore_signal(bar, inc=1, device_id=target, device_id_type=MESH)
-    pl.semaphore_wait(bar, 4)
-
-    half = ds(core * (width // 2), width // 2)
-    wc_copy = remote(wc.at[half], WC0.at[half], wc_s, wc_r, partner)
-    wc_share = remote(WC0.at[half], WC0.at[half], wh_s, wh_r, beside)
+    pl.semaphore_wait(bar, 5)
+
+    def quarter(x, c): return WC0.at[ds((2 * x + c) * (width // 4), width // 4)]
+    wc_copy = remote(wc.at[ds((2 * side + core) * (width // 4), width // 4)], quarter(side, core), wc_s, wc_r, partner)
+    wc_trades = [remote(quarter(side, core), quarter(side, core), wh_s.at[0], wh_r.at[0], across),
+                 remote(quarter(side, core), quarter(side, core), wh_s.at[1], wh_r.at[1], beside),
+                 remote(quarter(1 - side, core), quarter(1 - side, core), wh_s.at[2], wh_r.at[2], beside)]
 
     def mrows(m): return ds(m * length, length)
     def st_copy(m): return remote(ST.at[mrows(m)], ST.at[mrows(m)], st_s.at[m], st_r.at[m], partner)
-    ds_copy = remote(DST.at[mrows(1)], DST.at[mrows(1)], ds_s, ds_r, partner)
+    def ds_copy(m): return remote(DST.at[mrows(m)], DST.at[mrows(m)], ds_s.at[m], ds_r.at[m], partner)
     def dk_copy(m): return remote(DKV.at[mrows(m)], DKV.at[mrows(m)], dk_s.at[m], dk_r.at[m], partner)
 
     @pl.when(enc)
@@ -146,38 +150,46 @@
     def attention(m, q, q0, k, k0, v, v0, P, out_ref):
         rows = mrows(m)
         usable = lax.broadcasted_iota(jnp.int32, (length, length), 0) < lens[0, m]
-        def pair(j):
-            def cols(c0): return ds(c0 + j * 128, 128)
-            q2, k2, vt = q[rows, cols(q0)], k[rows, cols(k0)], v[rows, cols(v0)].T
-            parts = []
-            for e in (0, 1):
-                s = jnp.where(usable, dot_nt(k2, q2 * query_masks[e]), -1e30)
-                w = jnp.exp(s - jnp.max(s, axis=0, keepdims=True))
-                p = (w * (1.0 / jnp.sum(w, axis=0, keepdims=True))).astype(BF)
-                P[m * heads + 2 * j + e] = p
-                parts.append(dot(vt[64 * e:64 * (e + 1)], p))
-            out_ref[rows, cols(0)] = jnp.concatenate(parts, axis=0).T.astype(BF)
-        loop(0, pairs, pair, unroll=4)
+        def cols(c0, j): return pl.ds(c0 + j * 128, 128)
+        def score(h):
+            j, e = h // 2, h % 2
+            return dot_nt(k[rows, cols(k0, j)], q[rows, cols(q0, j)] * query_masks[e])
+        def soft(s, h):
+            s = jnp.where(usable, s, -1e30)
+            w = jnp.exp(s - jnp.max(s, axis=0, keepdims=True))
+            p = (w * (1.0 / jnp.sum(w, axis=0, keepdims=True))).astype(BF)
+            P[m * heads + h] = p
+        for h in range(heads): soft(score(h), h)
+        for j in range(pairs):
+            vt = v[rows, cols(v0, j)].T
+            parts = [dot(vt[64 * e:64 * (e + 1)], P[m * heads + 2 * j + e]) for e in (0, 1)]
+            out_ref[rows, cols(0, j)] = jnp.concatenate(parts, axis=0).T.astype(BF)
 
     def attention_back(m, do, q, q0, k, k0, v, v0, P, dq, dq0, dk, dk0, dv, dv0):
         rows = mrows(m)
-        def pair(j):
-            def cols(c0): return ds(c0 + j * 128, 128)
-            q2, k2, v2, do2 = q[rows, cols(q0)], k[rows, cols(k0)], v[rows, cols(v0)], do[rows, cols(0)]
-            kt = k2.T
-            dvs, dks, dqs = [], [], []
-            for e in (0, 1):
-                p = P[m * heads + 2 * j + e]
-                pf = p.astype(F4)
-                t = pf * dot_nt(v2, do2 * head_masks[e])
-                dsc = (t - pf * jnp.sum(t, axis=0, keepdims=True)).astype(BF)
-                dvs.append(dot(p, do2))
-                dks.append(dot(dsc, q2))
-                dqs.append(dot(kt[64 * e:64 * (e + 1)], dsc))
-            dv[rows, cols(dv0)] = jnp.where(lane_low, dvs[0], dvs[1]).astype(BF)
-            dk[rows, cols(dk0)] = (jnp.where(lane_low, dks[0], dks[1]) * 0.125).astype(BF)
-            dq[rows, cols(dq0)] = (jnp.concatenate(dqs, axis=0).T * 0.125).astype(BF)
-        loop(0, pairs, pair, unroll=4)
+        def cols(c0, j): return pl.ds(c0 + j * 128, 128)
+        def weights(h): return P.at[m * heads + h]
+        def grad_scores(h):
+            j, e = h // 2, h % 2
+            pf = weights(h)[...].astype(F4)
+            t = pf * dot_nt(v[rows, cols(v0, j)], do[rows, cols(0, j)] * head_masks[e])
+            return (t - pf * jnp.sum(t, axis=0, keepdims=True)).astype(BF)
+        def put_v(j):
+            do2 = do[rows, cols(0, j)]
+            dv[rows, cols(dv0, j)] = jnp.where(lane_low, dot(weights(2 * j)[...], do2), dot(weights(2 * j + 1)[...], do2)).astype(BF)
+        def put_k(j):
+            q2 = q[rows, cols(q0, j)]
+            dk[rows, cols(dk0, j)] = (jnp.where(lane_low, dot(weights(2 * j)[...], q2), dot(weights(2 * j + 1)[...], q2)) * 0.125).astype(BF)
+        def put_q(j):
+            kt = k[rows, cols(k0, j)].T
+            parts = [dot(kt[64 * e:64 * (e + 1)], weights(2 * j + e)[...]) for e in (0, 1)]
+            dq[rows, cols(dq0, j)] = (jnp.concatenate(parts, axis=0).T * 0.125).astype(BF)
+        for j in range(pairs):
+            put_v(j)
+            for h in (2 * j, 2 * j + 1): weights(h)[...] = grad_scores(h)
+        for j in range(pairs):
+            put_k(j)
+            put_q(j)
 
     def tiles(count): return [(t, pl.ds(t * TILE, TILE)) for t in range(count // TILE)]
     def tile_of(ref, b0, t): return block(ref, b0 + t * TILE // SIDE)[:, pl.ds(t * TILE % SIDE, TILE)]
@@ -225,21 +237,37 @@
     def _():
         arrived("ffn")
         wc_copy.wait_recv()
-        wc_share.start()
-        wc_share.wait_recv()
+        wc_trades[0].start()
+        wc_trades[1].start()
+        for m in (0, 1):
+            norm_into(RR.at[0], m, 1, HQ)
+            for t, at in tiles(width): CQ[mrows(m), at] = dot(HQ[mrows(m), :], tile_of(WR, 4, t)).astype(BF)
+        wc_trades[0].wait_recv()
+        wc_trades[2].start()
+        wc_trades[1].wait_recv()
+        wc_trades[2].wait_recv()
+
+    def bottom(m, hook=None):
+        rows = mrows(m)
+        LOWS[rows, :] = D[rows, :].astype(BF)
+        for t, at in tiles(width): DO[rows, at] = dot_nt(LOWS[rows, :], rows_of(WR, 3, t)).astype(BF)
+        if hook is not None: hook(m, 0)
+        attention_back(m, DO, QKV, 0, QKV, width, QKV, 2 * width, PT, DQKV, 0, DQKV, width, DQKV, 2 * width)
+        if hook is not None: hook(m, 1)
+        for t, at in tiles(width):
+            total = dot_nt(DQKV[rows, columns(0)], rows_of(WR, 0, t))
+            for b in (1, 2): total = total + dot_nt(DQKV[rows, columns(b)], rows_of(WR, b, t))
+            AFT[rows, at] = total
+        unit, scale = normalize(X[m].astype(F4))
+        grad = AFT[rows, :]
+        add_norm_grads(0, grad, unit)
+        GIN[m] = (D[rows, :] + norm_back(grad, unit, scale, gain_at(0))).astype(BF)
 
     def middle(m):
         rows = mrows(m)
         @pl.when(enc)
         def _():
-            @pl.when(m == 0)
-            def _():
-                dk_copy(0).wait_recv()
-                for t, at in tiles(width):
-                    total = dot_nt(DKV[rows, columns(0)], rows_of(WR, 4, t)) + dot_nt(DKV[rows, columns(1)], rows_of(WR, 5, t))
-                    DST[rows, at] = total.astype(BF)
-            @pl.when(m == 1)
-            def _(): ds_copy.wait_recv()
+            ds_copy(m).wait_recv()
             unit, scale = normalize(AFT[rows, :])
             grad = CT[m].astype(F4) + DST[rows, :].astype(F4)
             add_norm_grads(2, grad, unit)
@@ -248,8 +276,6 @@
             LOW[rows, :] = back.astype(BF)
         @pl.when(dec)
         def _():
-            norm_into(RR.at[0], m, 1, HQ)
-            for t, at in tiles(width): CQ[rows, at] = dot(HQ[rows, :], tile_of(WR, 4, t)).astype(BF)
             st_copy(m).wait_recv()
             for t, at in tiles(2 * width): KV[rows, at] = dot(ST[rows, :], WC0[:, at]).astype(BF)
             attention(m, CQ, 0, KV, 0, KV, width, PT2, O2)
@@ -272,74 +298,99 @@
             LOWC[rows, :] = D[rows, :].astype(BF)
             for t, at in tiles(width): DO[rows, at] = dot_nt(LOWC[rows, :], rows_of(WR, 5, t)).astype(BF)
             attention_back(m, DO, CQ, 0, KV, 0, KV, width, PT2, DCQ, 0, DKV, 0, DKV, width)
-            @pl.when(m == 1)
-            def _():
-                for t, at in tiles(width): DST[rows, at] = dot_nt(DKV[rows, :], WC0[at, :]).astype(BF)
-                ds_copy.start()
-            dk_copy(m).start()
+            for t, at in tiles(width): DST[rows, at] = dot_nt(DKV[rows, :], WC0[at, :]).astype(BF)
+            ds_copy(m).start()
+            if not direct:
+                @pl.when(m == 1)
+                def _():
+                    for i in (0, 1): dk_copy(i).start()
             for t, at in tiles(width): AFT[rows, at] = dot_nt(DCQ[rows, :], rows_of(WR, 4, t))
             unit, scale = normalize(RR[0, rows, :])
             grad = AFT[rows, :]
             add_norm_grads(1, grad, unit)
             D[rows, :] = D[rows, :] + norm_back(grad, unit, scale, gain_at(1))
+        @pl.when(enc & (m == 0))
+        def _(): bottom(m)
     loop(0, 2, middle)
 
     part = 16 * n
+    far = n // 2
     other_rows = ds((1 - core) * 2 * part, 2 * part)
     def rows_at(d, k, c): return ds((c * 2 + d) * part + k * 16, 16)
-    streams = []
+    group = [[], []]
     for g, (G, S, R, E) in enumerate(((G0, S0, R0, WF), (G1, S1, R1, WR))):
-        for d in (0, 1):
-            st = Stream()
-            st.i, st.d, st.g, st.to = len(streams), d, g, after if d == 0 else before
-            st.own = lambda k, G=G, d=d: G.at[:, rows_at(d, k, core), :]
-            st.sib = lambda k, S=S, d=d: S.at[:, rows_at(d, k, 0), :]
-            st.slot = lambda s, R=R, d=d: R.at[d, s]
-            st.res = lambda k, E=E, d=d: E.at[:, rows_at(d, k, core), :]
-            streams.append(st)
-    st = Stream()
-    st.i, st.d, st.g, st.to = 4, 0, 1, after
-    st.own, st.sib, st.slot, st.res = (lambda k: NG.at[core, k]), (lambda k: NS.at[k]), (lambda s: NR.at[s]), (lambda k: EN.at[core, k])
-    streams.append(st)
-    group = [[st for st in streams if st.g == g] for g in (0, 1)]
-
-    def chunk(st, s): return lax.rem(pos - s + 2 * n, n) if st.d == 0 else lax.rem(pos + s, n)
-    def rs_copy(st, s): return remote(st.own(chunk(st, s)), st.slot(s), rs_s.at[st.i, s], rs_r.at[st.i, s], st.to)
-    def ag_copy(st, t):
-        res = st.res(chunk(st, t + n - 1))
-        return remote(res, res, ag_s.at[st.i, t], ag_r.at[st.i, t], st.to)
-    def sh_copy(st, t):
-        res = st.res(chunk(st, t + n - 1))
-        return remote(res, res, sh_s.at[st.i, t], sh_r.at[st.i, t], beside)
+        cuts = (0, G.shape[0] // 2, G.shape[0]) if G.shape[0] > 1 else (0, 1)
+        for u, stop in zip(cuts, cuts[1:]):
+            us = pl.ds(u, stop - u)
+            for d in (0, 1):
+                for way in (1, -1):
+                    f = Flow()
+                    f.way, f.far = way, far if (d == 0) == (way == 1) else far - 1
+                    f.own = lambda k, G=G, d=d, us=us: G.at[us, rows_at(d, k, core), :]
+                    f.sib = lambda k, S=S, d=d, us=us: S.at[us, rows_at(d, k, 0), :]
+                    f.slot = lambda s, R=R, d=d, us=us, w=(1 - way) // 2: R.at[d, w, s, us]
+                    f.res = lambda k, E=E, d=d, us=us: E.at[us, rows_at(d, k, core), :]
+                    group[g].append(f)
+    for way in (1, -1):
+        f = Flow()
+        f.way, f.far = way, far if way == 1 else far - 1
+        f.own, f.sib, f.res = (lambda k: NG.at[core, k]), (lambda k: NS.at[k]), (lambda k: EN.at[core, k])
+        f.slot = lambda s, w=(1 - way) // 2: NR.at[w, s]
+        group[1].append(f)
+    for i, f in enumerate(group[0] + group[1]): f.i, f.to = i, after if f.way == 1 else before
+
+    def owner(f, steps): return lax.rem(pos + f.way * steps + n, n)
+    def rs_copy(f, s): return remote(f.own(owner(f, far - s)), f.slot(s), rs_s.at[f.i, s], rs_r.at[f.i, s], f.to)
+    def ag_copy(f, t):
+        res = f.res(owner(f, -t))
+        return remote(res, res, ag_s.at[f.i, t], ag_r.at[f.i, t], f.to)
+    def sh_copy(f, t):
+        res = f.res(owner(f, -t))
+        return remote(res, res, sh_s.at[f.i, t], sh_r.at[f.i, t], beside)
     sib_copies = [[remote(G.at[u, other_rows], S.at[u], sib_s.at[g, u], sib_r.at[g, u], beside) for u in range(G.shape[0])]
                   for g, (G, S) in enumerate(((G0, S0), (G1, S1)))]
     sib_copies[1].append(remote(NG.at[1 - core], NS, sib_s.at[1, G1.shape[0]], sib_r.at[1, G1.shape[0]], beside))
 
-    def reduce_step(g, s, first=False, last=False):
-        for st in group[g]:
-            own = st.own(chunk(st, s))
-            total = own[...].astype(F4) + st.sib(chunk(st, s))[...].astype(F4)
-            if not first:
-                rs_copy(st, s - 1).wait_recv()
-                total = total + st.slot(s - 1)[...].astype(F4)
-            if last:
-                st.res(chunk(st, s))[...] = total.astype(own.dtype)
-                ag_copy(st, 0).start()
-                sh_copy(st, 0).start()
-            else:
-                own[...] = total.astype(own.dtype)
-                rs_copy(st, s).start()
-
-    def gather_step(g, t):
-        for st in group[g]:
-            ag_copy(st, t).wait_recv()
-            @pl.when(t < n - 2)
-            def _(): ag_copy(st, t + 1).start()
-            sh_copy(st, t + 1).start()
+    def reduce_round(g, s):
+        for f in group[g]:
+            start = far - f.far
+            if isinstance(s, int) and s < start: continue
+            own, sib = f.own(owner(f, far - s)), f.sib(owner(f, far - s))
+            total = own[...].astype(F4) + sib[...].astype(F4)
+            if not isinstance(s, int) or s > start:
+                rs_copy(f, s - 1).wait_recv()
+                total = total + f.slot(s - 1)[...].astype(F4)
+            own[...] = total.astype(own.dtype)
+            rs_copy(f, s).start()
+
+    def settle(g):
+        for f, b in zip(group[g][::2], group[g][1::2]):
+            total = f.own(pos)[...].astype(F4) + f.sib(pos)[...].astype(F4)
+            for side_flow in (f, b):
+                rs_copy(side_flow, far - 1).wait_recv()
+                total = total + side_flow.slot(far - 1)[...].astype(F4)
+            f.res(pos)[...] = total.astype(f.own(pos).dtype)
+            ag_copy(f, 0).start()
+            ag_copy(b, 0).start()
+            sh_copy(f, 0).start()
+
+    def gather_round(g, t):
+        for f in group[g]:
+            if isinstance(t, int) and t > f.far: continue
+            ag_copy(f, t - 1).wait_recv()
+            if not isinstance(t, int) or t < f.far: ag_copy(f, t).start()
+            sh_copy(f, t).start()
+        for f in group[g]:
+            if isinstance(t, int) and t > f.far: continue
+            ag_copy(f, t - 1).wait_send()
+            rs_copy(f, far - t).wait_send()
 
     def begin(g):
-        for copy in sib_copies[g]: copy.wait_recv()
-        reduce_step(g, 0, first=True)
+        for u, copy in enumerate(sib_copies[g]):
+            if direct and g == 1 and u in (4, 5): pl.when(dec)(copy.wait_recv)
+            else: copy.wait_recv()
+        if direct and g == 1: pl.when(enc)(cg_copy.wait_recv)
+        reduce_round(g, 0)
 
     def done_blocks(g, G, count):
         per = G.shape[1] // SIDE
@@ -352,77 +403,85 @@
             block(G, b0 + b)[...] = dot(T[...], grad[:, columns(b)]).astype(BF)
             done_blocks(g, G, b0 + b + 1)
 
+    own_rows = ds(core * (SIDE // 2), SIDE // 2)
+    cg_trade = remote(CG.at[:, ds((1 - core) * (SIDE // 2), SIDE // 2)], CS, cg_s.at[0], cg_r.at[0], beside)
+    cg_copy = remote(CG.at[:, own_rows], G1.at[pl.ds(4, 2), own_rows], cg_s.at[1], cg_r.at[1], partner) if direct else None
+    if direct:
+        @pl.when(dec)
+        def _():
+            T[...] = ST[...].T
+            for b in range(2): CG[b] = dot(T[...], DKV[:, columns(b)]).astype(BF)
+            cg_trade.start()
+        @pl.when(enc)
+        def _(): S1[pl.ds(4, 2)] = jnp.zeros((2, SIDE // 2, SIDE), BF)
     weight_grads(0, G0, N2, GP, 4, 0)
+    if direct:
+        @pl.when(dec)
+        def _():
+            cg_trade.wait_recv()
+            CG[:, own_rows, :] = (CG[:, own_rows, :].astype(F4) + CS[...].astype(F4)).astype(BF)
+            cg_copy.start()
     for b in range(4):
         block(G0, 4 + b)[...] = dot(A[:, columns(b)].T, LOW[...]).astype(BF)
         done_blocks(0, G0, 4 + b + 1)
-    begin(0)
-
-    def bottom(m):
-        rows = mrows(m)
-        LOW[rows, :] = D[rows, :].astype(BF)
-        for t, at in tiles(width): DO[rows, at] = dot_nt(LOW[rows, :], rows_of(WR, 3, t)).astype(BF)
-        attention_back(m, DO, QKV, 0, QKV, width, QKV, 2 * width, PT, DQKV, 0, DQKV, width, DQKV, 2 * width)
-        for t, at in tiles(width):
-            total = dot_nt(DQKV[rows, columns(0)], rows_of(WR, 0, t))
-            for b in (1, 2): total = total + dot_nt(DQKV[rows, columns(b)], rows_of(WR, b, t))
-            AFT[rows, at] = total
-        unit, scale = normalize(X[m].astype(F4))
-        grad = AFT[rows, :]
-        add_norm_grads(0, grad, unit)
-        GIN[m] = (D[rows, :] + norm_back(grad, unit, scale, gain_at(0))).astype(BF)
-        reduce_step(0, m + 1)
-    loop(0, 2, bottom)
+    first_left = jnp.where(enc, 1, 0)
+
+    def start_ring(m, place):
+        @pl.when(m == first_left)
+        def _(): begin(0) if place == 0 else reduce_round(0, 1)
+    loop(first_left, 2, lambda m: bottom(m, start_ring))
     NG[...] = jnp.zeros_like(NG)
     for j in range(4):
         NG[0, j] = PG[:, 128 * j:128 * (j + 1)]
         NG[1, j] = PB[:, 128 * j:128 * (j + 1)]
     sib_copies[1][-1].start()
     weight_grads(1, G1, H1, DQKV, 3, 0)
-    weight_grads(1, G1, O, LOW, 1, 3)
-    @pl.when(enc)
-    def _():
-        dk_copy(1).wait_recv()
-        T[...] = ST[...].T
-        for b in range(2): block(G1, 4 + b)[...] = dot(T[...], DKV[:, columns(b)]).astype(BF)
+    weight_grads(1, G1, O, LOWS, 1, 3)
+    if not direct:
+        @pl.when(enc)
+        def _():
+            for m in (0, 1): dk_copy(m).wait_recv()
+            T[...] = ST[...].T
+            for b in range(2): block(G1, 4 + b)[...] = dot(T[...], DKV[:, columns(b)]).astype(BF)
     @pl.when(dec)
     def _():
         for b, (source, grad) in enumerate(((HQ, DCQ), (O2, LOWC))):
             T[...] = source[...].T
             block(G1, 4 + b)[...] = dot(T[...], grad[...]).astype(BF)
-    for b in range(2): done_blocks(1, G1, 5 + b)
-    reduce_step(0, 3)
-    ahead = 4
+            if direct: done_blocks(1, G1, 5 + b)
+    if not direct: done_blocks(1, G1, 6)
     begin(1)
-    if n - 1 > ahead:
-        reduce_step(0, ahead)
-        def both(i):
-            reduce_step(1, i)
-            reduce_step(0, i + ahead)
-        loop(1, n - 1 - ahead, both)
-        reduce_step(1, n - 1 - ahead)
-    reduce_step(0, n - 1, last=True)
-    def cross_over(i):
-        reduce_step(1, n - ahead + i)
-        gather_step(0, i)
-    loop(0, ahead - 1, cross_over)
-    reduce_step(1, n - 1, last=True)
-    gather_step(0, ahead - 1)
-    def both_out(i):
-        gather_step(0, ahead + i)
-        gather_step(1, i)
-    loop(0, n - 1 - ahead, both_out)
-    loop(n - 1 - ahead, n - 1, lambda t: gather_step(1, t))
-
-    def drain(s):
-        for st in streams:
-            sh_copy(st, s).wait()
-            @pl.when(s < n - 1)
-            def _():
-                rs_copy(st, s).wait_send()
-                ag_copy(st, s).wait_send()
-    loop(0, n, drain)
-    for copy in sib_copies[0] + sib_copies[1]: copy.wait_send()
+    if far == 4:
+        reduce_round(0, 2)
+        reduce_round(1, 1)
+        reduce_round(0, 3)
+        reduce_round(1, 2)
+        settle(0)
+        reduce_round(1, 3)
+        gather_round(0, 1)
+        settle(1)
+        gather_round(0, 2)
+        gather_round(1, 1)
+        gather_round(0, 3)
+        gather_round(1, 2)
+        gather_round(0, 4)
+        gather_round(1, 3)
+        gather_round(1, 4)
+    else:
+        reduce_round(1, 1)
+        for g in (0, 1):
+            loop(2, far, lambda s: reduce_round(g, s))
+            settle(g)
+            loop(1, far - 1, lambda t: gather_round(g, t))
+            gather_round(g, far - 1)
+            gather_round(g, far)
+    for f in group[0] + group[1]:
+        if f.way == 1: sh_copy(f, 0).wait()
+        loop(1, f.far + 1, lambda t: sh_copy(f, t).wait())
+    for g in (0, 1):
+        for u, copy in enumerate(sib_copies[g]):
+            if direct and g == 1 and u in (4, 5): pl.when(dec)(copy.wait_send)
+            else: copy.wait_send()
 
     @pl.when(enc)
     def _():
@@ -430,9 +489,13 @@
         for m in (0, 1): st_copy(m).wait_send()
     @pl.when(dec)
     def _():
-        wc_share.wait_send()
-        ds_copy.wait_send()
-        for m in (0, 1): dk_copy(m).wait_send()
+        for trade in wc_trades: trade.wait_send()
+        for m in (0, 1):
+            ds_copy(m).wait_send()
+            if not direct: dk_copy(m).wait_send()
+        if direct:
+            cg_trade.wait_send()
+            cg_copy.wait_send()
 
 
 def finish_kernel(e0, e1, en, out, gin, o_out, o_gin, o_qkv, o_wo, o_up, o_down, o_cross, o_gain, o_bias, F, sem, sem2):
@@ -467,21 +530,21 @@
     s0, s1 = units(8), units(6)
     norm = (2, n, 8, 128)
     def own(s): return (s[0], s[1] // 2, SIDE)
-    def slots(s): return (2, n - 1, s[0], 16, SIDE)
+    def slots(s): return (2, 2, n // 2, s[0], 16, SIDE)
     sq = V((rows, width), BF)
     probs = V((micro * width // 64, length, length), BF)
     scratch = [V(x.shape, BF), V(x.shape, BF), V(wc.shape, BF), V(gn.shape, F4), V(bs.shape, F4)]
     scratch += [sq, V((rows, 3 * width), BF), probs, sq, V((2, rows, width), F4), sq, sq, sq, V((rows, 2 * width), BF), probs, sq, sq,
                 V((rows, hidden), BF), V((rows, hidden), BF), V((rows, width), F4), V((rows, width), F4),
-                sq, sq, sq, V((rows, 3 * width), BF), sq, V((rows, 2 * width), BF), sq, V((width, rows), BF)]
-    scratch += [V(s0, BF), V(s1, BF), V(norm, F4), V(own(s0), BF), V(own(s1), BF), V(norm[1:], F4), V(slots(s0), BF), V(slots(s1), BF), V((n - 1, 8, 128), F4),
+                sq, sq, sq, sq, V((rows, 3 * width), BF), sq, V((rows, 2 * width), BF), sq, V((width, rows), BF)]
+    scratch += [V(s0, BF), V(s1, BF), V(norm, F4), V((2, SIDE, SIDE), BF), V((2, SIDE // 2, SIDE), BF), V(own(s0), BF), V(own(s1), BF), V(norm[1:], F4), V(slots(s0), BF), V(slots(s1), BF), V((2, n // 2, 8, 128), F4),
                 V((8, width), F4), V((8, width), F4)]
-    scratch += [DMA((18,)), DMA, DMA, DMA, DMA, DMA((2,)), DMA((2,)), DMA, DMA, DMA((2,)), DMA((2,)), DMA((2, 9)), DMA((2, 9))] + [DMA((5, n))] * 6
+    scratch += [DMA((18,)), DMA, DMA, DMA((3,)), DMA((3,)), DMA((2,)), DMA((2,)), DMA((2,)), DMA((2,)), DMA((2,)), DMA((2,)), DMA((2,)), DMA((2,)), DMA((2, 9)), DMA((2, 9))] + [DMA((18 if s0[0] > 1 else 10, n // 2 + 1))] * 6
     results = [V(s0, BF), V(s1, BF), V(norm, F4), V(x.shape, BF), V(x.shape, BF)]
     e0, e1, en, out, gin = pl.pallas_call(
         functools.partial(layers_kernel, n), out_shape=results,
         in_specs=[pl.BlockSpec(memory_space=pltpu.SMEM)] + [any_] * 9, out_specs=[vmem] * 5, scratch_shapes=scratch,
-        compiler_params=pltpu.CompilerParams(collective_id=1, has_side_effects=True, vmem_limit_bytes=52 * 2**20),
+        compiler_params=pltpu.CompilerParams(collective_id=1, has_side_effects=True, vmem_limit_bytes=54 * 2**20),
         name="layers",
     )(lens, x, ct, wq, wo, w1, w2, wc, gn, bs)
     def f4(*shape): return jax.ShapeDtypeStruct(shape, F4)

time: 160 us -> 138 us (0.86)
  Pallas kernels: 159 us -> 137 us
    pallas_call x1, Pallas kernels: 152 us -> 131 us  [layers(): pl.pallas_call(functools.partial(layers_kernel, n), out_shape=results, in...]
where the time goes in v4:
time: 138 us
  Pallas kernels  137 us (99%)
    pallas_call x1, Pallas kernels, layers(): pl.pallas_call(functools.partial(layers_kernel, n), out_shape=results, in...  131 us
    pallas_call x1, Pallas kernels, layers(): pl.pallas_call(finish_kernel, out_shape=[jax.ShapeDtypeStruct(x.shape, BF...  6.16 us

profile of v4, /device:TPU:0, one launch (start us, length us, event | category | flops | bytes accessed | tf_op | source)
XLA Modules:
  0.0 137.5 jit_solution(10993042111080365045)
XLA Ops:
  0.6 130.5 %layers.1 = (bf16[8,512,512]{2,1,0:T(8,128)(2,1)S(1)}, bf16[6,512,512]{2,1,0:T(8,128)(2,1)S(1)}, f32[2,8,8,128]{3,2,1,0:T(8,128)S(1)}, bf16[2,256,512]{2,1,0:T(8,128)(2,1)S(1)}, bf16[2,256,512]{2,1,0:T(8,128)(2,1)S(1)}) custom-call(s32[1,2]{1,0:T(1,128)} %bitcast.27, bf16[2,256,512]{2,1,0:T(8,128)(2,1)} %bitcast.22, bf16[2,256,512]{2,1,0:T(8,128)(2,1)} %bitcast.23, ...), custom_call_target="tpu_custom_call" | custom-call | tf_op jit(solution)/shard_map/layers/pallas_call | solution.py:544
  131.2 6.2 %finish.1 = (bf16[2,256,512]{2,1,0:T(8,128)(2,1)}, bf16[2,256,512]{2,1,0:T(8,128)(2,1)}, f32[1,512,1536]{2,1,0:T(8,128)}, f32[1,512,512]{2,1,0:T(8,128)}, f32[1,...) custom-call(bf16[8,512,512]{2,1,0:T(8,128)(2,1)S(1)} %get-tuple-elem, ...), custom_call_target="tpu_custom_call" | custom-call | tf_op jit(solution)/shard_map/finish/pallas_call | solution.py:551

commit v5 on v4

--- a/solution.py
+++ b/solution.py
@@ -313,89 +313,131 @@
         def _(): bottom(m)
     loop(0, 2, middle)
 
-    part = 16 * n
     far = n // 2
-    other_rows = ds((1 - core) * 2 * part, 2 * part)
-    def rows_at(d, k, c): return ds((c * 2 + d) * part + k * 16, 16)
+    def half_rows(c): return ds(c * 32 * n, 32 * n)
+    def rows_at(k, c, lo, count): return pl.ds(pl.multiple_of(c * 32 * n + k * 32 + lo, 16), count)
     group = [[], []]
     for g, (G, S, R, E) in enumerate(((G0, S0, R0, WF), (G1, S1, R1, WR))):
         cuts = (0, G.shape[0] // 2, G.shape[0]) if G.shape[0] > 1 else (0, 1)
-        for u, stop in zip(cuts, cuts[1:]):
+        for sub, (u, stop) in enumerate(zip(cuts, cuts[1:])):
             us = pl.ds(u, stop - u)
-            for d in (0, 1):
-                for way in (1, -1):
-                    f = Flow()
-                    f.way, f.far = way, far if (d == 0) == (way == 1) else far - 1
-                    f.own = lambda k, G=G, d=d, us=us: G.at[us, rows_at(d, k, core), :]
-                    f.sib = lambda k, S=S, d=d, us=us: S.at[us, rows_at(d, k, 0), :]
-                    f.slot = lambda s, R=R, d=d, us=us, w=(1 - way) // 2: R.at[d, w, s, us]
-                    f.res = lambda k, E=E, d=d, us=us: E.at[us, rows_at(d, k, core), :]
-                    group[g].append(f)
+            for way in (1, -1):
+                f = Flow()
+                f.way, f.norm, f.g, f.sub = way, False, g, sub
+                f.own = lambda k, lo, count, G=G, us=us: G.at[us, rows_at(k, core, lo, count), :]
+                f.sib = lambda k, lo, count, S=S, us=us: S.at[us, rows_at(k, 0, lo, count), :]
+                f.slot = lambda s, lo, count, R=R, us=us, w=(1 - way) // 2: R.at[w, s, us, pl.ds(lo, count)]
+                f.res = lambda k, lo, count, E=E, us=us: E.at[us, rows_at(k, core, lo, count), :]
+                group[g].append(f)
     for way in (1, -1):
         f = Flow()
-        f.way, f.far = way, far if way == 1 else far - 1
-        f.own, f.sib, f.res = (lambda k: NG.at[core, k]), (lambda k: NS.at[k]), (lambda k: EN.at[core, k])
-        f.slot = lambda s, w=(1 - way) // 2: NR.at[w, s]
+        f.way, f.norm, f.g, f.sub = way, True, 2, 2
+        f.own, f.sib, f.res = (lambda k, *_: NG.at[core, k]), (lambda k, *_: NS.at[k]), (lambda k, *_: EN.at[core, k])
+        f.slot = lambda s, *_, w=(1 - way) // 2: NR.at[w, s]
         group[1].append(f)
-    for i, f in enumerate(group[0] + group[1]): f.i, f.to = i, after if f.way == 1 else before
+    for i, f in enumerate(group[0] + group[1]): f.i, f.to, f.lo = i, after if f.way == 1 else before, 0 if f.way == 1 else 16
 
     def owner(f, steps): return lax.rem(pos + f.way * steps + n, n)
-    def rs_copy(f, s): return remote(f.own(owner(f, far - s)), f.slot(s), rs_s.at[f.i, s], rs_r.at[f.i, s], f.to)
+    def piece(f, outer): return (f.lo, 16) if outer else (0, 32)
+    def rs_copy(f, s):
+        at = piece(f, isinstance(s, int) and s == 0)
+        return remote(f.own(owner(f, far - s), *at), f.slot(s, *at), rs_s.at[f.g], rs_r.at[f.i, s], f.to)
+    def ag_piece(f, t): return piece(f, isinstance(t, int) and t == far - 1)
     def ag_copy(f, t):
-        res = f.res(owner(f, -t))
-        return remote(res, res, ag_s.at[f.i, t], ag_r.at[f.i, t], f.to)
-    def sh_copy(f, t):
-        res = f.res(owner(f, -t))
-        return remote(res, res, sh_s.at[f.i, t], sh_r.at[f.i, t], beside)
-    sib_copies = [[remote(G.at[u, other_rows], S.at[u], sib_s.at[g, u], sib_r.at[g, u], beside) for u in range(G.shape[0])]
-                  for g, (G, S) in enumerate(((G0, S0), (G1, S1)))]
-    sib_copies[1].append(remote(NG.at[1 - core], NS, sib_s.at[1, G1.shape[0]], sib_r.at[1, G1.shape[0]], beside))
-
-    def reduce_round(g, s):
+        res = f.res(owner(f, -t), *ag_piece(f, t))
+        return remote(res, res, ag_s.at[f.g], ag_r.at[f.i, t], f.to)
+    def sh_start(f, t, at):
+        res = f.res(owner(f, -t), *at)
+        remote(res, res, sh_s.at[f.g], sh_r.at[f.g], beside).start()
+
+    def sib_key(g, u): return g * 3 + (0 if G0.shape[0] == 1 else u // 4 if g == 0 else (0, 0, 0, 1, 2, 2)[u])
+    def sib_copy(g, u):
+        G, S = ((G0, S0), (G1, S1))[g]
+        return remote(G.at[u, half_rows(1 - core)], S.at[u], sib_s.at[sib_key(g, u)], sib_r.at[sib_key(g, u)], beside)
+    sib_norm = remote(NG.at[1 - core], NS, sib_s.at[6], sib_r.at[6], beside)
+    def sib_all(g, key):
+        G, S = ((G0, S0), (G1, S1))[g]
+        us = [u for u in range(G.shape[0]) if sib_key(g, u) == g * 3 + key]
+        if not us: return None
+        us = pl.ds(us[0], len(us))
+        return remote(G.at[us, half_rows(1 - core)], S.at[us], sib_s.at[g * 3 + key], sib_r.at[g * 3 + key], beside)
+    def sib_wait(g, sub):
+        for key in ((0,), (1, 2))[sub]:
+            copy = sib_all(g, key)
+            if copy is None: continue
+            if direct and g == 1 and key == 2: pl.when(dec)(copy.wait_recv)
+            else: copy.wait_recv()
+
+    def reduce_round(g, s, subs=(0, 1, 2)):
         for f in group[g]:
-            start = far - f.far
-            if isinstance(s, int) and s < start: continue
-            own, sib = f.own(owner(f, far - s)), f.sib(owner(f, far - s))
-            total = own[...].astype(F4) + sib[...].astype(F4)
-            if not isinstance(s, int) or s > start:
-                rs_copy(f, s - 1).wait_recv()
-                total = total + f.slot(s - 1)[...].astype(F4)
-            own[...] = total.astype(own.dtype)
+            if f.sub not in subs: continue
+            k = owner(f, far - s)
+            def partial(at, received):
+                own = f.own(k, *at)
+                total = own[...].astype(F4) + f.sib(k, *at)[...].astype(F4)
+                if received: total = total + f.slot(s - 1, *at)[...].astype(F4)
+                own[...] = total.astype(own.dtype)
+            first, second = isinstance(s, int) and s == 0, isinstance(s, int) and s == 1
+            if first and f.norm and f.way == -1: continue
+            if not first and not (second and f.norm and f.way == -1): rs_copy(f, s - 1).wait_recv()
+            if first: partial(piece(f, True), False)
+            elif second and f.norm: partial((0, 32), f.way == 1)
+            elif second:
+                partial((f.lo, 16), True)
+                partial((16 - f.lo, 16), False)
+            else: partial((0, 32), True)
             rs_copy(f, s).start()
 
     def settle(g):
         for f, b in zip(group[g][::2], group[g][1::2]):
-            total = f.own(pos)[...].astype(F4) + f.sib(pos)[...].astype(F4)
-            for side_flow in (f, b):
-                rs_copy(side_flow, far - 1).wait_recv()
-                total = total + side_flow.slot(far - 1)[...].astype(F4)
-            f.res(pos)[...] = total.astype(f.own(pos).dtype)
+            total = f.own(pos, 0, 32)[...].astype(F4) + f.sib(pos, 0, 32)[...].astype(F4)
+            for flow in (f, b):
+                rs_copy(flow, far - 1).wait_recv()
+                total = total + flow.slot(far - 1, 0, 32)[...].astype(F4)
+            f.res(pos, 0, 32)[...] = total.astype(f.res(pos, 0, 32).dtype)
             ag_copy(f, 0).start()
             ag_copy(b, 0).start()
-            sh_copy(f, 0).start()
+            sh_start(f, 0, (0, 32))
 
     def gather_round(g, t):
         for f in group[g]:
-            if isinstance(t, int) and t > f.far: continue
+            def active(t): return not (isinstance(t, int) and f.norm and f.way == -1 and t == far - 1)
+            if not active(t - 1): continue
             ag_copy(f, t - 1).wait_recv()
-            if not isinstance(t, int) or t < f.far: ag_copy(f, t).start()
-            sh_copy(f, t).start()
-        for f in group[g]:
-            if isinstance(t, int) and t > f.far: continue
-            ag_copy(f, t - 1).wait_send()
-            rs_copy(f, far - t).wait_send()
-
-    def begin(g):
-        for u, copy in enumerate(sib_copies[g]):
-            if direct and g == 1 and u in (4, 5): pl.when(dec)(copy.wait_recv)
-            else: copy.wait_recv()
-        if direct and g == 1: pl.when(enc)(cg_copy.wait_recv)
-        reduce_round(g, 0)
+            if not (isinstance(t, int) and t == far) and active(t): ag_copy(f, t).start()
+            sh_start(f, t, ag_piece(f, t - 1))
+
+    def begin(g, subs=(0, 1, 2)):
+        for sub in (0, 1):
+            if sub in subs and (sub == 0 or G0.shape[0] > 1):
+                sib_wait(g, sub)
+                if direct and g == 1 and sub == 1: pl.when(enc)(cg_copy.wait_recv)
+                reduce_round(g, 0, (sub,))
+        if g == 1:
+            sib_norm.wait_recv()
+            reduce_round(1, 0, (2,))
+
+    def close_ring():
+        for g, (G, E) in enumerate(((G0, WF), (G1, WR))):
+            sent = pl.ds(0, 32 * n - 32)
+            remote(E.at[:, half_rows(core)], E.at[:, half_rows(1 - core)], sh_s.at[g], sh_r.at[g], beside).wait()
+            remote(G.at[:, sent], G.at[:, sent], rs_s.at[g], rs_r.at[0, 0], after).wait_send()
+            remote(E.at[:, sent], E.at[:, sent], ag_s.at[g], ag_r.at[0, 0], after).wait_send()
+            for key in range(3):
+                copy = sib_all(g, key)
+                if copy is None: continue
+                if direct and g == 1 and key == 2: pl.when(dec)(copy.wait_send)
+                else: copy.wait_send()
+        sent = pl.ds(0, n - 1)
+        remote(EN.at[core], EN.at[1 - core], sh_s.at[2], sh_r.at[2], beside).wait()
+        remote(NG.at[0, sent], NG.at[0, sent], rs_s.at[2], rs_r.at[0, 0], after).wait_send()
+        remote(EN.at[0, sent], EN.at[0, sent], ag_s.at[2], ag_r.at[0, 0], after).wait_send()
+        sib_norm.wait_send()
 
     def done_blocks(g, G, count):
         per = G.shape[1] // SIDE
         for u in range(G.shape[0]):
-            if count == min((u + 1) * per, (8, 6)[g]): sib_copies[g][u].start()
+            if count == min((u + 1) * per, (8, 6)[g]): sib_copy(g, u).start()
 
     def weight_grads(g, G, source, grad, count, b0):
         T[...] = source[...].T
@@ -424,17 +466,18 @@
     for b in range(4):
         block(G0, 4 + b)[...] = dot(A[:, columns(b)].T, LOW[...]).astype(BF)
         done_blocks(0, G0, 4 + b + 1)
+        if b == 1 and G0.shape[0] > 1: begin(0, (0,))
     first_left = jnp.where(enc, 1, 0)
 
     def start_ring(m, place):
         @pl.when(m == first_left)
-        def _(): begin(0) if place == 0 else reduce_round(0, 1)
+        def _(): begin(0, (1,) if G0.shape[0] > 1 else (0,)) if place == 0 else reduce_round(0, 1)
     loop(first_left, 2, lambda m: bottom(m, start_ring))
     NG[...] = jnp.zeros_like(NG)
     for j in range(4):
         NG[0, j] = PG[:, 128 * j:128 * (j + 1)]
         NG[1, j] = PB[:, 128 * j:128 * (j + 1)]
-    sib_copies[1][-1].start()
+    sib_norm.start()
     weight_grads(1, G1, H1, DQKV, 3, 0)
     weight_grads(1, G1, O, LOWS, 1, 3)
     if not direct:
@@ -475,13 +518,7 @@
             loop(1, far - 1, lambda t: gather_round(g, t))
             gather_round(g, far - 1)
             gather_round(g, far)
-    for f in group[0] + group[1]:
-        if f.way == 1: sh_copy(f, 0).wait()
-        loop(1, f.far + 1, lambda t: sh_copy(f, t).wait())
-    for g in (0, 1):
-        for u, copy in enumerate(sib_copies[g]):
-            if direct and g == 1 and u in (4, 5): pl.when(dec)(copy.wait_send)
-            else: copy.wait_send()
+    close_ring()
 
     @pl.when(enc)
     def _():
@@ -530,7 +567,7 @@
     s0, s1 = units(8), units(6)
     norm = (2, n, 8, 128)
     def own(s): return (s[0], s[1] // 2, SIDE)
-    def slots(s): return (2, 2, n // 2, s[0], 16, SIDE)
+    def slots(s): return (2, n // 2, s[0], 32, SIDE)
     sq = V((rows, width), BF)
     probs = V((micro * width // 64, length, length), BF)
     scratch = [V(x.shape, BF), V(x.shape, BF), V(wc.shape, BF), V(gn.shape, F4), V(bs.shape, F4)]
@@ -539,7 +576,7 @@
                 sq, sq, sq, sq, V((rows, 3 * width), BF), sq, V((rows, 2 * width), BF), sq, V((width, rows), BF)]
     scratch += [V(s0, BF), V(s1, BF), V(norm, F4), V((2, SIDE, SIDE), BF), V((2, SIDE // 2, SIDE), BF), V(own(s0), BF), V(own(s1), BF), V(norm[1:], F4), V(slots(s0), BF), V(slots(s1), BF), V((2, n // 2, 8, 128), F4),
                 V((8, width), F4), V((8, width), F4)]
-    scratch += [DMA((18,)), DMA, DMA, DMA((3,)), DMA((3,)), DMA((2,)), DMA((2,)), DMA((2,)), DMA((2,)), DMA((2,)), DMA((2,)), DMA((2,)), DMA((2,)), DMA((2, 9)), DMA((2, 9))] + [DMA((18 if s0[0] > 1 else 10, n // 2 + 1))] * 6
+    scratch += [DMA((18,)), DMA, DMA, DMA((3,)), DMA((3,)), DMA((2,)), DMA((2,)), DMA((2,)), DMA((2,)), DMA((2,)), DMA((2,)), DMA((2,)), DMA((2,)), DMA((7,)), DMA((7,)), DMA((3,)), DMA((10, n // 2)), DMA((3,)), DMA((10, n // 2)), DMA((3,)), DMA((3,))]
     results = [V(s0, BF), V(s1, BF), V(norm, F4), V(x.shape, BF), V(x.shape, BF)]
     e0, e1, en, out, gin = pl.pallas_call(
         functools.partial(layers_kernel, n), out_shape=results,

time: 138 us -> 133 us (0.964)
  Pallas kernels: 137 us -> 132 us
    pallas_call x1, Pallas kernels: 131 us -> 126 us  [layers(): pl.pallas_call(functools.partial(layers_kernel, n), out_shape=results, in...]
where the time goes in v5:
time: 133 us
  Pallas kernels  132 us (99%)
    pallas_call x1, Pallas kernels, layers(): pl.pallas_call(functools.partial(layers_kernel, n), out_shape=results, in...  126 us
    pallas_call x1, Pallas kernels, layers(): pl.pallas_call(finish_kernel, out_shape=[jax.ShapeDtypeStruct(x.shape, BF...  6.16 us

profile of v5, /device:TPU:0, one launch (start us, length us, event | category | flops | bytes accessed | tf_op | source)
XLA Modules:
  0.0 133.0 jit_solution(18153593926975196819)
XLA Ops:
  0.6 126.0 %layers.1 = (bf16[8,512,512]{2,1,0:T(8,128)(2,1)S(1)}, bf16[6,512,512]{2,1,0:T(8,128)(2,1)S(1)}, f32[2,8,8,128]{3,2,1,0:T(8,128)S(1)}, bf16[2,256,512]{2,1,0:T(8,128)(2,1)S(1)}, bf16[2,256,512]{2,1,0:T(8,128)(2,1)S(1)}) custom-call(s32[1,2]{1,0:T(1,128)} %bitcast.27, bf16[2,256,512]{2,1,0:T(8,128)(2,1)} %bitcast.22, bf16[2,256,512]{2,1,0:T(8,128)(2,1)} %bitcast.23, ...), custom_call_target="tpu_custom_call" | custom-call | tf_op jit(solution)/shard_map/layers/pallas_call | solution.py:581
  126.7 6.2 %finish.1 = (bf16[2,256,512]{2,1,0:T(8,128)(2,1)}, bf16[2,256,512]{2,1,0:T(8,128)(2,1)}, f32[1,512,1536]{2,1,0:T(8,128)}, f32[1,512,512]{2,1,0:T(8,128)}, f32[1,...) custom-call(bf16[8,512,512]{2,1,0:T(8,128)(2,1)S(1)} %get-tuple-elem, ...), custom_call_target="tpu_custom_call" | custom-call | tf_op jit(solution)/shard_map/finish/pallas_call | solution.py:588

commit v6 on v5

--- a/solution.py
+++ b/solution.py
@@ -23,13 +23,8 @@
 
 
 def gelu_parts(u):
-    size = jnp.abs(u)
-    t = 1.0 / (1.0 + (0.3275911 * 0.5 ** 0.5) * size)
-    bell = jnp.exp(-0.5 * u * u)
-    poly = t * (0.127414796 + t * (-0.142248368 + t * (0.7107068705 + t * (-0.7265760135 + t * 0.5307027145))))
-    tail = poly * bell
-    cdf = jnp.where(u >= 0, 1.0 - tail, tail)
-    return u * cdf, cdf + u * bell * 0.3989422804014327
+    cdf = 0.5 + 0.5 * lax.erf(u * 0.5 ** 0.5)
+    return u * cdf, cdf + u * (jnp.exp(-0.5 * u * u) * 0.3989422804014327)
 
 
 def normalize(value):
@@ -104,11 +99,6 @@
     load("first", bs, BS)
     for b in range(3): load("first", wq.at[:, columns(b)], block(WR, b))
     load("first", wo, block(WR, 3))
-    for b in range(4): load("ffn", w1.at[:, columns(b)], block(WF, b))
-    for b in range(4): load("ffn", w2.at[columns(b), :], block(WF, 4 + b))
-    for b in range(2): load("cross", wc.at[:, columns(b)], block(WR, 4 + b))
-    load("cross", ct, CT)
-
     def arrived(name):
         for copy in loads[name]: copy.wait()
 
@@ -219,6 +209,10 @@
             AFT[rows, at] = total
 
     arrived("first")
+    for b in range(4): load("ffn", w1.at[:, columns(b)], block(WF, b))
+    for b in range(4): load("ffn", w2.at[columns(b), :], block(WF, 4 + b))
+    for b in range(2): load("cross", wc.at[:, columns(b)], block(WR, 4 + b))
+    load("cross", ct, CT)
 
     def front(m):
         self_forward(m)
@@ -262,6 +256,8 @@
         grad = AFT[rows, :]
         add_norm_grads(0, grad, unit)
         GIN[m] = (D[rows, :] + norm_back(grad, unit, scale, gain_at(0))).astype(BF)
+
+    first, second = pl.ds(0, length), pl.ds(length, length)
 
     def middle(m):
         rows = mrows(m)
@@ -304,14 +300,22 @@
                 @pl.when(m == 1)
                 def _():
                     for i in (0, 1): dk_copy(i).start()
-            for t, at in tiles(width): AFT[rows, at] = dot_nt(DCQ[rows, :], rows_of(WR, 4, t))
-            unit, scale = normalize(RR[0, rows, :])
-            grad = AFT[rows, :]
-            add_norm_grads(1, grad, unit)
-            D[rows, :] = D[rows, :] + norm_back(grad, unit, scale, gain_at(1))
         @pl.when(enc & (m == 0))
-        def _(): bottom(m)
+        def _():
+            bottom(m)
+            T[:, first] = N2[first, :].T
+            for b in range(4):
+                block(G0, b)[...] = dot(T[:, first], GP[first, columns(b)]).astype(BF)
+                block(G0, 4 + b)[...] = dot(A[first, columns(b)].T, LOW[first, :]).astype(BF)
     loop(0, 2, middle)
+
+    def cross_query_back(m):
+        rows = mrows(m)
+        for t, at in tiles(width): AFT[rows, at] = dot_nt(DCQ[rows, :], rows_of(WR, 4, t))
+        unit, scale = normalize(RR[0, rows, :])
+        grad = AFT[rows, :]
+        add_norm_grads(1, grad, unit)
+        D[rows, :] = D[rows, :] + norm_back(grad, unit, scale, gain_at(1))
 
     far = n // 2
     def half_rows(c): return ds(c * 32 * n, 32 * n)
@@ -456,7 +460,20 @@
             cg_trade.start()
         @pl.when(enc)
         def _(): S1[pl.ds(4, 2)] = jnp.zeros((2, SIDE // 2, SIDE), BF)
-    weight_grads(0, G0, N2, GP, 4, 0)
+    def grad_block(b, whole, rest):
+        out = block(G0, b)
+        @pl.when(dec)
+        def _(): out[...] = whole().astype(BF)
+        @pl.when(enc)
+        def _(): out[...] = (out[...].astype(F4) + rest()).astype(BF)
+        done_blocks(0, G0, b + 1)
+
+    @pl.when(dec)
+    def _(): T[...] = N2[...].T
+    @pl.when(enc)
+    def _(): T[:, second] = N2[second, :].T
+    for b in range(4):
+        grad_block(b, lambda: dot(T[...], GP[:, columns(b)]), lambda: dot(T[:, second], GP[second, columns(b)]))
     if direct:
         @pl.when(dec)
         def _():
@@ -464,9 +481,12 @@
             CG[:, own_rows, :] = (CG[:, own_rows, :].astype(F4) + CS[...].astype(F4)).astype(BF)
             cg_copy.start()
     for b in range(4):
-        block(G0, 4 + b)[...] = dot(A[:, columns(b)].T, LOW[...]).astype(BF)
-        done_blocks(0, G0, 4 + b + 1)
+        grad_block(4 + b, lambda: dot(A[:, columns(b)].T, LOW[...]), lambda: dot(A[second, columns(b)].T, LOW[second, :]))
         if b == 1 and G0.shape[0] > 1: begin(0, (0,))
+
+    @pl.when(dec)
+    def _(): loop(0, 2, cross_query_back)
+
     first_left = jnp.where(enc, 1, 0)
 
     def start_ring(m, place):

time: 133 us -> 130 us (0.977)
  Pallas kernels: 132 us -> 129 us
    pallas_call x1, Pallas kernels: 126 us -> 123 us  [layers(): pl.pallas_call(functools.partial(layers_kernel, n), out_shape=results, in...]
where the time goes in v6:
time: 130 us
  Pallas kernels  129 us (99%)
    pallas_call x1, Pallas kernels, layers(): pl.pallas_call(functools.partial(layers_kernel, n), out_shape=results, in...  123 us
    pallas_call x1, Pallas kernels, layers(): pl.pallas_call(finish_kernel, out_shape=[jax.ShapeDtypeStruct(x.shape, BF...  6.16 us

profile of v6, /device:TPU:0, one launch (start us, length us, event | category | flops | bytes accessed | tf_op | source)
XLA Modules:
  0.0 130.1 jit_solution(11216225709306318576)
XLA Ops:
  0.6 123.1 %layers.1 = (bf16[8,512,512]{2,1,0:T(8,128)(2,1)S(1)}, bf16[6,512,512]{2,1,0:T(8,128)(2,1)S(1)}, f32[2,8,8,128]{3,2,1,0:T(8,128)S(1)}, bf16[2,256,512]{2,1,0:T(8,128)(2,1)S(1)}, bf16[2,256,512]{2,1,0:T(8,128)(2,1)S(1)}) custom-call(s32[1,2]{1,0:T(1,128)} %bitcast.27, bf16[2,256,512]{2,1,0:T(8,128)(2,1)} %bitcast.22, bf16[2,256,512]{2,1,0:T(8,128)(2,1)} %bitcast.23, ...), custom_call_target="tpu_custom_call" | custom-call | tf_op jit(solution)/shard_map/layers/pallas_call | solution.py:601
  123.7 6.2 %finish.1 = (bf16[2,256,512]{2,1,0:T(8,128)(2,1)}, bf16[2,256,512]{2,1,0:T(8,128)(2,1)}, f32[1,512,1536]{2,1,0:T(8,128)}, f32[1,512,512]{2,1,0:T(8,128)}, f32[1,...) custom-call(bf16[8,512,512]{2,1,0:T(8,128)(2,1)S(1)} %get-tuple-elem, ...), custom_call_target="tpu_custom_call" | custom-call | tf_op jit(solution)/shard_map/finish/pallas_call | solution.py:608

commit v7 on v6

--- a/solution.py
+++ b/solution.py
@@ -64,7 +64,7 @@
 
 def layers_kernel(n, lens, x, ct, wq, wo, w1, w2, wc, gn, bs,
                   WF, WR, EN, OUT, GIN,
-                  X, CT, WC0, GN, BS, H1, QKV, PT, O, RR, ST, HQ, CQ, KV, PT2, O2, N2, A, GP, AFT, D, LOW, LOWC, LOWS, DO, DQKV, DCQ, DKV, DST, T,
+                  X, CT, WC0, GN, BS, H1, QKV, PT, O, RR, ST, HQ, CQ, KV, PT2, O2, N2, A, GP, DA, AFT, D, LOW, LOWC, LOWS, DO, DQKV, DCQ, DKV, DST, T,
                   G0, G1, NG, CG, CS, S0, S1, NS, R0, R1, NR, PG, PB,
                   ld, wc_s, wc_r, wh_s, wh_r, st_s, st_r, ds_s, ds_r, dk_s, dk_r, cg_s, cg_r,
                   sib_s, sib_r, rs_s, rs_r, ag_s, ag_r, sh_s, sh_r):
@@ -198,11 +198,16 @@
         attention(m, QKV, 0, QKV, width, QKV, 2 * width, PT, O)
         for t, at in tiles(width): RR[0, rows, at] = dot(O[rows, :], tile_of(WR, 3, t)) + X[m, :, at].astype(F4)
 
-    def ffn_forward(m, source, index):
+    def ffn_up(m, source, index, grad=None):
         rows = mrows(m)
         norm_into(source, m, index, N2)
         for t, at in tiles(hidden):
-            A[rows, at], GP[rows, at] = (part.astype(BF) for part in gelu_parts(dot(N2[rows, :], tile_of(WF, 0, t))))
+            act, slope = gelu_parts(dot(N2[rows, :], tile_of(WF, 0, t)))
+            A[rows, at] = act.astype(BF)
+            GP[rows, at] = (slope if grad is None else slope * grad[rows, at].astype(F4)).astype(BF)
+
+    def ffn_down(m, source):
+        rows = mrows(m)
         for t, at in tiles(width):
             total = source[rows, at]
             for b in range(hidden // SIDE): total = total + dot(A[rows, columns(b)], tile_of(WF, 4 + b, t))
@@ -220,7 +225,8 @@
         def _():
             @pl.when(m == 0)
             def _(): arrived("ffn")
-            ffn_forward(m, RR.at[0], 1)
+            ffn_up(m, RR.at[0], 1)
+            ffn_down(m, RR.at[0])
             norm_into(AFT, m, 2, ST)
             st_copy(m).start()
             OUT[m] = ST[mrows(m), :]
@@ -236,93 +242,18 @@
         for m in (0, 1):
             norm_into(RR.at[0], m, 1, HQ)
             for t, at in tiles(width): CQ[mrows(m), at] = dot(HQ[mrows(m), :], tile_of(WR, 4, t)).astype(BF)
+            for t, at in tiles(hidden): DA[mrows(m), at] = dot_nt(CT[m], rows_of(WF, 4, t)).astype(BF)
         wc_trades[0].wait_recv()
         wc_trades[2].start()
         wc_trades[1].wait_recv()
         wc_trades[2].wait_recv()
-
-    def bottom(m, hook=None):
-        rows = mrows(m)
-        LOWS[rows, :] = D[rows, :].astype(BF)
-        for t, at in tiles(width): DO[rows, at] = dot_nt(LOWS[rows, :], rows_of(WR, 3, t)).astype(BF)
-        if hook is not None: hook(m, 0)
-        attention_back(m, DO, QKV, 0, QKV, width, QKV, 2 * width, PT, DQKV, 0, DQKV, width, DQKV, 2 * width)
-        if hook is not None: hook(m, 1)
-        for t, at in tiles(width):
-            total = dot_nt(DQKV[rows, columns(0)], rows_of(WR, 0, t))
-            for b in (1, 2): total = total + dot_nt(DQKV[rows, columns(b)], rows_of(WR, b, t))
-            AFT[rows, at] = total
-        unit, scale = normalize(X[m].astype(F4))
-        grad = AFT[rows, :]
-        add_norm_grads(0, grad, unit)
-        GIN[m] = (D[rows, :] + norm_back(grad, unit, scale, gain_at(0))).astype(BF)
-
-    first, second = pl.ds(0, length), pl.ds(length, length)
-
-    def middle(m):
-        rows = mrows(m)
-        @pl.when(enc)
-        def _():
-            ds_copy(m).wait_recv()
-            unit, scale = normalize(AFT[rows, :])
-            grad = CT[m].astype(F4) + DST[rows, :].astype(F4)
-            add_norm_grads(2, grad, unit)
-            back = norm_back(grad, unit, scale, gain_at(2))
-            D[rows, :] = back
-            LOW[rows, :] = back.astype(BF)
-        @pl.when(dec)
-        def _():
-            st_copy(m).wait_recv()
-            for t, at in tiles(2 * width): KV[rows, at] = dot(ST[rows, :], WC0[:, at]).astype(BF)
-            attention(m, CQ, 0, KV, 0, KV, width, PT2, O2)
-            for t, at in tiles(width): RR[1, rows, at] = dot(O2[rows, :], tile_of(WR, 5, t)) + RR[0, rows, at]
-            ffn_forward(m, RR.at[1], 2)
-            OUT[m] = AFT[rows, :].astype(BF)
-            D[rows, :] = CT[m].astype(F4)
-            LOW[rows, :] = CT[m]
-        for t, at in tiles(hidden): GP[rows, at] = (dot_nt(LOW[rows, :], rows_of(WF, 4, t)) * GP[rows, at].astype(F4)).astype(BF)
-        for t, at in tiles(width):
-            total = dot_nt(GP[rows, columns(0)], rows_of(WF, 0, t))
-            for b in range(1, hidden // SIDE): total = total + dot_nt(GP[rows, columns(b)], rows_of(WF, b, t))
-            AFT[rows, at] = total
-        unit, scale = normalize(RR[sec, rows, :])
-        grad = AFT[rows, :]
-        add_norm_grads(1 + sec, grad, unit)
-        D[rows, :] = D[rows, :] + norm_back(grad, unit, scale, gain_at(1 + sec))
-        @pl.when(dec)
-        def _():
-            LOWC[rows, :] = D[rows, :].astype(BF)
-            for t, at in tiles(width): DO[rows, at] = dot_nt(LOWC[rows, :], rows_of(WR, 5, t)).astype(BF)
-            attention_back(m, DO, CQ, 0, KV, 0, KV, width, PT2, DCQ, 0, DKV, 0, DKV, width)
-            for t, at in tiles(width): DST[rows, at] = dot_nt(DKV[rows, :], WC0[at, :]).astype(BF)
-            ds_copy(m).start()
-            if not direct:
-                @pl.when(m == 1)
-                def _():
-                    for i in (0, 1): dk_copy(i).start()
-        @pl.when(enc & (m == 0))
-        def _():
-            bottom(m)
-            T[:, first] = N2[first, :].T
-            for b in range(4):
-                block(G0, b)[...] = dot(T[:, first], GP[first, columns(b)]).astype(BF)
-                block(G0, 4 + b)[...] = dot(A[first, columns(b)].T, LOW[first, :]).astype(BF)
-    loop(0, 2, middle)
-
-    def cross_query_back(m):
-        rows = mrows(m)
-        for t, at in tiles(width): AFT[rows, at] = dot_nt(DCQ[rows, :], rows_of(WR, 4, t))
-        unit, scale = normalize(RR[0, rows, :])
-        grad = AFT[rows, :]
-        add_norm_grads(1, grad, unit)
-        D[rows, :] = D[rows, :] + norm_back(grad, unit, scale, gain_at(1))
 
     far = n // 2
     def half_rows(c): return ds(c * 32 * n, 32 * n)
     def rows_at(k, c, lo, count): return pl.ds(pl.multiple_of(c * 32 * n + k * 32 + lo, 16), count)
     group = [[], []]
     for g, (G, S, R, E) in enumerate(((G0, S0, R0, WF), (G1, S1, R1, WR))):
-        cuts = (0, G.shape[0] // 2, G.shape[0]) if G.shape[0] > 1 else (0, 1)
+        cuts = (0, G.shape[0] // 2, G.shape[0]) if direct else (0, 1)
         for sub, (u, stop) in enumerate(zip(cuts, cuts[1:])):
             us = pl.ds(u, stop - u)
             for way in (1, -1):
@@ -354,7 +285,7 @@
         res = f.res(owner(f, -t), *at)
         remote(res, res, sh_s.at[f.g], sh_r.at[f.g], beside).start()
 
-    def sib_key(g, u): return g * 3 + (0 if G0.shape[0] == 1 else u // 4 if g == 0 else (0, 0, 0, 1, 2, 2)[u])
+    def sib_key(g, u): return g * 3 + (0 if not direct else u // 4 if g == 0 else (0, 0, 0, 1, 2, 2)[u])
     def sib_copy(g, u):
         G, S = ((G0, S0), (G1, S1))[g]
         return remote(G.at[u, half_rows(1 - core)], S.at[u], sib_s.at[sib_key(g, u)], sib_r.at[sib_key(g, u)], beside)
@@ -413,7 +344,7 @@
 
     def begin(g, subs=(0, 1, 2)):
         for sub in (0, 1):
-            if sub in subs and (sub == 0 or G0.shape[0] > 1):
+            if sub in subs and (sub == 0 or direct):
                 sib_wait(g, sub)
                 if direct and g == 1 and sub == 1: pl.when(enc)(cg_copy.wait_recv)
                 reduce_round(g, 0, (sub,))
@@ -452,6 +383,95 @@
     own_rows = ds(core * (SIDE // 2), SIDE // 2)
     cg_trade = remote(CG.at[:, ds((1 - core) * (SIDE // 2), SIDE // 2)], CS, cg_s.at[0], cg_r.at[0], beside)
     cg_copy = remote(CG.at[:, own_rows], G1.at[pl.ds(4, 2), own_rows], cg_s.at[1], cg_r.at[1], partner) if direct else None
+    early = direct
+
+    def bottom(m, hook=None):
+        rows = mrows(m)
+        LOWS[rows, :] = D[rows, :].astype(BF)
+        for t, at in tiles(width): DO[rows, at] = dot_nt(LOWS[rows, :], rows_of(WR, 3, t)).astype(BF)
+        if hook is not None: hook(m, 0)
+        attention_back(m, DO, QKV, 0, QKV, width, QKV, 2 * width, PT, DQKV, 0, DQKV, width, DQKV, 2 * width)
+        if hook is not None: hook(m, 1)
+        for t, at in tiles(width):
+            total = dot_nt(DQKV[rows, columns(0)], rows_of(WR, 0, t))
+            for b in (1, 2): total = total + dot_nt(DQKV[rows, columns(b)], rows_of(WR, b, t))
+            AFT[rows, at] = total
+        unit, scale = normalize(X[m].astype(F4))
+        grad = AFT[rows, :]
+        add_norm_grads(0, grad, unit)
+        GIN[m] = (D[rows, :] + norm_back(grad, unit, scale, gain_at(0))).astype(BF)
+
+    first, second = pl.ds(0, length), pl.ds(length, length)
+
+    def middle(m):
+        rows = mrows(m)
+        @pl.when(enc)
+        def _():
+            ds_copy(m).wait_recv()
+            unit, scale = normalize(AFT[rows, :])
+            grad = CT[m].astype(F4) + DST[rows, :].astype(F4)
+            add_norm_grads(2, grad, unit)
+            back = norm_back(grad, unit, scale, gain_at(2))
+            D[rows, :] = back
+            LOW[rows, :] = back.astype(BF)
+            if early:
+                @pl.when(m == 1)
+                def _():
+                    for b in range(4):
+                        out = block(G0, 4 + b)
+                        out[...] = (out[...].astype(F4) + dot(A[second, columns(b)].T, LOW[second, :])).astype(BF)
+                        done_blocks(0, G0, 5 + b)
+        @pl.when(dec)
+        def _():
+            st_copy(m).wait_recv()
+            for t, at in tiles(2 * width): KV[rows, at] = dot(ST[rows, :], WC0[:, at]).astype(BF)
+            attention(m, CQ, 0, KV, 0, KV, width, PT2, O2)
+            for t, at in tiles(width): RR[1, rows, at] = dot(O2[rows, :], tile_of(WR, 5, t)) + RR[0, rows, at]
+            ffn_up(m, RR.at[1], 2, DA)
+            D[rows, :] = CT[m].astype(F4)
+            LOW[rows, :] = CT[m]
+        @pl.when(enc)
+        def _():
+            for t, at in tiles(hidden): GP[rows, at] = (dot_nt(LOW[rows, :], rows_of(WF, 4, t)) * GP[rows, at].astype(F4)).astype(BF)
+            if early: pl.when(m == 1)(lambda: begin(0, (1,)))
+        for t, at in tiles(width):
+            total = dot_nt(GP[rows, columns(0)], rows_of(WF, 0, t))
+            for b in range(1, hidden // SIDE): total = total + dot_nt(GP[rows, columns(b)], rows_of(WF, b, t))
+            AFT[rows, at] = total
+        unit, scale = normalize(RR[sec, rows, :])
+        grad = AFT[rows, :]
+        add_norm_grads(1 + sec, grad, unit)
+        D[rows, :] = D[rows, :] + norm_back(grad, unit, scale, gain_at(1 + sec))
+        @pl.when(dec)
+        def _():
+            LOWC[rows, :] = D[rows, :].astype(BF)
+            for t, at in tiles(width): DO[rows, at] = dot_nt(LOWC[rows, :], rows_of(WR, 5, t)).astype(BF)
+            attention_back(m, DO, CQ, 0, KV, 0, KV, width, PT2, DCQ, 0, DKV, 0, DKV, width)
+            for t, at in tiles(width): DST[rows, at] = dot_nt(DKV[rows, :], WC0[at, :]).astype(BF)
+            ds_copy(m).start()
+            if not direct:
+                @pl.when(m == 1)
+                def _():
+                    for i in (0, 1): dk_copy(i).start()
+        @pl.when(enc & (m == 0))
+        def _():
+            bottom(m)
+            T[:, first] = N2[first, :].T
+            for b in range(4):
+                block(G0, b)[...] = dot(T[:, first], GP[first, columns(b)]).astype(BF)
+                block(G0, 4 + b)[...] = dot(A[first, columns(b)].T, LOW[first, :]).astype(BF)
+    loop(0, 2, middle)
+
+    def decoder_rest(m):
+        rows = mrows(m)
+        ffn_down(m, RR.at[1])
+        OUT[m] = AFT[rows, :].astype(BF)
+        for t, at in tiles(width): AFT[rows, at] = dot_nt(DCQ[rows, :], rows_of(WR, 4, t))
+        unit, scale = normalize(RR[0, rows, :])
+        grad = AFT[rows, :]
+        add_norm_grads(1, grad, unit)
+        D[rows, :] = D[rows, :] + norm_back(grad, unit, scale, gain_at(1))
+
     if direct:
         @pl.when(dec)
         def _():
@@ -480,19 +500,35 @@
             cg_trade.wait_recv()
             CG[:, own_rows, :] = (CG[:, own_rows, :].astype(F4) + CS[...].astype(F4)).astype(BF)
             cg_copy.start()
-    for b in range(4):
-        grad_block(4 + b, lambda: dot(A[:, columns(b)].T, LOW[...]), lambda: dot(A[second, columns(b)].T, LOW[second, :]))
-        if b == 1 and G0.shape[0] > 1: begin(0, (0,))
+    def down_block(b): return dot(A[:, columns(b)].T, LOW[...])
+    if early:
+        @pl.when(dec)
+        def _():
+            for b in range(4):
+                block(G0, 4 + b)[...] = down_block(b).astype(BF)
+                done_blocks(0, G0, 5 + b)
+                if b == 1: begin(0, (0,))
+    else:
+        for b in range(4): grad_block(4 + b, lambda: down_block(b), lambda: dot(A[second, columns(b)].T, LOW[second, :]))
 
     @pl.when(dec)
-    def _(): loop(0, 2, cross_query_back)
+    def _(): loop(0, 2, decoder_rest)
 
     first_left = jnp.where(enc, 1, 0)
 
     def start_ring(m, place):
         @pl.when(m == first_left)
-        def _(): begin(0, (1,) if G0.shape[0] > 1 else (0,)) if place == 0 else reduce_round(0, 1)
+        def _():
+            if not early: begin(0) if place == 0 else reduce_round(0, 1)
+            elif place == 0:
+                @pl.when(enc)
+                def _():
+                    begin(0, (0,))
+                    reduce_round(0, 1, (1,))
+                pl.when(dec)(lambda: begin(0, (1,)))
+            else: pl.when(dec)(lambda: reduce_round(0, 1))
     loop(first_left, 2, lambda m: bottom(m, start_ring))
+    if early: pl.when(enc)(lambda: reduce_round(0, 1, (0,)))
     NG[...] = jnp.zeros_like(NG)
     for j in range(4):
         NG[0, j] = PG[:, 128 * j:128 * (j + 1)]
@@ -513,9 +549,10 @@
             block(G1, 4 + b)[...] = dot(T[...], grad[...]).astype(BF)
             if direct: done_blocks(1, G1, 5 + b)
     if not direct: done_blocks(1, G1, 6)
+    if early: reduce_round(0, 2, (1,))
     begin(1)
     if far == 4:
-        reduce_round(0, 2)
+        reduce_round(0, 2, (0,))
         reduce_round(1, 1)
         reduce_round(0, 3)
         reduce_round(1, 2)
@@ -592,7 +629,7 @@
     probs = V((micro * width // 64, length, length), BF)
     scratch = [V(x.shape, BF), V(x.shape, BF), V(wc.shape, BF), V(gn.shape, F4), V(bs.shape, F4)]
     scratch += [sq, V((rows, 3 * width), BF), probs, sq, V((2, rows, width), F4), sq, sq, sq, V((rows, 2 * width), BF), probs, sq, sq,
-                V((rows, hidden), BF), V((rows, hidden), BF), V((rows, width), F4), V((rows, width), F4),
+                V((rows, hidden), BF), V((rows, hidden), BF), V((rows, hidden), BF), V((rows, width), F4), V((rows, width), F4),
                 sq, sq, sq, sq, V((rows, 3 * width), BF), sq, V((rows, 2 * width), BF), sq, V((width, rows), BF)]
     scratch += [V(s0, BF), V(s1, BF), V(norm, F4), V((2, SIDE, SIDE), BF), V((2, SIDE // 2, SIDE), BF), V(own(s0), BF), V(own(s1), BF), V(norm[1:], F4), V(slots(s0), BF), V(slots(s1), BF), V((2, n // 2, 8, 128), F4),
                 V((8, width), F4), V((8, width), F4)]
@@ -601,7 +638,7 @@
     e0, e1, en, out, gin = pl.pallas_call(
         functools.partial(layers_kernel, n), out_shape=results,
         in_specs=[pl.BlockSpec(memory_space=pltpu.SMEM)] + [any_] * 9, out_specs=[vmem] * 5, scratch_shapes=scratch,
-        compiler_params=pltpu.CompilerParams(collective_id=1, has_side_effects=True, vmem_limit_bytes=54 * 2**20),
+        compiler_params=pltpu.CompilerParams(collective_id=1, has_side_effects=True, vmem_limit_bytes=53 * 2**20),
         name="layers",
     )(lens, x, ct, wq, wo, w1, w2, wc, gn, bs)
     def f4(*shape): return jax.ShapeDtypeStruct(shape, F4)

time: 130 us -> 128 us (0.985)
  Pallas kernels: 129 us -> 127 us
    pallas_call x1, Pallas kernels: 123 us -> 120 us  [layers(): pl.pallas_call(functools.partial(layers_kernel, n), out_shape=results, in...]
where the time goes in v7:
time: 128 us; the launch traced here: 127 us
  Pallas kernels  127 us (99%)
    pallas_call x1, Pallas kernels, layers(): pl.pallas_call(functools.partial(layers_kernel, n), out_shape=results, in...  120 us
    pallas_call x1, Pallas kernels, layers(): pl.pallas_call(finish_kernel, out_shape=[jax.ShapeDtypeStruct(x.shape, BF...  6.16 us

profile of v7, /device:TPU:0, one launch (start us, length us, event | category | flops | bytes accessed | tf_op | source)
XLA Modules:
  0.0 127.5 jit_solution(15687538400176733816)
XLA Ops:
  0.6 120.5 %layers.1 = (bf16[8,512,512]{2,1,0:T(8,128)(2,1)S(1)}, bf16[6,512,512]{2,1,0:T(8,128)(2,1)S(1)}, f32[2,8,8,128]{3,2,1,0:T(8,128)S(1)}, bf16[2,256,512]{2,1,0:T(8,128)(2,1)S(1)}, bf16[2,256,512]{2,1,0:T(8,128)(2,1)S(1)}) custom-call(s32[1,2]{1,0:T(1,128)} %bitcast.27, bf16[2,256,512]{2,1,0:T(8,128)(2,1)} %bitcast.22, bf16[2,256,512]{2,1,0:T(8,128)(2,1)} %bitcast.23, ...), custom_call_target="tpu_custom_call" | custom-call | tf_op jit(solution)/shard_map/layers/pallas_call | solution.py:638
  121.1 6.2 %finish.1 = (bf16[2,256,512]{2,1,0:T(8,128)(2,1)}, bf16[2,256,512]{2,1,0:T(8,128)(2,1)}, f32[1,512,1536]{2,1,0:T(8,128)}, f32[1,512,512]{2,1,0:T(8,128)}, f32[1,...) custom-call(bf16[8,512,512]{2,1,0:T(8,128)(2,1)S(1)} %get-tuple-elem, ...), custom_call_target="tpu_custom_call" | custom-call | tf_op jit(solution)/shard_map/finish/pallas_call | solution.py:645
